TPU v7x, 32 devices: a whole 2x2x4 slice. The times are simulated.
32 devices in a mesh: space: 4 (over x, core), vel: 8 (over z, y).
Axes of the slice: x: 2, y: 2, z: 4, core: 2. Of those that a mesh axis runs over, the one named last changes fastest.
Arguments:
- particles: float32 [2048, 32768], P('space', 'vel'), may hold values from 0.1 to 2
- gain_spectrum: float32 [32, 32, 32], replicated, may hold values from 0 to 1
- freq_spectrum: float32 [32, 32, 32], replicated, may hold values from 0 to 1
- panel_temp: float32 [32], replicated, may hold values from 0.5 to 4
- wall_cells: int32 [32, 16], replicated, may hold values from 0 to 2047, as said below
Outputs:
- particles_out: float32 [2048, 32768], P('space', 'vel')
Inputs may be any that keep to these rules, and one draw needn't show every extreme that they name: `wall_cells`: all 512 entries are distinct cells, so each wall cell belongs to one panel.
All inputs are finite; a program needn't handle non-finite values.
Results may differ from a plain program's by a relative error of at most 0.000059.
Values sent between devices are 32-bit elements; how exact they have to be, the bound alone decides.
No kernel may reach another device: no remote copies, remote signals or barrier semaphores. Data moves between devices by JAX's collectives and lax.ppermute only.
A program may use at most 256 MiB of HBM per device.

v0:
```python
from functools import partial
import math

import jax
import jax.numpy as jnp
from jax import lax
from jax.sharding import PartitionSpec as P

courant = 0.9
top_speed = 3.0
collide_rate = 0.5
accommodation = 0.8
highest = lax.Precision.HIGHEST


def with_halo(block, sides, width):
    for axis, dim in sides:
        count = lax.axis_size(axis)
        forward = [(i, i + 1) for i in range(count - 1)]
        backward = [(target, source) for source, target in forward]
        low = lax.ppermute(
            lax.slice_in_dim(block, block.shape[dim] - width, None, axis=dim), axis, forward
        )
        high = lax.ppermute(lax.slice_in_dim(block, 0, width, axis=dim), axis, backward)
        block = jnp.concatenate([low, block, high], axis=dim)
    return block


def dft_tables(points):
    line = jnp.arange(points, dtype=jnp.int32)
    phase_line = line[:, None] * line[None, :] % points
    angle_line = 2.0 * math.pi / points * phase_line.astype(jnp.float32)
    plane = jnp.arange(points * points, dtype=jnp.int32)
    outer = plane // points
    inner = plane % points
    phase_plane = (outer[:, None] * outer[None, :] + inner[:, None] * inner[None, :]) % points
    angle_plane = 2.0 * math.pi / points * phase_plane.astype(jnp.float32)
    return (jnp.cos(angle_line), jnp.sin(angle_line), jnp.cos(angle_plane), jnp.sin(angle_plane))


def plane_product(values, table):
    return jnp.einsum("rak,kj->raj", values, table, precision=highest)


def line_product(values, table):
    return jnp.einsum("rak,ab->rbk", values, table, precision=highest)


def collide_cells(cube_rows, gain_flat, freq_flat, tables):
    cos_line, sin_line, cos_plane, sin_plane = tables
    row_count, cube_size = cube_rows.shape
    points = cos_line.shape[0]
    cube_view = cube_rows.reshape(row_count, points, points * points)
    plane_re = plane_product(cube_view, cos_plane)
    plane_im = -plane_product(cube_view, sin_plane)
    spec_re = line_product(plane_re, cos_line) + line_product(plane_im, sin_line)
    spec_im = line_product(plane_im, cos_line) - line_product(plane_re, sin_line)
    both_re = jnp.concatenate([spec_re * gain_flat, spec_re * freq_flat], axis=0)
    both_im = jnp.concatenate([spec_im * gain_flat, spec_im * freq_flat], axis=0)
    back_re = line_product(both_re, cos_line) - line_product(both_im, sin_line)
    back_im = line_product(both_im, cos_line) + line_product(both_re, sin_line)
    real_part = (plane_product(back_re, cos_plane) - plane_product(back_im, sin_plane)) / cube_size
    real_part = real_part.reshape(2 * row_count, cube_size)
    gain_part = real_part[:row_count]
    freq_part = real_part[row_count:]
    return cube_rows + collide_rate * (gain_part - cube_rows * freq_part)


def collide_items(cubes_in, gain_spectrum, freq_spectrum):
    item_count, group_size, cube_size = cubes_in.shape
    points = gain_spectrum.shape[0]
    row_count = item_count * group_size
    group_rows = math.gcd(row_count, 16)
    grouped = cubes_in.reshape(row_count // group_rows, group_rows, cube_size)
    tables = dft_tables(points)
    gain_flat = gain_spectrum.reshape(1, points, points * points)
    freq_flat = freq_spectrum.reshape(1, points, points * points)
    one_group = partial(collide_cells, gain_flat=gain_flat, freq_flat=freq_flat, tables=tables)
    return lax.map(one_group, grouped).reshape(item_count, group_size, cube_size)


def on_device(particles, gain_spectrum, freq_spectrum, panel_temp, wall_cells):
    cell_dev, vel_dev = particles.shape
    points = gain_spectrum.shape[0]
    plane_size = points * points
    planes = vel_dev // plane_size
    columns = jnp.arange(vel_dev, dtype=jnp.int32)
    plane_index = lax.axis_index("vel") * planes + columns // plane_size
    courant_col = courant * (2 * plane_index + 1 - points).astype(jnp.float32) / points
    padded = with_halo(particles, (("space", 0),), 1)
    left_cells = padded[:-2]
    right_cells = padded[2:]
    moved = jnp.where(
        courant_col > 0,
        particles - courant_col * (particles - left_cells),
        particles - courant_col * (right_cells - particles),
    )
    vel_count = lax.axis_size("vel")
    per_device = cell_dev // vel_count
    group_size = math.gcd(per_device, 8)
    item_count = per_device // group_size
    sectioned = moved.reshape(item_count, vel_count * group_size, vel_dev)
    cubes_in = lax.all_to_all(sectioned, "vel", split_axis=1, concat_axis=2, tiled=True)
    cubes_out = collide_items(cubes_in, gain_spectrum, freq_spectrum)
    settled = lax.all_to_all(cubes_out, "vel", split_axis=2, concat_axis=1, tiled=True)
    post = settled.reshape(cell_dev, vel_dev)
    cell_ids = lax.axis_index("space") * cell_dev + jnp.arange(cell_dev, dtype=jnp.int32)
    panels, per_panel = wall_cells.shape
    member = jnp.any(
        wall_cells.reshape(1, panels, per_panel) == cell_ids[:, None, None], axis=2
    ).astype(jnp.float32)
    cell_sums = jnp.sum(post, axis=1)
    mass_all = lax.psum(cell_sums, "vel")
    wall_mass = lax.psum(jnp.dot(mass_all, member, precision=highest), "space")
    velocity = (
        top_speed
        * (2 * jnp.arange(points, dtype=jnp.int32) + 1 - points).astype(jnp.float32)
        / points
    )
    line_weight = jnp.exp(-(velocity**2)[None, :] / (2.0 * panel_temp[:, None]))
    normal_sum = jnp.sum(line_weight, axis=1) ** 3
    first_vel = velocity[plane_index]
    second_vel = velocity[columns // points % points]
    third_vel = velocity[columns % points]
    speed_sq = first_vel**2 + second_vel**2 + third_vel**2
    profile = jnp.exp(-speed_sq[None, :] / (2.0 * panel_temp[:, None]))
    maxwellian = profile / normal_sum[:, None]
    emission = jnp.dot(member, (wall_mass / per_panel)[:, None] * maxwellian, precision=highest)
    wall_share = jnp.sum(member, axis=1)
    return post + accommodation * (emission - wall_share[:, None] * post)


def solution(mesh):
    in_specs = (P("space", "vel"), P(), P(), P(), P())
    out_specs = P("space", "vel")
    return jax.shard_map(
        on_device, mesh=mesh, in_specs=in_specs, out_specs=out_specs, check_vma=False
    )
```

profile of v0, /device:TPU:18, one launch (start us, length us, event | category | flops | bytes accessed | tf_op | source)
XLA Modules:
  0.0 1506.1 jit_solution(8394341410663896529)
XLA Ops:
  33.1 177.9 %all-to-all-done = f32[8,64,4096]{2,0,1:T(8,128)} async-done(((f32[8,64,4096]{2,0,1:T(8,128)}), f32[8,64,4096]{2,0,1:T(8,128)}, u32[]{:S(2)}, u32[]{:S(2)}) %all-to-all-start) | async-done | bytes 8388640 | tf_op jit(solution)/shard_map/all_to_all | solution.py:103
  222.4 638.4 %while.13 = (s32[]{:T(128)}, f32[4,16,32768]{2,1,0:T(8,128)}, f32[4,16,32768]{2,1,0:T(8,128)}, f32[1,32,1024]{2,1,0:T(8,128)S(1)}, f32[1,32,1024]{2,1,0:T(8,128)...) while((s32[]{:T(128)}, f32[4,16,32768]{2,1,0:T(8,128)}, ...), condition=%wide.region_1.2_spmd.clone.clone.clone, body=%wide.region_0.1_spmd.clone.clone.clone.sunk | while | flops 41152528384 | bytes 134512752 | solution.py:79
  225.6 23.6 %fusion.220 = f32[16,32,1024]{2,1,0:T(8,128)S(1)} fusion(f32[16,32,1024]{2,1,0:T(8,128)S(1)} %bitcast.165, s32[1024]{0:T(1024)S(1)} %get-tuple-element.323, s32[1024]{0:T(1024)S(1)} %get-tuple-element.322), kind=kOutput, calls=%fused_computation.20.clone.1 | convolution fusion | flops 6459228160 | bytes 4202496 | tf_op jit(solution)/shard_map/while/body/eval_jaxpr/rak,kj->raj/dot_general | solution.py:42
  251.4 24.2 %fusion.222 = f32[16,32,1024]{2,1,0:T(8,128)S(1)} fusion(f32[16,32,1024]{2,1,0:T(8,128)S(1)} %bitcast.166, s32[1024]{0:T(1024)S(1)} %get-tuple-element.323, s32[1024]{0:T(1024)S(1)} %get-tuple-element.322), kind=kOutput, calls=%fused_computation.17.clone.1 | convolution fusion | flops 6459228160 | bytes 4202496 | tf_op jit(solution)/shard_map/while/body/eval_jaxpr/rak,kj->raj/dot_general | solution.py:42
  294.8 31.8 %fusion.227 = f32[32,32,1024]{2,1,0:T(8,128)S(1)} fusion(f32[32,1024,32]{1,2,0:T(8,128)S(1)} %fusion.225, f32[32,1024,32]{1,2,0:T(8,128)S(1)} %fusion.226, s32[1024]{0:T(1024)S(1)} %get-tuple-element.323, s32[1024]{0:T(1024)S(1)} %get-tuple-element.322), kind=kOutput, calls=%fused_computation.12.clone.1 | convolution fusion | flops 12902727680 | bytes 12591104 | tf_op jit(solution)/shard_map/while/body/eval_jaxpr/rak,kj->raj/dot_general | solution.py:42
  337.9 31.2 %subtract_multiply_fusion.2 = f32[32,32,1024]{2,1,0:T(8,128)S(1)} fusion(f32[32,32,1024]{2,1,0:T(8,128)S(1)} %fusion.227, s32[1024]{0:T(1024)S(1)} %get-tuple-element.323, s32[1024]{0:T(1024)S(1)} %get-tuple-element.322, f32[32,1024,32]{1,2,0:T(8,128)S(1)} %fusion.228, f32[32,1024,32]{1,2,0:T(8,128)S(1)} %fusion.229), kind=kOutput, calls=%fused_computation.22.clone.1 | convolution fusion | flops 12904824832 | bytes 16785408 | tf_op jit(solution)/shard_map/while/body/eval_jaxpr/rak,kj->raj/dot_general | solution.py:42
  383.0 23.6 %fusion.220 = f32[16,32,1024]{2,1,0:T(8,128)S(1)} fusion(f32[16,32,1024]{2,1,0:T(8,128)S(1)} %bitcast.165, s32[1024]{0:T(1024)S(1)} %get-tuple-element.323, s32[1024]{0:T(1024)S(1)} %get-tuple-element.322), kind=kOutput, calls=%fused_computation.20.clone.1 | convolution fusion | flops 6459228160 | bytes 4202496 | tf_op jit(solution)/shard_map/while/body/eval_jaxpr/rak,kj->raj/dot_general | solution.py:42
  408.9 24.3 %fusion.222 = f32[16,32,1024]{2,1,0:T(8,128)S(1)} fusion(f32[16,32,1024]{2,1,0:T(8,128)S(1)} %bitcast.166, s32[1024]{0:T(1024)S(1)} %get-tuple-element.323, s32[1024]{0:T(1024)S(1)} %get-tuple-element.322), kind=kOutput, calls=%fused_computation.17.clone.1 | convolution fusion | flops 6459228160 | bytes 4202496 | tf_op jit(solution)/shard_map/while/body/eval_jaxpr/rak,kj->raj/dot_general | solution.py:42
  452.3 31.6 %fusion.227 = f32[32,32,1024]{2,1,0:T(8,128)S(1)} fusion(f32[32,1024,32]{1,2,0:T(8,128)S(1)} %fusion.225, f32[32,1024,32]{1,2,0:T(8,128)S(1)} %fusion.226, s32[1024]{0:T(1024)S(1)} %get-tuple-element.323, s32[1024]{0:T(1024)S(1)} %get-tuple-element.322), kind=kOutput, calls=%fused_computation.12.clone.1 | convolution fusion | flops 12902727680 | bytes 12591104 | tf_op jit(solution)/shard_map/while/body/eval_jaxpr/rak,kj->raj/dot_general | solution.py:42
  495.2 31.4 %subtract_multiply_fusion.2 = f32[32,32,1024]{2,1,0:T(8,128)S(1)} fusion(f32[32,32,1024]{2,1,0:T(8,128)S(1)} %fusion.227, s32[1024]{0:T(1024)S(1)} %get-tuple-element.323, s32[1024]{0:T(1024)S(1)} %get-tuple-element.322, f32[32,1024,32]{1,2,0:T(8,128)S(1)} %fusion.228, f32[32,1024,32]{1,2,0:T(8,128)S(1)} %fusion.229), kind=kOutput, calls=%fused_computation.22.clone.1 | convolution fusion | flops 12904824832 | bytes 16785408 | tf_op jit(solution)/shard_map/while/body/eval_jaxpr/rak,kj->raj/dot_general | solution.py:42
  540.5 23.6 %fusion.220 = f32[16,32,1024]{2,1,0:T(8,128)S(1)} fusion(f32[16,32,1024]{2,1,0:T(8,128)S(1)} %bitcast.165, s32[1024]{0:T(1024)S(1)} %get-tuple-element.323, s32[1024]{0:T(1024)S(1)} %get-tuple-element.322), kind=kOutput, calls=%fused_computation.20.clone.1 | convolution fusion | flops 6459228160 | bytes 4202496 | tf_op jit(solution)/shard_map/while/body/eval_jaxpr/rak,kj->raj/dot_general | solution.py:42
  566.4 24.2 %fusion.222 = f32[16,32,1024]{2,1,0:T(8,128)S(1)} fusion(f32[16,32,1024]{2,1,0:T(8,128)S(1)} %bitcast.166, s32[1024]{0:T(1024)S(1)} %get-tuple-element.323, s32[1024]{0:T(1024)S(1)} %get-tuple-element.322), kind=kOutput, calls=%fused_computation.17.clone.1 | convolution fusion | flops 6459228160 | bytes 4202496 | tf_op jit(solution)/shard_map/while/body/eval_jaxpr/rak,kj->raj/dot_general | solution.py:42
  609.7 31.6 %fusion.227 = f32[32,32,1024]{2,1,0:T(8,128)S(1)} fusion(f32[32,1024,32]{1,2,0:T(8,128)S(1)} %fusion.225, f32[32,1024,32]{1,2,0:T(8,128)S(1)} %fusion.226, s32[1024]{0:T(1024)S(1)} %get-tuple-element.323, s32[1024]{0:T(1024)S(1)} %get-tuple-element.322), kind=kOutput, calls=%fused_computation.12.clone.1 | convolution fusion | flops 12902727680 | bytes 12591104 | tf_op jit(solution)/shard_map/while/body/eval_jaxpr/rak,kj->raj/dot_general | solution.py:42
  652.6 31.4 %subtract_multiply_fusion.2 = f32[32,32,1024]{2,1,0:T(8,128)S(1)} fusion(f32[32,32,1024]{2,1,0:T(8,128)S(1)} %fusion.227, s32[1024]{0:T(1024)S(1)} %get-tuple-element.323, s32[1024]{0:T(1024)S(1)} %get-tuple-element.322, f32[32,1024,32]{1,2,0:T(8,128)S(1)} %fusion.228, f32[32,1024,32]{1,2,0:T(8,128)S(1)} %fusion.229), kind=kOutput, calls=%fused_computation.22.clone.1 | convolution fusion | flops 12904824832 | bytes 16785408 | tf_op jit(solution)/shard_map/while/body/eval_jaxpr/rak,kj->raj/dot_general | solution.py:42
  697.9 23.6 %fusion.220 = f32[16,32,1024]{2,1,0:T(8,128)S(1)} fusion(f32[16,32,1024]{2,1,0:T(8,128)S(1)} %bitcast.165, s32[1024]{0:T(1024)S(1)} %get-tuple-element.323, s32[1024]{0:T(1024)S(1)} %get-tuple-element.322), kind=kOutput, calls=%fused_computation.20.clone.1 | convolution fusion | flops 6459228160 | bytes 4202496 | tf_op jit(solution)/shard_map/while/body/eval_jaxpr/rak,kj->raj/dot_general | solution.py:42
  723.7 24.2 %fusion.222 = f32[16,32,1024]{2,1,0:T(8,128)S(1)} fusion(f32[16,32,1024]{2,1,0:T(8,128)S(1)} %bitcast.166, s32[1024]{0:T(1024)S(1)} %get-tuple-element.323, s32[1024]{0:T(1024)S(1)} %get-tuple-element.322), kind=kOutput, calls=%fused_computation.17.clone.1 | convolution fusion | flops 6459228160 | bytes 4202496 | tf_op jit(solution)/shard_map/while/body/eval_jaxpr/rak,kj->raj/dot_general | solution.py:42
  767.1 31.6 %fusion.227 = f32[32,32,1024]{2,1,0:T(8,128)S(1)} fusion(f32[32,1024,32]{1,2,0:T(8,128)S(1)} %fusion.225, f32[32,1024,32]{1,2,0:T(8,128)S(1)} %fusion.226, s32[1024]{0:T(1024)S(1)} %get-tuple-element.323, s32[1024]{0:T(1024)S(1)} %get-tuple-element.322), kind=kOutput, calls=%fused_computation.12.clone.1 | convolution fusion | flops 12902727680 | bytes 12591104 | tf_op jit(solution)/shard_map/while/body/eval_jaxpr/rak,kj->raj/dot_general | solution.py:42
  810.0 31.4 %subtract_multiply_fusion.2 = f32[32,32,1024]{2,1,0:T(8,128)S(1)} fusion(f32[32,32,1024]{2,1,0:T(8,128)S(1)} %fusion.227, s32[1024]{0:T(1024)S(1)} %get-tuple-element.323, s32[1024]{0:T(1024)S(1)} %get-tuple-element.322, f32[32,1024,32]{1,2,0:T(8,128)S(1)} %fusion.228, f32[32,1024,32]{1,2,0:T(8,128)S(1)} %fusion.229), kind=kOutput, calls=%fused_computation.22.clone.1 | convolution fusion | flops 12904824832 | bytes 16785408 | tf_op jit(solution)/shard_map/while/body/eval_jaxpr/rak,kj->raj/dot_general | solution.py:42
  860.8 60.3 %copy.19 = f32[8,8,32768]{1,0,2:T(8,128)} copy(f32[8,8,32768]{2,1,0:T(8,128)} %bitcast.168) | data formatting | bytes 16777216 | tf_op jit(solution)/shard_map/reshape | solution.py:79
  921.1 125.0 %reshape.705 = f32[8,1,262144]{2,1,0:T(1,128)} reshape(f32[32768,8,8]{2,1,0:T(8,128)} %bitcast.106) | data formatting | bytes 16777216
  1099.4 133.9 %all-to-all-done.1 = f32[8,1,262144]{2,1,0:T(1,128)} async-done(((f32[8,1,262144]{2,1,0:T(1,128)}), f32[8,1,262144]{2,1,0:T(1,128)}, u32[]{:S(2)}, u32[]{:S(2)}) %all-to-all-start.1) | async-done | bytes 8388640 | tf_op jit(solution)/shard_map/all_to_all | solution.py:105
  1233.8 26.3 %reduce.151 = f32[8,262144]{1,0:T(8,128)} reduce(f32[8,1,262144]{2,1,0:T(1,128)} %all-to-all-done.1, f32[]{:T(128)} %broadcast.1472), dimensions={1}, to_apply=%all_to_all.25.reduce_sub_computation | reduce | bytes 16777220 | tf_op jit(solution)/shard_map/all_to_all | solution.py:105
  1260.1 135.8 %reshape.706 = f32[32768,8,8]{2,1,0:T(8,128)} reshape(f32[8,262144]{1,0:T(8,128)} %reduce.151) | data formatting | bytes 16777216
  1395.9 73.3 %copy.20 = f32[8,8,8,4096]{3,1,2,0:T(8,128)} copy(f32[8,8,8,4096]{1,0,3,2:T(8,128)} %bitcast.5) | data formatting | bytes 16777216 | tf_op jit(solution)/shard_map/all_to_all | solution.py:105
  (165 shorter events, 319.8 us)
Async XLA Ops:
  1.0 4.4 collective-permute-start.1
  2.9 5.1 collective-permute-start
  26.0 6.6 copy-start
  26.0 6.8 copy-start.1
  26.0 185.0 %all-to-all-start = ((f32[8,64,4096]{2,0,1:T(8,128)}), f32[8,64,4096]{2,0,1:T(8,128)}, u32[]{:S(2)}, u32[]{:S(2)}) async-start(f32[8,64,4096]{2,0,1:T(8,128)} %copy.17), calls=%async_computation | async-start | bytes 16777216 | tf_op jit(solution)/shard_map/all_to_all | solution.py:103
  1046.2 8.4 copy-start.2
  1046.2 28.5 %copy-start.3 = (f32[32]{0:T(128)S(1)}, f32[32]{0:T(128)}, u32[]{:S(2)}) copy-start(f32[32]{0:T(128)} %param.10) | copy-start | bytes 388
  1046.2 187.1 %all-to-all-start.1 = ((f32[8,1,262144]{2,1,0:T(1,128)}), f32[8,1,262144]{2,1,0:T(1,128)}, u32[]{:S(2)}, u32[]{:S(2)}) async-start(f32[8,1,262144]{2,1,0:T(1,128)} %reshape.705), calls=%async_computation.1 | async-start | bytes 16777216 | tf_op jit(solution)/shard_map/all_to_all | solution.py:105
where the time goes:
time: 1520 us; the launch traced here: 1510 us
  matrix products  582 us (38%)
  local copies, waits for them, and re-layouts  457 us (30%)
  waiting for transfers between devices  314 us (21%)
  other arithmetic  98.7 us (6%)
  blocking collectives  23.6 us (2%)
  starting transfers between devices  19.3 us (1%)
    dot_general x16, matrix products, plane_product(): return jnp.einsum('rak,kj->raj', values, table, precision=highest)  443 us
    unnamed x11, local copies, waits for them, and re-layouts  261 us
    all_to_all x1, waiting for transfers between devices, on_device(): lax.all_to_all(sectioned, 'vel', split_axis=1, concat_axis=2, tiled=True)  178 us
    all_to_all x1, waiting for transfers between devices, on_device(): lax.all_to_all(cubes_out, 'vel', split_axis=2, concat_axis=1, tiled=True)  134 us
    dot_general x32, matrix products, line_product(): return jnp.einsum('rak,ab->rbk', values, table, precision=highest)  130 us
    all_to_all x2, local copies, waits for them, and re-layouts, on_device(): lax.all_to_all(cubes_out, 'vel', split_axis=2, concat_axis=1, tiled=True)  73.8 us
    reshape x1, local copies, waits for them, and re-layouts, collide_items(): lax.map(one_group, grouped).reshape(item_count, group_size, cube_size)  60.3 us
  transfers between devices with their start and end apart: 4, of which 3 were waited for; matrix products, arithmetic and copies ran while one was open for 3% of the time, Pallas kernels for 0%

commit v1 on v0

v1 whole, which is shorter than its diff:
```python
import functools
import math

import jax
import jax.numpy as jnp
import numpy as np
from jax import lax
from jax.experimental import pallas as pl
from jax.experimental.pallas import tpu as pltpu
from jax.sharding import PartitionSpec as P

courant = 0.9
top_speed = 3.0
collide_rate = 0.5
accommodation = 0.8
highest = lax.Precision.HIGHEST
sub = 8
lane = 128
parts = 2
vmem_bytes = 56 * 2**20


def split_table(table):
    high = table.astype(np.float32).astype(jnp.bfloat16)
    low = (table - high.astype(np.float64)).astype(np.float32).astype(jnp.bfloat16)
    return jnp.asarray(high), jnp.asarray(low)


def dft_tables(points):
    half = points // 2
    plane = points * points
    self_modes = [(0, 0), (0, half), (half, 0), (half, half)]
    reps = [(kb, kc) for kb in range(points) for kc in range(1, half)]
    reps += [(kb, 0) for kb in range(1, half)] + [(kb, half) for kb in range(1, half)]
    pairs = [(self_modes[0], self_modes[1]), (self_modes[2], self_modes[3])]
    slots = len(reps) + len(pairs)
    outer, inner = np.divmod(np.arange(plane), points)

    def angle(mode):
        return 2.0 * np.pi / points * ((outer * mode[0] + inner * mode[1]) % points)

    to_modes = np.zeros((plane, plane))
    from_modes = np.zeros((plane, plane))
    for slot, mode in enumerate(reps):
        theta = angle(mode)
        to_modes[:, slot] = np.cos(theta)
        to_modes[:, slots + slot] = -np.sin(theta)
        from_modes[slot] = 2.0 * np.cos(theta)
        from_modes[slots + slot] = -2.0 * np.sin(theta)
    for slot, (first, second) in enumerate(pairs, len(reps)):
        to_modes[:, slot] = from_modes[slot] = np.cos(angle(first))
        to_modes[:, slots + slot] = from_modes[slots + slot] = np.cos(angle(second))
    from_modes /= points * plane
    line = np.arange(points)
    theta = 2.0 * np.pi / points * (line[:, None] * line[None, :] % points)
    forward = np.block([[np.cos(theta), np.sin(theta)], [-np.sin(theta), np.cos(theta)]])
    forward = np.kron(forward, np.eye(sub))

    pick = np.zeros((2, plane, slots + lane), np.float32)

    def add(mode, column, weight):
        kb, kc = mode
        pick[0, kb * points + kc, column] += 0.5 * weight
        pick[1, -kb % points * points + -kc % points, column] += 0.5 * weight

    for slot, mode in enumerate(reps):
        add(mode, slot, 1.0)
    for slot, (first, second) in enumerate(pairs, len(reps)):
        add(first, slot, 0.5)
        add(second, slot, 0.5)
        add(first, slot + lane, 0.5)
        add(second, slot + lane, -0.5)
    return {
        "to_modes": split_table(to_modes),
        "from_modes": split_table(from_modes),
        "forward": split_table(forward),
        "backward": split_table(forward.T),
        "pick": jnp.asarray(pick.reshape(2 * plane, slots + lane)),
    }


def multipliers(spectrum, pick):
    points = spectrum.shape[0]
    rows = spectrum.reshape(points, points * points)
    mirrored = jnp.concatenate([rows[:1], lax.rev(rows[1:], (0,))], axis=0)
    both = jnp.concatenate([rows, mirrored], axis=1)
    return jnp.repeat(jnp.dot(both, pick, precision=highest), sub, axis=0)


def split(values):
    high = values.astype(jnp.bfloat16)
    return high, (values - high.astype(jnp.float32)).astype(jnp.bfloat16)


def dot(a, b):
    return jnp.dot(a, b, preferred_element_type=jnp.float32)


def move_kernel(rows_total, first_block, turn, body, before, after, low, high, nu, out):
    step = pl.program_id(0)
    block = jnp.where(step < turn[0], first_block + step, turn[1] + step)
    rows = body.shape[0]
    here = body[...]
    row = lax.broadcasted_iota(jnp.int32, here.shape, 0)
    first = jnp.where(block == 0, low[...], before[sub - 1 :, :])
    last = jnp.where(block == rows_total // rows - 1, high[...], after[:1, :])
    left = jnp.where(row == 0, first, pltpu.roll(here, 1, 0))
    right = jnp.where(row == rows - 1, last, pltpu.roll(here, rows - 1, 0))
    drift = nu[...]
    rising = jnp.broadcast_to(drift > 0, here.shape)
    out[...] = here - drift * jnp.where(rising, here - left, right - here)


def move(particles, low, high, nu, first_block, turn, count, rows):
    total, width = particles.shape
    per = rows // sub

    def block(step):
        return jnp.where(step < turn[0], first_block + step, turn[1] + step)

    return pl.pallas_call(
        functools.partial(move_kernel, total, first_block, turn),
        grid=(count,),
        in_specs=[
            pl.BlockSpec((rows, width), lambda i: (block(i), 0)),
            pl.BlockSpec((sub, width), lambda i: (jnp.maximum(block(i) * per - 1, 0), 0)),
            pl.BlockSpec((sub, width), lambda i: (jnp.minimum((block(i) + 1) * per, total // sub - 1), 0)),
            pl.BlockSpec((1, width), lambda i: (0, 0)),
            pl.BlockSpec((1, width), lambda i: (0, 0)),
            pl.BlockSpec((1, width), lambda i: (0, 0)),
        ],
        out_specs=pl.BlockSpec((rows, width), lambda i: (i, 0)),
        out_shape=jax.ShapeDtypeStruct((count * rows, width), jnp.float32),
        compiler_params=pltpu.CompilerParams(vmem_limit_bytes=vmem_bytes),
        cost_estimate=pl.CostEstimate(
            flops=5 * count * rows * width, bytes_accessed=8 * count * rows * width, transcendentals=0
        ),
    )(particles, particles, particles, low, high, nu)


def collide_kernel(
    x, to_high, to_low, from_high, from_low, ahead_high, ahead_low, back_high, back_low, gain, freq,
    out, mass, wide_high, wide_low, mid, both_high, both_low, fields,
):
    sources, cells, width = x.shape
    plane = to_high.shape[0]
    slots = plane // 2
    planes = width // plane
    points = sources * planes
    groups = cells // sub
    chunk = points * sub
    tile = min(256, plane)

    def where_of(a):
        return a // planes, slice(a % planes * plane, (a % planes + 1) * plane)

    for group in range(groups):
        for a in range(points):
            source, columns = where_of(a)
            mid[(group * points + a) * sub : (group * points + a + 1) * sub, :] = x[
                source, group * sub : (group + 1) * sub, columns
            ]
    high, low = split(mid[...])
    wide_high[: groups * chunk, :] = high
    wide_low[: groups * chunk, :] = low

    @pl.loop(0, plane // tile)
    def _(at):
        columns = pl.ds(pl.multiple_of(at * tile, tile), tile)
        table = to_high[:, columns]
        mid[:, columns] = (
            dot(wide_low[: groups * chunk, :], table)
            + dot(wide_high[: groups * chunk, :], to_low[:, columns])
            + dot(wide_high[: groups * chunk, :], table)
        )

    @pl.loop(0, groups)
    def _(group):
        rows = pl.ds(pl.multiple_of(group * chunk, chunk), chunk)
        spectrum = jnp.concatenate([mid[rows, :slots], mid[rows, slots:]], axis=0)
        high, low = split(spectrum)
        waves = dot(ahead_high[...], low) + dot(ahead_low[...], high) + dot(ahead_high[...], high)
        real, imag = waves[:chunk], waves[chunk:]

        def mirror(values):
            tail = values[:, slots - lane :]
            turned = [tail[-a % points * sub : (-a % points + 1) * sub] for a in range(points)]
            return jnp.concatenate(turned, axis=0)

        real_tail, imag_tail = mirror(real), mirror(imag)
        for index, table in enumerate((gain, freq)):
            pad = jnp.zeros((chunk, slots - lane), jnp.float32)
            extra = table[:, slots:]
            upper = real * table[:, :slots] + jnp.concatenate([pad, real_tail * extra], axis=1)
            lower = imag * table[:, :slots] - jnp.concatenate([pad, imag_tail * extra], axis=1)
            for start, values in ((0, upper), (chunk, lower)):
                high, low = split(values)
                both_high[start : start + chunk, index * slots : (index + 1) * slots] = high
                both_low[start : start + chunk, index * slots : (index + 1) * slots] = low
        for index in range(2):
            columns = slice(index * slots, (index + 1) * slots)
            lines = (
                dot(back_high[...], both_low[:, columns])
                + dot(back_low[...], both_high[:, columns])
                + dot(back_high[...], both_high[:, columns])
            )
            high, low = split(jnp.concatenate([lines[:chunk], lines[chunk:]], axis=1))
            at = pl.ds(pl.multiple_of((index * groups + group) * chunk, chunk), chunk)
            wide_high[at, :] = high
            wide_low[at, :] = low

    @pl.loop(0, plane // tile)
    def _(at):
        columns = pl.ds(pl.multiple_of(at * tile, tile), tile)
        table = from_high[:, columns]
        fields[:, columns] = (
            dot(wide_low[...], table) + dot(wide_high[...], from_low[:, columns]) + dot(wide_high[...], table)
        )

    for group in range(groups):
        total = jnp.zeros((sub, plane), jnp.float32)
        for a in range(points):
            source, columns = where_of(a)
            start = (group * points + a) * sub
            cells_here = slice(group * sub, (group + 1) * sub)
            here = x[source, cells_here, columns]
            gained = fields[start : start + sub, :]
            lost = fields[groups * chunk + start : groups * chunk + start + sub, :]
            post = here + collide_rate * (gained - here * lost)
            out[source, cells_here, columns] = post
            total = total + post
        lanes = total[:, :lane]
        for at in range(lane, plane, lane):
            lanes = lanes + total[:, at : at + lane]
        mass[group * sub : (group + 1) * sub, :] = lanes


def collide(cubes, tables, gain, freq):
    sources, cells, width = cubes.shape
    plane = tables["to_modes"][0].shape[0]
    points = sources * width // plane
    step = math.gcd(cells, 2 * sub)
    chunk = step * points
    operands = [*tables["to_modes"], *tables["from_modes"], *tables["forward"], *tables["backward"], gain, freq]
    whole = pl.BlockSpec(memory_space=pltpu.VMEM)
    bf16, f32 = jnp.bfloat16, jnp.float32
    multiply_adds = 3 * cells * points * (3 * plane * plane + 6 * points * sub * plane)
    return pl.pallas_call(
        collide_kernel,
        grid=(cells // step,),
        in_specs=[pl.BlockSpec((sources, step, width), lambda i: (0, i, 0))] + [whole] * len(operands),
        out_specs=[
            pl.BlockSpec((sources, step, width), lambda i: (0, i, 0)),
            pl.BlockSpec((step, lane), lambda i: (i, 0)),
        ],
        out_shape=[
            jax.ShapeDtypeStruct(cubes.shape, f32),
            jax.ShapeDtypeStruct((cells, lane), f32),
        ],
        scratch_shapes=[
            pltpu.VMEM((2 * chunk, plane), bf16),
            pltpu.VMEM((2 * chunk, plane), bf16),
            pltpu.VMEM((chunk, plane), f32),
            pltpu.VMEM((2 * points * sub, plane), bf16),
            pltpu.VMEM((2 * points * sub, plane), bf16),
            pltpu.VMEM((2 * chunk, plane), f32),
        ],
        compiler_params=pltpu.CompilerParams(vmem_limit_bytes=vmem_bytes),
        cost_estimate=pl.CostEstimate(
            flops=2 * multiply_adds, bytes_accessed=8 * cubes.size, transcendentals=0
        ),
    )(cubes, *operands)


def settle_kernel(post, member, emit_high, emit_low, *rest):
    out = rest[-1]
    chosen = member[...]
    share = jnp.sum(chosen, axis=1, keepdims=True)
    picked = chosen.astype(jnp.bfloat16)
    emission = dot(picked, emit_low[...]) + dot(picked, emit_high[...])
    out[...] = post[...] + accommodation * (emission - share * post[...])


def settle(post, member, emit, earlier, shape, first_block, turn, rows):
    count = post.shape[0] // rows
    width = post.shape[1]
    panels = member.shape[1]

    def block(step):
        return jnp.where(step < turn[0], first_block + step, turn[1] + step)

    operands = [post, member, *emit]
    in_specs = [
        pl.BlockSpec((rows, width), lambda i: (i, 0)),
        pl.BlockSpec((rows, panels), lambda i: (i, 0)),
        pl.BlockSpec((panels, width), lambda i: (0, 0)),
        pl.BlockSpec((panels, width), lambda i: (0, 0)),
    ]
    aliases = {}
    if earlier is not None:
        aliases = {len(operands): 0}
        operands.append(earlier)
        in_specs.append(pl.BlockSpec(memory_space=pl.ANY))
    return pl.pallas_call(
        settle_kernel,
        grid=(count,),
        in_specs=in_specs,
        out_specs=pl.BlockSpec((rows, width), lambda i: (block(i), 0)),
        out_shape=jax.ShapeDtypeStruct(shape, jnp.float32),
        input_output_aliases=aliases,
        compiler_params=pltpu.CompilerParams(vmem_limit_bytes=vmem_bytes),
        cost_estimate=pl.CostEstimate(
            flops=4 * panels * post.size, bytes_accessed=8 * post.size, transcendentals=0
        ),
    )(*operands)


def on_device(particles, gain_spectrum, freq_spectrum, panel_temp, wall_cells):
    cell_dev, vel_dev = particles.shape
    points = gain_spectrum.shape[0]
    plane_size = points * points
    planes = vel_dev // plane_size
    vel_count = lax.axis_size("vel")
    vel_at = lax.axis_index("vel")
    space_at = lax.axis_index("space")
    space_count = lax.axis_size("space")
    tables = dft_tables(points)

    columns = jnp.arange(vel_dev, dtype=jnp.int32)
    plane_index = vel_at * planes + columns // plane_size
    nu = (courant * (2 * plane_index + 1 - points).astype(jnp.float32) / points)[None, :]

    up = [(i, i + 1) for i in range(space_count - 1)]
    down = [(i + 1, i) for i in range(space_count - 1)]
    low = lax.ppermute(particles[-1:], "space", up)
    high = lax.ppermute(particles[:1], "space", down)

    rows = math.gcd(cell_dev // (2 * parts), 32)
    blocks = cell_dev // rows
    quarter, half = blocks // 4, blocks // 2
    zero = jnp.zeros((1, vel_dev), jnp.float32)
    plans = [(quarter, (half, 0)), (0, (quarter, half))]
    edges = [(zero, zero), (low, high)]
    share = half * rows // vel_count

    def cells_of(plan):
        first_block, turn = plan
        step = jnp.arange(half, dtype=jnp.int32)
        block = jnp.where(step < turn[0], first_block + step, turn[1] + step)
        at = block[:, None] * rows + jnp.arange(rows, dtype=jnp.int32)[None, :]
        return space_at * cell_dev + at.reshape(-1)

    def membership(cell_ids):
        panels, per_panel = wall_cells.shape
        hit = wall_cells.reshape(1, panels, per_panel) == cell_ids[:, None, None]
        return jnp.any(hit, axis=2).astype(jnp.float32)

    arrived = []
    for plan, edge in zip(plans, edges):
        moved = move(particles, *edge, nu, *plan, half, rows)
        moved = moved.reshape(vel_count, share, vel_dev)
        arrived.append(lax.all_to_all(moved, "vel", 0, 0, tiled=True))

    gain = multipliers(gain_spectrum, tables["pick"])
    freq = multipliers(freq_spectrum, tables["pick"])
    panels, per_panel = wall_cells.shape
    members = [membership(cells_of(plan)) for plan in plans]
    returned = []
    part_mass = jnp.zeros((panels,), jnp.float32)
    for cubes, member in zip(arrived, members):
        post, mass = collide(cubes, tables, gain, freq)
        returned.append(lax.all_to_all(post, "vel", 0, 0, tiled=True))
        mine = lax.dynamic_slice_in_dim(member, vel_at * share, share, axis=0)
        part_mass = part_mass + jnp.sum(mine * jnp.sum(mass, axis=1)[:, None], axis=0)
    wall_mass = lax.psum(part_mass, ("space", "vel"))

    line = jnp.arange(points, dtype=jnp.int32)
    velocity = top_speed * (2 * line + 1 - points).astype(jnp.float32) / points
    line_weight = jnp.exp(-(velocity**2)[None, :] / (2.0 * panel_temp[:, None]))
    normal_sum = jnp.sum(line_weight, axis=1) ** 3

    def speed(index):
        return top_speed * (2 * index + 1 - points).astype(jnp.float32) / points

    speed_sq = speed(plane_index) ** 2 + speed(columns // points % points) ** 2 + speed(columns % points) ** 2
    profile = jnp.exp(-speed_sq[None, :] / (2.0 * panel_temp[:, None]))
    maxwellian = profile / normal_sum[:, None]
    emission = (wall_mass / per_panel)[:, None] * maxwellian
    emit_high = lax.reduce_precision(emission, exponent_bits=8, mantissa_bits=7)
    emit = (emit_high.astype(jnp.bfloat16), (emission - emit_high).astype(jnp.bfloat16))

    out = None
    for back, member, plan in zip(returned, members, plans):
        out = settle(back.reshape(half * rows, vel_dev), member, emit, out, particles.shape, *plan, rows)
    return out


def solution(mesh):
    in_specs = (P("space", "vel"), P(), P(), P(), P())
    out_specs = P("space", "vel")
    return jax.shard_map(on_device, mesh=mesh, in_specs=in_specs, out_specs=out_specs, check_vma=False)
```

time: 1520 us -> 440 us (0.29)
  matrix products: 582 us -> 8.09 us
  local copies, waits for them, and re-layouts: 457 us -> 16.5 us
  waiting for transfers between devices: 314 us -> 149 us
  Pallas kernels: 0 us -> 114 us
  other arithmetic: 98.7 us -> 2.69 us
  blocking collectives: 23.6 us -> 110 us
    dot_general x50 -> x4, matrix products: 582 us -> 8.09 us  [multipliers(): return jnp.repeat(jnp.dot(both, pick, precision=highest), sub, axis=0)]
    unnamed x11 -> x27, local copies, waits for them, and re-layouts: 261 us -> 0.72 us
    all_to_all x2 -> x4, waiting for transfers between devices: 312 us -> 147 us  [the longest x2 99.1 us: on_device(): arrived.append(lax.all_to_all(moved, 'vel', 0, 0, tiled=True))]
    pallas_call x0 -> x6, Pallas kernels: none -> 114 us  [the longest x2 83.3 us: collide(): pl.pallas_call(collide_kernel, grid=(cells // step,), in_specs=[pl.BlockS...]
    psum x2 -> x1, blocking collectives: 23.6 us -> 110 us  [on_device(): wall_mass = lax.psum(part_mass, ('space', 'vel'))]
    all_to_all x3 -> x0, local copies, waits for them, and re-layouts: 85.3 us -> none  [the longest x2 73.8 us: on_device(): lax.all_to_all(cubes_out, 'vel', split_axis=2, concat_axis=1, tiled=True)]
    reshape x4 -> x3, local copies, waits for them, and re-layouts: 68.9 us -> 1.65 us  [the longest x1 1.18 us: multipliers(): return jnp.repeat(jnp.dot(both, pick, precision=highest), sub, axis=0)]
    gather x65 -> x0, other arithmetic: 26.9 us -> none  [the longest x26 19.3 us: on_device(): third_vel = velocity[columns % points]]
  transfers between devices with their start and end apart: 4 -> 6, of which waited for: 3 -> 4; matrix products, arithmetic and copies ran while one was open for 3% -> 6% of each run, Pallas kernels for 0% -> 23%
where the time goes in v1:
time: 440 us; the launch traced here: 435 us
  waiting for transfers between devices  149 us (34%)
  Pallas kernels  114 us (26%)
  blocking collectives  110 us (25%)
  starting transfers between devices  34.3 us (8%)
  local copies, waits for them, and re-layouts  16.5 us (4%)
  matrix products  8.09 us (2%)
    psum x1, blocking collectives, on_device(): wall_mass = lax.psum(part_mass, ('space', 'vel'))  110 us
    all_to_all x2, waiting for transfers between devices, on_device(): arrived.append(lax.all_to_all(moved, 'vel', 0, 0, tiled=True))  99.1 us
    pallas_call x2, Pallas kernels, collide(): pl.pallas_call(collide_kernel, grid=(cells // step,), in_specs=[pl.BlockS...  83.3 us
    all_to_all x2, waiting for transfers between devices, on_device(): returned.append(lax.all_to_all(post, 'vel', 0, 0, tiled=True))  47.6 us
    all_to_all x2, starting transfers between devices, on_device(): returned.append(lax.all_to_all(post, 'vel', 0, 0, tiled=True))  15.9 us
    pallas_call x2, Pallas kernels, move(): pl.pallas_call(functools.partial(move_kernel, total, first_block, turn),...  15.7 us
    pallas_call x2, Pallas kernels, settle(): pl.pallas_call(settle_kernel, grid=(count,), in_specs=in_specs, out_specs...  15.3 us
    all_to_all x2, starting transfers between devices, on_device(): arrived.append(lax.all_to_all(moved, 'vel', 0, 0, tiled=True))  14.1 us
  transfers between devices with their start and end apart: 6, of which 4 were waited for; matrix products, arithmetic and copies ran while one was open for 6% of the time, Pallas kernels for 23%

profile of v1, /device:TPU:18, one launch (start us, length us, event | category | flops | bytes accessed | tf_op | source)
XLA Modules:
  0.0 435.4 jit_solution(15777496733498512857)
XLA Ops:
  1.2 7.9 %shard_map.138 = f32[256,4096]{1,0:T(8,128)} custom-call(f32[512,4096]{1,0:T(8,128)} %after.3, f32[512,4096]{1,0:T(8,128)} %after.3, f32[512,4096]{1,0:T(8,128)} %after.3, f32[1,4096]{1,0:T(1,128)} %broadcast_in_dim.8.low.high, f32[1,4096]{1,0:T(1,128)} %broadcast_in_dim.8.low.high, f32[1,4096]{1,0:T(1,128)} %fusion.34.nu), custom_call_target="tpu_custom_call" | custom-call | flops 5242880 | bytes 8388608 | tf_op jit(solution)/shard_map/pallas_call | solution.py:121
  9.2 6.2 %all-to-all-start.2 = ((f32[8,32,4096]{2,1,0:T(8,128)}), f32[8,32,4096]{2,1,0:T(8,128)}, u32[]{:S(2)}, u32[]{:S(2)}) async-start(f32[8,32,4096]{2,1,0:T(8,128)} %bitcast.19), calls=%async_computation.2 | async-start | bytes 8388608 | tf_op jit(solution)/shard_map/all_to_all | solution.py:362
  16.4 1.9 collective-permute-start.1
  18.3 2.4 collective-permute-start
  20.7 2.6 collective-permute-done.low
  23.9 7.8 %shard_map.136 = f32[256,4096]{1,0:T(8,128)} custom-call(f32[512,4096]{1,0:T(8,128)} %after.3, f32[512,4096]{1,0:T(8,128)} %after.3, f32[512,4096]{1,0:T(8,128)} %after.3, f32[1,4096]{1,0:T(1,128)} %copy-done.8, f32[1,4096]{1,0:T(1,128)} %copy-done.7, f32[1,4096]{1,0:T(1,128)} %fusion.34.nu), custom_call_target="tpu_custom_call" | custom-call | flops 5242880 | bytes 8388608 | tf_op jit(solution)/shard_map/pallas_call | solution.py:121
  31.7 73.5 %all-to-all-done.2.x = f32[8,32,4096]{2,1,0:T(8,128)} async-done(((f32[8,32,4096]{2,1,0:T(8,128)}), f32[8,32,4096]{2,1,0:T(8,128)}, u32[]{:S(2)}, u32[]{:S(2)}) %all-to-all-start.2) | async-done | bytes 4194336 | tf_op jit(solution)/shard_map/all_to_all | solution.py:362
  105.3 8.0 %all-to-all-start = ((f32[8,32,4096]{2,1,0:T(8,128)}), f32[8,32,4096]{2,1,0:T(8,128)}, u32[]{:S(2)}, u32[]{:S(2)}) async-start(f32[8,32,4096]{2,1,0:T(8,128)} %bitcast.18), calls=%async_computation | async-start | bytes 8388608 | tf_op jit(solution)/shard_map/all_to_all | solution.py:362
  116.0 1.9 slice.35
  117.9 4.1 rev.6
  122.9 3.0 rev.7
  125.9 3.4 convolution_bitcast_fusion.1
  129.4 1.6 convolution_add_fusion.1
  131.0 1.5 convolution_bitcast_fusion
  132.5 1.6 convolution_add_fusion
  135.3 41.7 %shard_map.139 = (f32[8,32,4096]{2,1,0:T(8,128)}, f32[32,128]{1,0:T(8,128)}) custom-call(f32[8,32,4096]{2,1,0:T(8,128)} %all-to-all-done.2.x, bf16[1024,1024]{1,0:T(8,128)(2,1)} %constant.131.clone.to_high, bf16[1024,1024]{1,0:T(8,128)(2,1)} %constant.132.clone.to_low, bf16[1024,1024]{1,0:T(8,128)(2,1)} %constant.133.clone.from_high, ...), custom_call_target="tpu_custom_call" | custom-call | flops 28991029248 | bytes 8388608 | tf_op jit(solution)/shard_map/pallas_call | solution.py:248
  177.0 25.6 %all-to-all-done.x = f32[8,32,4096]{2,1,0:T(8,128)} async-done(((f32[8,32,4096]{2,1,0:T(8,128)}), f32[8,32,4096]{2,1,0:T(8,128)}, u32[]{:S(2)}, u32[]{:S(2)}) %all-to-all-start) | async-done | bytes 4194336 | tf_op jit(solution)/shard_map/all_to_all | solution.py:362
  202.5 7.9 %all-to-all-start.3 = ((f32[8,32,4096]{2,1,0:T(8,128)}), f32[8,32,4096]{2,1,0:T(8,128)}, u32[]{:S(2)}, u32[]{:S(2)}) async-start(f32[8,32,4096]{2,1,0:T(8,128)} %get-tuple-element.12), calls=%async_computation.3 | async-start | bytes 8388608 | tf_op jit(solution)/shard_map/all_to_all | solution.py:372
  210.4 41.6 %shard_map.137 = (f32[8,32,4096]{2,1,0:T(8,128)}, f32[32,128]{1,0:T(8,128)}) custom-call(f32[8,32,4096]{2,1,0:T(8,128)} %all-to-all-done.x, bf16[1024,1024]{1,0:T(8,128)(2,1)} %constant.131.clone.to_high, bf16[1024,1024]{1,0:T(8,128)(2,1)} %constant.132.clone.to_low, bf16[1024,1024]{1,0:T(8,128)(2,1)} %constant.133.clone.from_high, ...), custom_call_target="tpu_custom_call" | custom-call | flops 28991029248 | bytes 8388608 | tf_op jit(solution)/shard_map/pallas_call | solution.py:248
  252.0 47.6 %all-to-all-done.3 = f32[8,32,4096]{2,1,0:T(8,128)} async-done(((f32[8,32,4096]{2,1,0:T(8,128)}), f32[8,32,4096]{2,1,0:T(8,128)}, u32[]{:S(2)}, u32[]{:S(2)}) %all-to-all-start.3) | async-done | bytes 4194336 | tf_op jit(solution)/shard_map/all_to_all | solution.py:372
  299.6 8.0 %all-to-all-start.1 = ((f32[8,32,4096]{2,1,0:T(8,128)}), f32[8,32,4096]{2,1,0:T(8,128)}, u32[]{:S(2)}, u32[]{:S(2)}) async-start(f32[8,32,4096]{2,1,0:T(8,128)} %get-tuple-element.9), calls=%async_computation.1 | async-start | bytes 8388608 | tf_op jit(solution)/shard_map/all_to_all | solution.py:372
  309.2 109.8 %psum.7 = f32[32]{0:T(128)S(1)} all-reduce(f32[32]{0:T(128)S(1)} %add.214), channel_id=1, replica_groups=mesh['space'=4,'vel'=8] {'space','vel'}, use_global_device_ids=true, to_apply=%region_6.7 | all-reduce | flops 32 | bytes 256 | tf_op jit(solution)/shard_map/psum | solution.py:375
  420.1 7.6 %shard_map.140.rest_0_ = f32[512,4096]{1,0:T(8,128)} custom-call(f32[256,4096]{1,0:T(8,128)} %bitcast.7.post, f32[256,32]{1,0:T(8,128)} %copy-done.5, bf16[32,4096]{1,0:T(8,128)(2,1)} %get-tuple-element.18.emit_high, bf16[32,4096]{1,0:T(8,128)(2,1)} %get-tuple-element.17.emit_low), custom_call_target="tpu_custom_call" | custom-call | flops 134217728 | bytes 8388608 | tf_op jit(solution)/shard_map/pallas_call | solution.py:304
  427.7 7.7 %shard_map.141 = f32[512,4096]{1,0:T(8,128)} custom-call(f32[256,4096]{1,0:T(8,128)} %bitcast.5.post, f32[256,32]{1,0:T(8,128)} %copy-done.4, bf16[32,4096]{1,0:T(8,128)(2,1)} %get-tuple-element.18.emit_high, bf16[32,4096]{1,0:T(8,128)(2,1)} %get-tuple-element.17.emit_low, f32[512,4096]{1,0:T(8,128)} %shard_map.140.rest_0_), custom_call_target="tpu_custom_call", output_to_operand_aliasing={{}: (4, {})} | custom-call | flops 134217728 | bytes 8388608 | tf_op jit(solution)/shard_map/pallas_call | solution.py:304
  (66 shorter events, 10.2 us)
Async XLA Ops:
  9.2 96.1 %all-to-all-start.2 = ((f32[8,32,4096]{2,1,0:T(8,128)}), f32[8,32,4096]{2,1,0:T(8,128)}, u32[]{:S(2)}, u32[]{:S(2)}) async-start(f32[8,32,4096]{2,1,0:T(8,128)} %bitcast.19), calls=%async_computation.2 | async-start | bytes 8388608 | tf_op jit(solution)/shard_map/all_to_all | solution.py:362
  16.4 4.3 collective-permute-start.1
  18.3 5.1 %collective-permute-start = (f32[1,4096]{1,0:T(1,128)S(1)}, f32[1,4096]{1,0:T(1,128)S(1)}, u32[]{:S(2)}, u32[]{:S(2)}) collective-permute-start(f32[1,4096]{1,0:T(1,128)S(1)} %get-tuple-element.16), channel_id=1, source_target_pairs={{0,8},{8,16},{16,24},{1,9},{9,17},{17,25},{2,10},{10,18},{18,26},{... | collective-permute-start | bytes 49160 | tf_op jit(solution)/shard_map/ppermute | solution.py:335
  20.7 2.6 copy-start.7
  23.3 0.6 copy-start.8
  105.3 8.0 %copy-start.2 = (f32[32,32,32]{2,1,0:T(8,128)S(1)}, f32[32,32,32]{2,1,0:T(8,128)}, u32[]{:S(2)}) copy-start(f32[32,32,32]{2,1,0:T(8,128)} %param.15) | copy-start | bytes 393220
  105.3 8.2 %copy-start.3 = (f32[32,32,32]{2,1,0:T(8,128)S(1)}, f32[32,32,32]{2,1,0:T(8,128)}, u32[]{:S(2)}) copy-start(f32[32,32,32]{2,1,0:T(8,128)} %param.16) | copy-start | bytes 393220
  105.3 97.2 %all-to-all-start = ((f32[8,32,4096]{2,1,0:T(8,128)}), f32[8,32,4096]{2,1,0:T(8,128)}, u32[]{:S(2)}, u32[]{:S(2)}) async-start(f32[8,32,4096]{2,1,0:T(8,128)} %bitcast.18), calls=%async_computation | async-start | bytes 8388608 | tf_op jit(solution)/shard_map/all_to_all | solution.py:362
  113.2 2.6 slice-start
  113.2 2.7 slice-start.1
  114.6 14.7 %copy-start = (f32[1024,640]{1,0:T(8,128)S(1)}, f32[1024,640]{1,0:T(8,128)}, u32[]{:S(2)}) copy-start(f32[1024,640]{1,0:T(8,128)} %constant.141) | copy-start | bytes 7864324
  122.9 6.4 %copy-start.6 = (f32[31,1024]{1,0:T(8,128)S(1)}, f32[31,1024]{1,0:T(8,128)}, u32[]{:S(2)}) copy-start(f32[31,1024]{1,0:T(8,128)} %rev.6) | copy-start | bytes 380932
  125.9 5.0 %copy-start.1 = (f32[1024,640]{1,0:T(8,128)S(1)}, f32[1024,640]{1,0:T(8,128)}, u32[]{:S(2)}) copy-start(f32[1024,640]{1,0:T(8,128)} %constant.140) | copy-start | bytes 7864324
  202.5 97.1 %all-to-all-start.3 = ((f32[8,32,4096]{2,1,0:T(8,128)}), f32[8,32,4096]{2,1,0:T(8,128)}, u32[]{:S(2)}, u32[]{:S(2)}) async-start(f32[8,32,4096]{2,1,0:T(8,128)} %get-tuple-element.12), calls=%async_computation.3 | async-start | bytes 8388608 | tf_op jit(solution)/shard_map/all_to_all | solution.py:372
  299.6 8.2 %copy-start.11 = (s32[32,16]{0,1:T(8,128)S(1)}, s32[32,16]{0,1:T(8,128)}, u32[]{:S(2)}) copy-start(s32[32,16]{0,1:T(8,128)} %param.18) | copy-start | bytes 6148
  299.6 8.9 %copy-start.12 = (f32[32]{0:T(128)S(1)}, f32[32]{0:T(128)}, u32[]{:S(2)}) copy-start(f32[32]{0:T(128)} %param.17) | copy-start | bytes 388
  299.6 9.1 %copy-start.9 = (f32[32,128]{1,0:T(8,128)S(1)}, f32[32,128]{1,0:T(8,128)}, u32[]{:S(2)}) copy-start(f32[32,128]{1,0:T(8,128)} %get-tuple-element.10) | copy-start | bytes 49156
  299.6 9.4 %copy-start.10 = (f32[32,128]{1,0:T(8,128)S(1)}, f32[32,128]{1,0:T(8,128)}, u32[]{:S(2)}) copy-start(f32[32,128]{1,0:T(8,128)} %get-tuple-element.11) | copy-start | bytes 49156
  299.6 128.1 %all-to-all-start.1 = ((f32[8,32,4096]{2,1,0:T(8,128)}), f32[8,32,4096]{2,1,0:T(8,128)}, u32[]{:S(2)}, u32[]{:S(2)}) async-start(f32[8,32,4096]{2,1,0:T(8,128)} %get-tuple-element.9), calls=%async_computation.1 | async-start | bytes 8388608 | tf_op jit(solution)/shard_map/all_to_all | solution.py:372
  308.5 119.2 %copy-start.4 = (f32[256,32]{1,0:T(8,128)}, f32[256,32]{1,0:T(8,128)S(1)}, u32[]{:S(2)}) copy-start(f32[256,32]{1,0:T(8,128)S(1)} %convert_element_type.50.member) | copy-start | bytes 98308
  308.5 111.6 %copy-start.5 = (f32[256,32]{1,0:T(8,128)}, f32[256,32]{1,0:T(8,128)S(1)}, u32[]{:S(2)}) copy-start(f32[256,32]{1,0:T(8,128)S(1)} %convert_element_type.51.member) | copy-start | bytes 98308

commit v2 on v1

v2 whole, which is shorter than its diff:
```python
import functools
import math

import jax
import jax.numpy as jnp
import numpy as np
from jax import lax
from jax.experimental import pallas as pl
from jax.experimental.pallas import tpu as pltpu
from jax.sharding import PartitionSpec as P

courant = 0.9
top_speed = 3.0
collide_rate = 0.5
accommodation = 0.8
highest = lax.Precision.HIGHEST
sub = 8
lane = 128
vmem_bytes = 56 * 2**20


def split_table(table):
    high = table.astype(np.float32).astype(jnp.bfloat16)
    low = (table - high.astype(np.float64)).astype(np.float32).astype(jnp.bfloat16)
    return jnp.asarray(high), jnp.asarray(low)


def dft_tables(points):
    half = points // 2
    plane = points * points
    self_modes = [(0, 0), (0, half), (half, 0), (half, half)]
    reps = [(kb, kc) for kb in range(points) for kc in range(1, half)]
    reps += [(kb, 0) for kb in range(1, half)] + [(kb, half) for kb in range(1, half)]
    pairs = [(self_modes[0], self_modes[1]), (self_modes[2], self_modes[3])]
    slots = len(reps) + len(pairs)
    outer, inner = np.divmod(np.arange(plane), points)

    def angle(mode):
        return 2.0 * np.pi / points * ((outer * mode[0] + inner * mode[1]) % points)

    to_modes = np.zeros((plane, plane))
    from_modes = np.zeros((plane, plane))
    for slot, mode in enumerate(reps):
        theta = angle(mode)
        to_modes[:, slot] = np.cos(theta)
        to_modes[:, slots + slot] = -np.sin(theta)
        from_modes[slot] = 2.0 * np.cos(theta)
        from_modes[slots + slot] = -2.0 * np.sin(theta)
    for slot, (first, second) in enumerate(pairs, len(reps)):
        to_modes[:, slot] = from_modes[slot] = np.cos(angle(first))
        to_modes[:, slots + slot] = from_modes[slots + slot] = np.cos(angle(second))
    from_modes /= points * plane
    line = np.arange(points)
    theta = 2.0 * np.pi / points * (line[:, None] * line[None, :] % points)
    forward = np.block([[np.cos(theta), np.sin(theta)], [-np.sin(theta), np.cos(theta)]])
    forward = np.kron(forward, np.eye(sub))

    pick = np.zeros((2, plane, slots + lane), np.float32)

    def add(mode, column, weight):
        kb, kc = mode
        pick[0, kb * points + kc, column] += 0.5 * weight
        pick[1, -kb % points * points + -kc % points, column] += 0.5 * weight

    for slot, mode in enumerate(reps):
        add(mode, slot, 1.0)
    for slot, (first, second) in enumerate(pairs, len(reps)):
        add(first, slot, 0.5)
        add(second, slot, 0.5)
        add(first, slot + lane, 0.5)
        add(second, slot + lane, -0.5)
    return {
        "to_modes": split_table(to_modes),
        "from_modes": split_table(from_modes),
        "forward": split_table(forward),
        "backward": split_table(forward.T),
        "pick": jnp.asarray(pick.astype(jnp.bfloat16)),
    }


def split(values):
    high = values.astype(jnp.bfloat16)
    return high, (values - high.astype(jnp.float32)).astype(jnp.bfloat16)


def dot(a, b):
    return jnp.dot(a, b, preferred_element_type=jnp.float32)


def multiplier_kernel(gain, freq, pick, gain_out, freq_out):
    points = gain.shape[0]
    rows = jnp.concatenate([gain[...], freq[...]], axis=0)
    high, _ = split(rows)
    mid, low = split(rows - high.astype(jnp.float32))
    here, mirrored = (dot(low, pick[i]) + dot(mid, pick[i]) + dot(high, pick[i]) for i in range(2))
    for index, out in enumerate((gain_out, freq_out)):
        for a in range(points):
            at, turned = index * points + a, index * points + -a % points
            row = here[at : at + 1] + mirrored[turned : turned + 1]
            out[a * sub : (a + 1) * sub, :] = jnp.broadcast_to(row, (sub, row.shape[1]))


def multipliers(gain_spectrum, freq_spectrum, pick):
    points = gain_spectrum.shape[0]
    out = jax.ShapeDtypeStruct((points * sub, pick.shape[2]), jnp.float32)
    return pl.pallas_call(
        multiplier_kernel,
        in_specs=[local(pltpu.VMEM)] * 3,
        out_specs=[local(pltpu.VMEM)] * 2,
        out_shape=[out, out],
        compiler_params=pltpu.CompilerParams(vmem_limit_bytes=vmem_bytes),
        cost_estimate=pl.CostEstimate(flops=24 * points * pick.size, bytes_accessed=2 * pick.size, transcendentals=0),
    )(gain_spectrum.reshape(points, -1), freq_spectrum.reshape(points, -1), pick)


def partners(count):
    far = tuple(range(count // 2, count))
    return far, tuple(sorted(range(1, count // 2), key=lambda step: (-step.bit_length(), step)))


def swap(values, axis, step):
    return lax.ppermute(values, axis, [(i, i ^ step) for i in range(lax.axis_size(axis))])


def local(array):
    return pl.BlockSpec(memory_space=array)


def start_of(group, cells, low_groups, gap):
    return pl.multiple_of(group * cells + jnp.where(group < low_groups, 0, gap), sub)


def move_kernel(order, offset, low_groups, gap, points, has_halo, has_after, has_edges, me, particles, *rest):
    count = len(order)
    low, high = rest[:2] if has_halo else (None, None)
    outs = rest[2 * has_halo + has_after :][:count]
    edges = rest[2 * has_halo + has_after + count :][: 2 * has_edges]
    inside, made, rim, in_sems, out_sems = rest[-5:]
    cells, width = outs[0].shape
    total = particles.shape[0]
    planes = width // points**2
    span = inside.shape[1]
    at = me[0]

    def place(step):
        first = offset + start_of(at ^ step, cells, low_groups, gap)
        begin = pl.multiple_of(jnp.clip(first - sub, 0, total - span), sub)
        return first, begin

    def fetch(k, step):
        return pltpu.make_async_copy(particles.at[pl.ds(place(step)[1], span)], inside.at[k], in_sems.at[k])

    def store(k):
        return pltpu.make_async_copy(made.at[k], outs[k], out_sems.at[k])

    def edge_in(k):
        rows = pl.ds((total - sub) * k, sub)
        return pltpu.make_async_copy(particles.at[rows], rim.at[k], in_sems.at[count + k])

    def edge_out(k):
        return pltpu.make_async_copy(rim.at[k], edges[k], out_sems.at[count + k])

    for k, step in enumerate(order):
        fetch(k, step).start()
    for k in range(len(edges)):
        edge_in(k).start()
    for k, step in enumerate(order):
        fetch(k, step).wait()
        first, begin = place(step)
        skip = pl.multiple_of(first - begin, sub)
        ahead = pl.multiple_of(jnp.maximum(skip - sub, 0), sub)
        behind = pl.multiple_of(jnp.minimum(skip + cells, span - sub), sub)
        for plane in range(planes):
            columns = slice(plane * points**2, (plane + 1) * points**2)
            nu = courant * (2 * (at * planes + plane) + 1 - points).astype(jnp.float32) / points
            here = inside[k, pl.ds(skip, cells), columns]
            before = inside[k, pl.ds(ahead, sub), columns][sub - 1 :, :]
            after = inside[k, pl.ds(behind, sub), columns][:1, :]
            if has_halo:
                before = jnp.where(first == 0, low[sub - 1 :, columns], before)
                after = jnp.where(first + cells == total, high[:1, columns], after)
            row = lax.broadcasted_iota(jnp.int32, here.shape, 0)
            left = jnp.where(row == 0, before, pltpu.roll(here, 1, 0))
            right = jnp.where(row == cells - 1, after, pltpu.roll(here, cells - 1, 0))
            made[k, :, columns] = here - nu * jnp.where(nu > 0, here - left, right - here)
        store(k).start()
    for k in range(len(edges)):
        edge_in(k).wait()
        edge_out(k).start()
    for k in range(len(edges)):
        edge_out(k).wait()
    for k in range(count):
        store(k).wait()


def move(me, particles, order, cells, offset, low_groups, gap, points, halo=(), after=(), edges=False):
    total, width = particles.shape
    count = len(order)
    span = min(cells + 2 * sub, total)
    size = count * cells * width
    shape = jax.ShapeDtypeStruct((cells, width), jnp.float32)
    rim = jax.ShapeDtypeStruct((sub, width), jnp.float32)
    flags = (bool(halo), len(after), edges)
    return pl.pallas_call(
        functools.partial(move_kernel, order, offset, low_groups, gap, points, *flags),
        in_specs=[local(pltpu.SMEM), local(pltpu.HBM)]
        + [local(pltpu.VMEM)] * len(halo)
        + [local(pltpu.HBM)] * len(after),
        out_specs=[local(pltpu.HBM)] * (count + 2 * edges),
        out_shape=[shape] * count + [rim] * (2 * edges),
        scratch_shapes=[
            pltpu.VMEM((count, span, width), jnp.float32),
            pltpu.VMEM((count, cells, width), jnp.float32),
            pltpu.VMEM((2, sub, width), jnp.float32),
            pltpu.SemaphoreType.DMA((count + 2,)),
            pltpu.SemaphoreType.DMA((count + 2,)),
        ],
        compiler_params=pltpu.CompilerParams(vmem_limit_bytes=vmem_bytes),
        cost_estimate=pl.CostEstimate(flops=5 * size, bytes_accessed=10 * size, transcendentals=0),
    )(me, particles, *halo, *after)


def collide_kernel(steps, me, *rest):
    count = len(steps)
    xs, rest = rest[:count], rest[count:]
    to_high, to_low, from_high, from_low, ahead_high, ahead_low, back_high, back_low, gain, freq = rest[:10]
    outs, rest = rest[10 : 10 + count], rest[10 + count :]
    mass, wide_high, wide_low, mid, both_high, both_low, fields = rest
    cells, width = xs[0].shape
    plane = to_high.shape[0]
    slots = plane // 2
    planes = width // plane
    points = count * planes
    groups = cells // sub
    chunk = points * sub
    tile = min(256, plane)
    at = me[0]

    def pieces():
        for k, step in enumerate(steps):
            for group in range(groups):
                for j in range(planes):
                    start = (group * points + (at ^ step) * planes + j) * sub
                    here = (slice(group * sub, (group + 1) * sub), slice(j * plane, (j + 1) * plane))
                    yield k, group, here, pl.multiple_of(start, sub)

    for k, group, here, start in pieces():
        mid[pl.ds(start, sub), :] = xs[k][here]
    high, low = split(mid[...])
    wide_high[: groups * chunk, :] = high
    wide_low[: groups * chunk, :] = low

    @pl.loop(0, plane // tile)
    def _(at):
        columns = pl.ds(pl.multiple_of(at * tile, tile), tile)
        table = to_high[:, columns]
        mid[:, columns] = (
            dot(wide_low[: groups * chunk, :], table)
            + dot(wide_high[: groups * chunk, :], to_low[:, columns])
            + dot(wide_high[: groups * chunk, :], table)
        )

    @pl.loop(0, groups)
    def _(group):
        rows = pl.ds(pl.multiple_of(group * chunk, chunk), chunk)
        spectrum = jnp.concatenate([mid[rows, :slots], mid[rows, slots:]], axis=0)
        high, low = split(spectrum)
        waves = dot(ahead_high[...], low) + dot(ahead_low[...], high) + dot(ahead_high[...], high)
        real, imag = waves[:chunk], waves[chunk:]

        def mirror(values):
            tail = values[:, slots - lane :]
            turned = [tail[-a % points * sub : (-a % points + 1) * sub] for a in range(points)]
            return jnp.concatenate(turned, axis=0)

        real_tail, imag_tail = mirror(real), mirror(imag)
        for index, table in enumerate((gain, freq)):
            pad = jnp.zeros((chunk, slots - lane), jnp.float32)
            extra = table[:, slots:]
            upper = real * table[:, :slots] + jnp.concatenate([pad, real_tail * extra], axis=1)
            lower = imag * table[:, :slots] - jnp.concatenate([pad, imag_tail * extra], axis=1)
            for start, values in ((0, upper), (chunk, lower)):
                high, low = split(values)
                both_high[start : start + chunk, index * slots : (index + 1) * slots] = high
                both_low[start : start + chunk, index * slots : (index + 1) * slots] = low
        for index in range(2):
            columns = slice(index * slots, (index + 1) * slots)
            lines = (
                dot(back_high[...], both_low[:, columns])
                + dot(back_low[...], both_high[:, columns])
                + dot(back_high[...], both_high[:, columns])
            )
            high, low = split(jnp.concatenate([lines[:chunk], lines[chunk:]], axis=1))
            at = pl.ds(pl.multiple_of((index * groups + group) * chunk, chunk), chunk)
            wide_high[at, :] = high
            wide_low[at, :] = low

    @pl.loop(0, plane // tile)
    def _(at):
        columns = pl.ds(pl.multiple_of(at * tile, tile), tile)
        table = from_high[:, columns]
        fields[:, columns] = (
            dot(wide_low[...], table) + dot(wide_high[...], from_low[:, columns]) + dot(wide_high[...], table)
        )

    totals = [jnp.zeros((sub, plane), jnp.float32)] * groups
    for k, group, here, start in pieces():
        cube = xs[k][here]
        gained = fields[pl.ds(start, sub), :]
        lost = fields[pl.ds(pl.multiple_of(groups * chunk + start, sub), sub), :]
        post = cube + collide_rate * (gained - cube * lost)
        outs[k][here] = post
        totals[group] = totals[group] + post
    for group, total in enumerate(totals):
        lanes = total[:, :lane]
        for column in range(lane, plane, lane):
            lanes = lanes + total[:, column : column + lane]
        mass[group * sub : (group + 1) * sub, :] = lanes


def collide(me, cubes, steps, tables, gain, freq):
    cells, width = cubes[0].shape
    count = len(cubes)
    plane = tables["to_modes"][0].shape[0]
    points = count * width // plane
    step = math.gcd(cells, 2 * sub)
    chunk = step * points
    operands = [*tables["to_modes"], *tables["from_modes"], *tables["forward"], *tables["backward"], gain, freq]
    bf16, f32 = jnp.bfloat16, jnp.float32
    block = pl.BlockSpec((step, width), lambda i: (i, 0))
    multiply_adds = 3 * cells * points * (3 * plane * plane + 6 * points * sub * plane)
    *posts, mass = pl.pallas_call(
        functools.partial(collide_kernel, steps),
        grid=(cells // step,),
        in_specs=[local(pltpu.SMEM)] + [block] * count + [local(pltpu.VMEM)] * len(operands),
        out_specs=[block] * count + [pl.BlockSpec((step, lane), lambda i: (i, 0))],
        out_shape=[jax.ShapeDtypeStruct((cells, width), f32)] * count + [jax.ShapeDtypeStruct((cells, lane), f32)],
        scratch_shapes=[
            pltpu.VMEM((2 * chunk, plane), bf16),
            pltpu.VMEM((2 * chunk, plane), bf16),
            pltpu.VMEM((chunk, plane), f32),
            pltpu.VMEM((2 * points * sub, plane), bf16),
            pltpu.VMEM((2 * points * sub, plane), bf16),
            pltpu.VMEM((2 * chunk, plane), f32),
        ],
        compiler_params=pltpu.CompilerParams(vmem_limit_bytes=vmem_bytes),
        cost_estimate=pl.CostEstimate(
            flops=3 * multiply_adds, bytes_accessed=8 * count * cells * width, transcendentals=0
        ),
    )(me, *cubes, *operands)
    return posts, mass


def mass_kernel(count, *refs):
    parts, out = refs[:count], refs[-1]
    total = jnp.zeros(out.shape, jnp.float32)
    for mass, member in zip(parts[::2], parts[1::2]):
        cell = jnp.sum(mass[...], axis=1, keepdims=True)
        total = total + jnp.sum(member[...] * cell, axis=0, keepdims=True)
    out[...] = total


def panel_mass(pairs, after):
    flat = [array for pair in pairs for array in pair]
    return pl.pallas_call(
        functools.partial(mass_kernel, len(flat)),
        in_specs=[local(pltpu.VMEM)] * len(flat) + [local(pl.ANY)] * len(after),
        out_specs=local(pltpu.VMEM),
        out_shape=jax.ShapeDtypeStruct((1, flat[1].shape[1]), jnp.float32),
    )(*flat, *after)


def settle_kernel(steps, offset, low_groups, gap, me, member, emit, *rest):
    count = len(steps)
    posts = rest[:count]
    out, held, emission, in_sems, out_sems = rest[-5:]
    cells, width = held.shape[1:]
    at = me[0]

    def fetch(k):
        return pltpu.make_async_copy(posts[k], held.at[k], in_sems.at[k])

    def store(k):
        first = offset + start_of(at ^ steps[k], cells, low_groups, gap)
        return pltpu.make_async_copy(held.at[k], out.at[pl.ds(first, cells)], out_sems.at[k])

    for k in range(count):
        fetch(k).start()
    chosen = member[...]
    share = accommodation * jnp.sum(chosen, axis=1, keepdims=True)
    emission[...] = dot(jnp.concatenate([chosen, chosen], axis=1).astype(jnp.bfloat16), emit[...])
    for k in range(count):
        fetch(k).wait()
        rows = pl.ds(pl.multiple_of(k * cells, sub), cells)
        post = held[k]
        held[k] = post + (accommodation * emission[rows, :] - share[k * cells : (k + 1) * cells] * post)
        store(k).start()
    for k in range(count):
        store(k).wait()


def settle(me, posts, steps, member, emit, earlier, shape, offset, low_groups, gap):
    cells, width = posts[0].shape
    count = len(posts)
    size = count * cells * width
    operands = [me, member, emit, *posts]
    in_specs = [local(pltpu.SMEM), local(pltpu.VMEM), local(pltpu.VMEM)] + [local(pl.ANY)] * count
    aliases = {}
    if earlier is not None:
        aliases = {len(operands): 0}
        operands.append(earlier)
        in_specs.append(local(pltpu.HBM))
    return pl.pallas_call(
        functools.partial(settle_kernel, steps, offset, low_groups, gap),
        in_specs=in_specs,
        out_specs=local(pltpu.HBM),
        out_shape=jax.ShapeDtypeStruct(shape, jnp.float32),
        scratch_shapes=[
            pltpu.VMEM((count, cells, width), jnp.float32),
            pltpu.VMEM((count * cells, width), jnp.float32),
            pltpu.SemaphoreType.DMA((count,)),
            pltpu.SemaphoreType.DMA((count,)),
        ],
        input_output_aliases=aliases,
        compiler_params=pltpu.CompilerParams(vmem_limit_bytes=vmem_bytes),
        cost_estimate=pl.CostEstimate(
            flops=4 * member.shape[1] * size, bytes_accessed=8 * size, transcendentals=0
        ),
    )(*operands)


def on_device(particles, gain_spectrum, freq_spectrum, panel_temp, wall_cells):
    cell_dev, vel_dev = particles.shape
    points = gain_spectrum.shape[0]
    plane_size = points * points
    planes = vel_dev // plane_size
    vel_count = lax.axis_size("vel")
    vel_at = lax.axis_index("vel")
    space_at = lax.axis_index("space")
    space_count = lax.axis_size("space")
    me = vel_at.astype(jnp.int32)[None]
    tables = dft_tables(points)
    panels, per_panel = wall_cells.shape

    quarter, half = cell_dev // 4, cell_dev // 2
    cells = half // vel_count
    inner, outer = (quarter, vel_count, 0), (0, vel_count // 2, half)
    far, near = partners(vel_count)
    steps = (*far, *near, 0)
    urgent, ready = far[:2], (*far[:2], *near[:1], *far[2:3])

    def send(arrays):
        return {step: swap(array, "vel", step) if step else array for step, array in arrays.items()}

    def rest(done):
        return tuple(step for step in steps if step not in done)

    early = move(me, particles, urgent, cells, *inner, points)
    *late, first_rows, last_rows = move(
        me, particles, rest(urgent), cells, *inner, points, after=early[:1], edges=True
    )
    inner_cubes = send(dict(zip((*urgent, *rest(urgent)), (*early, *late))))
    space_pairs = [(i, i + 1) for i in range(space_count - 1)]
    low = lax.ppermute(last_rows, "space", space_pairs)
    high = lax.ppermute(first_rows, "space", [(target, source) for source, target in space_pairs])
    outer_early = move(me, particles, ready, cells, *outer, points, halo=(low, high))
    gain, freq = multipliers(gain_spectrum, freq_spectrum, tables["pick"])

    def collided(cubes):
        posts, mass = collide(me, [cubes[step] for step in steps], steps, tables, gain, freq)
        return dict(zip(steps, posts)), mass

    inner_posts, inner_mass = collided(inner_cubes)
    outer_late = move(
        me, particles, rest(ready), cells, *outer, points, halo=(low, high), after=(inner_mass,)
    )
    outer_cubes = send(dict(zip((*ready, *rest(ready)), (*outer_early, *outer_late))))
    outer_posts, outer_mass = collided(outer_cubes)

    def cells_of(plan, group):
        offset, low_groups, gap = plan
        first = offset + group * cells + jnp.where(group < low_groups, 0, gap)
        return space_at * cell_dev + first + jnp.arange(cells, dtype=jnp.int32)

    def membership(cell_ids):
        hit = wall_cells.reshape(1, panels, per_panel) == cell_ids[:, None, None]
        return jnp.any(hit, axis=2).astype(jnp.float32)

    held = near
    *tied, outer_mass = lax.optimization_barrier((*(inner_posts[step] for step in held), outer_mass))
    inner_back = send({**inner_posts, **dict(zip(held, tied))})
    outer_back = send(outer_posts)
    pairs = [
        (mass, membership(cells_of(plan, vel_at))) for mass, plan in ((inner_mass, inner), (outer_mass, outer))
    ]
    wall_mass = lax.psum(panel_mass(pairs, [inner_back[step] for step in (*far, *near)]), "space")
    step = 1
    while step < vel_count:
        wall_mass = wall_mass + swap(wall_mass, "vel", step)
        step *= 2

    def speed(index):
        return top_speed * (2 * index + 1 - points).astype(jnp.float32) / points

    line = jnp.arange(points, dtype=jnp.int32)
    line_weight = jnp.exp(-(speed(line) ** 2)[None, :] / (2.0 * panel_temp[:, None]))
    normal_sum = jnp.sum(line_weight, axis=1) ** 3
    columns = jnp.arange(vel_dev, dtype=jnp.int32)
    plane_index = vel_at * planes + columns // plane_size
    speed_sq = speed(plane_index) ** 2 + speed(columns // points % points) ** 2 + speed(columns % points) ** 2
    profile = jnp.exp(-speed_sq[None, :] / (2.0 * panel_temp[:, None]))
    maxwellian = profile / normal_sum[:, None]
    emission = (wall_mass.reshape(panels, 1) / per_panel) * maxwellian
    emit_high = lax.reduce_precision(emission, exponent_bits=8, mantissa_bits=7)
    emit = jnp.concatenate([emit_high, emission - emit_high], axis=0).astype(jnp.bfloat16)

    def wall(posts, part, plan, earlier):
        ids = jnp.concatenate([cells_of(plan, vel_at ^ step) for step in part])
        posts = [posts[step] for step in part]
        return settle(me, posts, part, membership(ids), emit, earlier, particles.shape, *plan)

    last = far[-2:]
    out = wall(inner_back, steps, inner, None)
    out = wall(outer_back, rest(last), outer, out)
    return wall(outer_back, last, outer, out)


def solution(mesh):
    in_specs = (P("space", "vel"), P(), P(), P(), P())
    out_specs = P("space", "vel")
    return jax.shard_map(on_device, mesh=mesh, in_specs=in_specs, out_specs=out_specs, check_vma=False)
```

time: 440 us -> 392 us (0.89); the launches traced: 435 us -> 392 us
  blocking collectives: 110 us -> 6.17 us
  waiting for transfers between devices: 149 us -> 205 us
  starting transfers between devices: 34.3 us -> 51.2 us
  matrix products: 8.09 us -> 0 us
  local copies, waits for them, and re-layouts: 16.5 us -> 9.12 us
    ppermute x2 -> x33, waiting for transfers between devices: 2.63 us -> 205 us  [the longest x31 205 us: swap(): lax.ppermute(values, axis, [(i, i ^ step) for i in range(lax.axis_size(ax...]
    all_to_all x4 -> x0, waiting for transfers between devices: 147 us -> none  [the longest x2 99.1 us: on_device(): arrived.append(lax.all_to_all(moved, 'vel', 0, 0, tiled=True))]
    psum x1, blocking collectives: 110 us -> 6.17 us  [on_device(): lax.psum(panel_mass(pairs, [inner_back[step] for step in (*far, *near)]),...]
    ppermute x2 -> x33, starting transfers between devices: 4.32 us -> 51.2 us  [the longest x31 45.7 us: swap(): lax.ppermute(values, axis, [(i, i ^ step) for i in range(lax.axis_size(ax...]
    all_to_all x4 -> x0, starting transfers between devices: 30 us -> none  [the longest x2 15.9 us: on_device(): returned.append(lax.all_to_all(post, 'vel', 0, 0, tiled=True))]
    dot_general x4 -> x0, matrix products: 8.09 us -> none  [multipliers(): return jnp.repeat(jnp.dot(both, pick, precision=highest), sub, axis=0)]
    rev x2 -> x0, local copies, waits for them, and re-layouts: 7.09 us -> none  [multipliers(): mirrored = jnp.concatenate([rows[:1], lax.rev(rows[1:], (0,))], axis=0)]
    slice x11 -> x0, local copies, waits for them, and re-layouts: 6.06 us -> none  [the longest x10 5.07 us: multipliers(): mirrored = jnp.concatenate([rows[:1], lax.rev(rows[1:], (0,))], axis=0)]
  transfers between devices with their start and end apart: 6 -> 33, of which waited for: 4 -> 15; matrix products, arithmetic and copies ran while one was open for 6% -> 2% of each run, Pallas kernels for 23% -> 28%
where the time goes in v2:
time: 392 us
  waiting for transfers between devices  205 us (52%)
  Pallas kernels  116 us (30%)
  starting transfers between devices  51.2 us (13%)
  local copies, waits for them, and re-layouts  9.12 us (2%)
  blocking collectives  6.17 us (2%)
    ppermute x31, waiting for transfers between devices, swap(): lax.ppermute(values, axis, [(i, i ^ step) for i in range(lax.axis_size(ax...  205 us
    pallas_call x2, Pallas kernels, collide(): pl.pallas_call(functools.partial(collide_kernel, steps), grid=(cells // s...  84.3 us
    ppermute x31, starting transfers between devices, swap(): lax.ppermute(values, axis, [(i, i ^ step) for i in range(lax.axis_size(ax...  45.7 us
    pallas_call x4, Pallas kernels, move(): pl.pallas_call(functools.partial(move_kernel, order, offset, low_groups,...  14.2 us
    pallas_call x3, Pallas kernels, settle(): pl.pallas_call(functools.partial(settle_kernel, steps, offset, low_groups...  11.8 us
  transfers between devices with their start and end apart: 33, of which 15 were waited for; matrix products, arithmetic and copies ran while one was open for 2% of the time, Pallas kernels for 28%

profile of v2, /device:TPU:18, one launch (start us, length us, event | category | flops | bytes accessed | tf_op | source)
XLA Modules:
  0.0 392.0 jit_solution(8866461952487853634)
XLA Ops:
  2.9 3.8 shard_map.137
  23.2 39.3 %collective-permute-done.2.rest_2_ = f32[32,4096]{1,0:T(8,128)S(1)} collective-permute-done((f32[32,4096]{1,0:T(8,128)}, f32[32,4096]{1,0:T(8,128)S(1)}, u32[]{:S(2)}, u32[]{:S(2)}) %collective-permute-start.2) | collective-permute-done | bytes 524320 | tf_op jit(solution)/shard_map/ppermute | solution.py:122
  63.9 10.7 %collective-permute-done.3.rest_3_ = f32[32,4096]{1,0:T(8,128)S(1)} collective-permute-done((f32[32,4096]{1,0:T(8,128)}, f32[32,4096]{1,0:T(8,128)S(1)}, u32[]{:S(2)}, u32[]{:S(2)}) %collective-permute-start.3) | collective-permute-done | bytes 524320 | tf_op jit(solution)/shard_map/ppermute | solution.py:122
  75.7 4.5 %shard_map.138 = (f32[256,640]{1,0:T(8,128)}, f32[256,640]{1,0:T(8,128)}) custom-call(f32[32,1024]{1,0:T(8,128)} %reshape.108.gain, f32[32,1024]{1,0:T(8,128)} %reshape.109.freq, bf16[2,1024,640]{2,1,0:T(8,128)(2,1)} %constant.140.clone.pick), custom_call_target="tpu_custom_call" | custom-call | flops 1006632960 | bytes 2621440 | tf_op jit(solution)/shard_map/pallas_call | solution.py:106
  80.2 3.9 shard_map.140
  84.2 3.9 collective-permute-start.10
  88.6 19.7 %collective-permute-done.6.rest_6_ = f32[32,4096]{1,0:T(8,128)} collective-permute-done((f32[32,4096]{1,0:T(8,128)}, f32[32,4096]{1,0:T(8,128)}, u32[]{:S(2)}, u32[]{:S(2)}) %collective-permute-start.6) | collective-permute-done | bytes 524320 | tf_op jit(solution)/shard_map/ppermute | solution.py:122
  110.4 9.9 %collective-permute-done.1.rest_1_ = f32[32,4096]{1,0:T(8,128)} collective-permute-done((f32[32,4096]{1,0:T(8,128)S(1)}, f32[32,4096]{1,0:T(8,128)}, u32[]{:S(2)}, u32[]{:S(2)}) %collective-permute-start.1) | collective-permute-done | bytes 524320 | tf_op jit(solution)/shard_map/ppermute | solution.py:122
  120.3 42.0 %shard_map.139 = (f32[32,4096]{1,0:T(8,128)}, f32[32,4096]{1,0:T(8,128)}, f32[32,4096]{1,0:T(8,128)}, f32[32,4096]{1,0:T(8,128)}, f32[32,4096]{1,0:T(8,128)}, /*...) custom-call(s32[1]{0:T(128)} %bitcast.me, f32[32,4096]{1,0:T(8,128)} %copy-done.16, ...), custom_call_target="tpu_custom_call" | custom-call | flops 43486543872 | bytes 8388608 | tf_op jit(solution)/shard_map/pallas_call | solution.py:332
  162.4 4.1 %shard_map.141 = (f32[32,4096]{1,0:T(8,128)}, f32[32,4096]{1,0:T(8,128)}, f32[32,4096]{1,0:T(8,128)}, f32[32,4096]{1,0:T(8,128)}) custom-call(s32[1]{0:T(128)} %bitcast.me, f32[512,4096]{1,0:T(8,128)} %particles.7, f32[8,4096]{1,0:T(8,128)} %copy-done.6, f32[8,4096]{1,0:T(8,128)} %copy-done.7, f32[32,128]{1,0:T(8,128)} %get-tuple-element.57.rest_2_.refs_0_), custom_call_target="tpu_custom_call" | custom-call | flops 2621440 | bytes 5242880 | tf_op jit(solution)/shard_map/pallas_call | solution.py:204
  167.5 5.4 %collective-permute-start.14 = (f32[32,4096]{1,0:T(8,128)}, f32[32,4096]{1,0:T(8,128)S(1)}, u32[]{:S(2)}, u32[]{:S(2)}) collective-permute-start(f32[32,4096]{1,0:T(8,128)} %get-tuple-element.68), channel_id=1, source_target_pairs={{0,3},{1,2},{2,1},{3,0},{4,7},{5,6},{6,5},{7,4},{8,11},{9,10},{10,... | collective-permute-start | bytes 1572872 | tf_op jit(solution)/shard_map/ppermute | solution.py:122
  177.7 64.5 %collective-permute-done.12.rest_3_ = f32[32,4096]{1,0:T(8,128)S(1)} collective-permute-done((f32[32,4096]{1,0:T(8,128)}, f32[32,4096]{1,0:T(8,128)S(1)}, u32[]{:S(2)}, u32[]{:S(2)}) %collective-permute-start.12) | collective-permute-done | bytes 524320 | tf_op jit(solution)/shard_map/ppermute | solution.py:122
  244.7 42.3 %shard_map.142 = (f32[32,4096]{1,0:T(8,128)}, f32[32,4096]{1,0:T(8,128)}, f32[32,4096]{1,0:T(8,128)}, f32[32,4096]{1,0:T(8,128)}, f32[32,4096]{1,0:T(8,128)}, /*...) custom-call(s32[1]{0:T(128)} %bitcast.me, f32[32,4096]{1,0:T(8,128)} %copy-done.31, ...), custom_call_target="tpu_custom_call" | custom-call | flops 43486543872 | bytes 8388608 | tf_op jit(solution)/shard_map/pallas_call | solution.py:332
  287.1 4.3 %collective-permute-start.21 = (f32[32,4096]{1,0:T(8,128)S(1)}, f32[32,4096]{1,0:T(8,128)S(1)}, u32[]{:S(2)}, u32[]{:S(2)}) collective-permute-start(f32[32,4096]{1,0:T(8,128)S(1)} %copy-done.21), channel_id=1, source_target_pairs={{0,3},{1,2},{2,1},{3,0},{4,7},{5,6},{6,5},{7,4},{8,11},{9,10},{10,... | collective-permute-start | bytes 1572872 | tf_op jit(solution)/shard_map/ppermute | solution.py:122
  296.2 4.8 %collective-permute-done.20.refs_8_.rest_4_ = f32[32,4096]{1,0:T(8,128)S(1)} collective-permute-done((f32[32,4096]{1,0:T(8,128)S(1)}, f32[32,4096]{1,0:T(8,128)S(1)}, u32[]{:S(2)}, u32[]{:S(2)}) %collective-permute-start.20) | collective-permute-done | bytes 524320 | tf_op jit(solution)/shard_map/ppermute | solution.py:122
  300.9 11.9 %collective-permute-done.21.refs_9_.rest_5_ = f32[32,4096]{1,0:T(8,128)S(1)} collective-permute-done((f32[32,4096]{1,0:T(8,128)S(1)}, f32[32,4096]{1,0:T(8,128)S(1)}, u32[]{:S(2)}, u32[]{:S(2)}) %collective-permute-start.21) | collective-permute-done | bytes 524320 | tf_op jit(solution)/shard_map/ppermute | solution.py:122
  315.0 6.2 %psum.7 = f32[1,32]{1,0:T(1,128)S(1)} all-reduce(f32[1,32]{1,0:T(1,128)} %shard_map.143), channel_id=1, replica_groups=mesh['space'=4,'vel'=8] {'space'}, use_global_device_ids=true, to_apply=%region_3.4 | all-reduce | flops 32 | bytes 256 | tf_op jit(solution)/shard_map/psum | solution.py:496
  328.7 4.4 %collective-permute-start.25 = (f32[1,32]{1,0:T(1,128)S(1)}, f32[1,32]{1,0:T(1,128)S(1)}, u32[]{:S(2)}, u32[]{:S(2)}) collective-permute-start(f32[1,32]{1,0:T(1,128)S(1)} %add.334), channel_id=1, source_target_pairs={{0,4},{1,5},{2,6},{3,7},{4,0},{5,1},{6,2},{7,3},{8,12},{9,13},{10,... | collective-permute-start | bytes 392 | tf_op jit(solution)/shard_map/ppermute | solution.py:122
  333.1 11.4 %collective-permute-done.25 = f32[1,32]{1,0:T(1,128)S(1)} collective-permute-done((f32[1,32]{1,0:T(1,128)S(1)}, f32[1,32]{1,0:T(1,128)S(1)}, u32[]{:S(2)}, u32[]{:S(2)}) %collective-permute-start.25) | collective-permute-done | bytes 160 | tf_op jit(solution)/shard_map/ppermute | solution.py:122
  349.1 4.6 %shard_map.144.rest_6_ = f32[512,4096]{1,0:T(8,128)} custom-call(s32[1]{0:T(128)} %bitcast.me, f32[256,32]{1,0:T(8,128)} %copy.30.member, bf16[64,4096]{1,0:T(8,128)(2,1)} %pad_maximum_fusion.emit, f32[32,4096]{1,0:T(8,128)} %copy-done, f32[32,4096]{1,0:T(8,128)} %copy-done.1, f32[32,4096]{1,0:T(8,128)} %copy-done.2, f32[32,4096]{1,0:T(8,128)} %copy-done.3, ...), custom_call_target="tpu_custom_call" | custom-call | flops 134217728 | bytes 8388608 | tf_op jit(solution)/shard_map/pallas_call | solution.py:413
  355.4 10.7 %collective-permute-done.32.rest_4_ = f32[32,4096]{1,0:T(8,128)S(1)} collective-permute-done((f32[32,4096]{1,0:T(8,128)}, f32[32,4096]{1,0:T(8,128)S(1)}, u32[]{:S(2)}, u32[]{:S(2)}) %collective-permute-start.32) | collective-permute-done | bytes 524320 | tf_op jit(solution)/shard_map/ppermute | solution.py:122
  366.9 4.0 %shard_map.145.rest_2_ = f32[512,4096]{1,0:T(8,128)} custom-call(s32[1]{0:T(128)} %bitcast.me, f32[192,32]{1,0:T(8,128)} %copy.31.member, bf16[64,4096]{1,0:T(8,128)(2,1)} %pad_maximum_fusion.emit, f32[32,4096]{1,0:T(8,128)} %collective-permute-done.28.rest_0_, f32[32,4096]{1,0:T(8,128)} %collective-permute-done.29.rest_1_, ...), custom_call_target="tpu_custom_call", output_to_operand_aliasing={{}: (9, {})} | custom-call | flops 100663296 | bytes 6291456 | tf_op jit(solution)/shard_map/pallas_call | solution.py:413
  370.9 10.8 %collective-permute-done.26.rest_0_ = f32[32,4096]{1,0:T(8,128)S(1)} collective-permute-done((f32[32,4096]{1,0:T(8,128)}, f32[32,4096]{1,0:T(8,128)S(1)}, u32[]{:S(2)}, u32[]{:S(2)}) %collective-permute-start.26) | collective-permute-done | bytes 524320 | tf_op jit(solution)/shard_map/ppermute | solution.py:122
  381.7 6.1 %collective-permute-done.27.rest_1_ = f32[32,4096]{1,0:T(8,128)S(1)} collective-permute-done((f32[32,4096]{1,0:T(8,128)}, f32[32,4096]{1,0:T(8,128)S(1)}, u32[]{:S(2)}, u32[]{:S(2)}) %collective-permute-start.27) | collective-permute-done | bytes 524320 | tf_op jit(solution)/shard_map/ppermute | solution.py:122
  (163 shorter events, 58.3 us)
Async XLA Ops:
  2.5 105.9 %collective-permute-start = (f32[32,4096]{1,0:T(8,128)}, f32[32,4096]{1,0:T(8,128)S(1)}, u32[]{:S(2)}, u32[]{:S(2)}) collective-permute-start(f32[32,4096]{1,0:T(8,128)} %get-tuple-element.47.rest_0_), channel_id=1, source_target_pairs={{0,4},{1,5},{2,6},{3,7},{4,0},{5,1},{6,2},{7,3},{8,12},{9,13},{10,... | collective-permute-start | bytes 1572872 | tf_op jit(solution)/shard_map/ppermute | solution.py:122
  6.7 55.8 %collective-permute-start.2 = (f32[32,4096]{1,0:T(8,128)}, f32[32,4096]{1,0:T(8,128)S(1)}, u32[]{:S(2)}, u32[]{:S(2)}) collective-permute-start(f32[32,4096]{1,0:T(8,128)} %get-tuple-element.49), channel_id=1, source_target_pairs={{0,6},{1,7},{2,4},{3,5},{4,2},{5,3},{6,0},{7,1},{8,14},{9,15},{10,... | collective-permute-start | bytes 1572872 | tf_op jit(solution)/shard_map/ppermute | solution.py:122
  9.4 65.2 %collective-permute-start.3 = (f32[32,4096]{1,0:T(8,128)}, f32[32,4096]{1,0:T(8,128)S(1)}, u32[]{:S(2)}, u32[]{:S(2)}) collective-permute-start(f32[32,4096]{1,0:T(8,128)} %get-tuple-element.50), channel_id=1, source_target_pairs={{0,7},{1,6},{2,5},{3,4},{4,3},{5,2},{6,1},{7,0},{8,15},{9,14},{10,... | collective-permute-start | bytes 1572872 | tf_op jit(solution)/shard_map/ppermute | solution.py:122
  20.5 63.7 %collective-permute-start.4 = (f32[32,4096]{1,0:T(8,128)}, f32[32,4096]{1,0:T(8,128)S(1)}, u32[]{:S(2)}, u32[]{:S(2)}) collective-permute-start(f32[32,4096]{1,0:T(8,128)} %get-tuple-element.51), channel_id=1, source_target_pairs={{0,2},{1,3},{2,0},{3,1},{4,6},{5,7},{6,4},{7,5},{8,10},{9,11},{10,... | collective-permute-start | bytes 1572872 | tf_op jit(solution)/shard_map/ppermute | solution.py:122
  23.1 64.9 %collective-permute-start.5 = (f32[32,4096]{1,0:T(8,128)}, f32[32,4096]{1,0:T(8,128)}, u32[]{:S(2)}, u32[]{:S(2)}) collective-permute-start(f32[32,4096]{1,0:T(8,128)} %get-tuple-element.52), channel_id=1, source_target_pairs={{0,3},{1,2},{2,1},{3,0},{4,7},{5,6},{6,5},{7,4},{8,11},{9,10},{10,... | collective-permute-start | bytes 1572872 | tf_op jit(solution)/shard_map/ppermute | solution.py:122
  62.4 45.9 %collective-permute-start.6 = (f32[32,4096]{1,0:T(8,128)}, f32[32,4096]{1,0:T(8,128)}, u32[]{:S(2)}, u32[]{:S(2)}) collective-permute-start(f32[32,4096]{1,0:T(8,128)} %get-tuple-element.53), channel_id=1, source_target_pairs={{0,1},{1,0},{2,3},{3,2},{4,5},{5,4},{6,7},{7,6},{8,9},{9,8},{10,11... | collective-permute-start | bytes 1572872 | tf_op jit(solution)/shard_map/ppermute | solution.py:122
  74.6 45.7 %collective-permute-start.1 = (f32[32,4096]{1,0:T(8,128)S(1)}, f32[32,4096]{1,0:T(8,128)}, u32[]{:S(2)}, u32[]{:S(2)}) collective-permute-start(f32[32,4096]{1,0:T(8,128)S(1)} %copy-done.18), channel_id=1, source_target_pairs={{0,5},{1,4},{2,7},{3,6},{4,1},{5,0},{6,3},{7,2},{8,13},{9,12},{10,... | collective-permute-start | bytes 1572872 | tf_op jit(solution)/shard_map/ppermute | solution.py:122
  84.2 83.4 %collective-permute-start.10 = (f32[32,4096]{1,0:T(8,128)}, f32[32,4096]{1,0:T(8,128)S(1)}, u32[]{:S(2)}, u32[]{:S(2)}) collective-permute-start(f32[32,4096]{1,0:T(8,128)} %get-tuple-element.64), channel_id=1, source_target_pairs={{0,5},{1,4},{2,7},{3,6},{4,1},{5,0},{6,3},{7,2},{8,13},{9,12},{10,... | collective-permute-start | bytes 1572872 | tf_op jit(solution)/shard_map/ppermute | solution.py:122
  88.0 84.9 %collective-permute-start.11 = (f32[32,4096]{1,0:T(8,128)}, f32[32,4096]{1,0:T(8,128)S(1)}, u32[]{:S(2)}, u32[]{:S(2)}) collective-permute-start(f32[32,4096]{1,0:T(8,128)} %get-tuple-element.65), channel_id=1, source_target_pairs={{0,6},{1,7},{2,4},{3,5},{4,2},{5,3},{6,0},{7,1},{8,14},{9,15},{10,... | collective-permute-start | bytes 1572872 | tf_op jit(solution)/shard_map/ppermute | solution.py:122
  108.3 65.8 %collective-permute-start.13 = (f32[32,4096]{1,0:T(8,128)}, f32[32,4096]{1,0:T(8,128)S(1)}, u32[]{:S(2)}, u32[]{:S(2)}) collective-permute-start(f32[32,4096]{1,0:T(8,128)} %get-tuple-element.67), channel_id=1, source_target_pairs={{0,2},{1,3},{2,0},{3,1},{4,6},{5,7},{6,4},{7,5},{8,10},{9,11},{10,... | collective-permute-start | bytes 1572872 | tf_op jit(solution)/shard_map/ppermute | solution.py:122
  108.3 65.9 %collective-permute-start.9 = (f32[32,4096]{1,0:T(8,128)}, f32[32,4096]{1,0:T(8,128)S(1)}, u32[]{:S(2)}, u32[]{:S(2)}) collective-permute-start(f32[32,4096]{1,0:T(8,128)} %get-tuple-element.63), channel_id=1, source_target_pairs={{0,4},{1,5},{2,6},{3,7},{4,0},{5,1},{6,2},{7,3},{8,12},{9,13},{10,... | collective-permute-start | bytes 1572872 | tf_op jit(solution)/shard_map/ppermute | solution.py:122
  166.5 75.7 %collective-permute-start.12 = (f32[32,4096]{1,0:T(8,128)}, f32[32,4096]{1,0:T(8,128)S(1)}, u32[]{:S(2)}, u32[]{:S(2)}) collective-permute-start(f32[32,4096]{1,0:T(8,128)} %get-tuple-element.66), channel_id=1, source_target_pairs={{0,7},{1,6},{2,5},{3,4},{4,3},{5,2},{6,1},{7,0},{8,15},{9,14},{10,... | collective-permute-start | bytes 1572872 | tf_op jit(solution)/shard_map/ppermute | solution.py:122
  167.5 75.5 %collective-permute-start.14 = (f32[32,4096]{1,0:T(8,128)}, f32[32,4096]{1,0:T(8,128)S(1)}, u32[]{:S(2)}, u32[]{:S(2)}) collective-permute-start(f32[32,4096]{1,0:T(8,128)} %get-tuple-element.68), channel_id=1, source_target_pairs={{0,3},{1,2},{2,1},{3,0},{4,7},{5,6},{6,5},{7,4},{8,11},{9,10},{10,... | collective-permute-start | bytes 1572872 | tf_op jit(solution)/shard_map/ppermute | solution.py:122
  172.9 70.2 %collective-permute-start.15 = (f32[32,4096]{1,0:T(8,128)}, f32[32,4096]{1,0:T(8,128)S(1)}, u32[]{:S(2)}, u32[]{:S(2)}) collective-permute-start(f32[32,4096]{1,0:T(8,128)} %get-tuple-element.69), channel_id=1, source_target_pairs={{0,1},{1,0},{2,3},{3,2},{4,5},{5,4},{6,7},{7,6},{8,9},{9,8},{10,11... | collective-permute-start | bytes 1572872 | tf_op jit(solution)/shard_map/ppermute | solution.py:122
  174.2 112.9 %collective-permute-start.16 = (f32[32,4096]{1,0:T(8,128)S(1)}, f32[32,4096]{1,0:T(8,128)S(1)}, u32[]{:S(2)}, u32[]{:S(2)}) collective-permute-start(f32[32,4096]{1,0:T(8,128)S(1)} %copy-done.30), channel_id=1, source_target_pairs={{0,4},{1,5},{2,6},{3,7},{4,0},{5,1},{6,2},{7,3},{8,12},{9,13},{10,... | collective-permute-start | bytes 1572872 | tf_op jit(solution)/shard_map/ppermute | solution.py:122
  174.3 117.1 %collective-permute-start.17 = (f32[32,4096]{1,0:T(8,128)S(1)}, f32[32,4096]{1,0:T(8,128)S(1)}, u32[]{:S(2)}, u32[]{:S(2)}) collective-permute-start(f32[32,4096]{1,0:T(8,128)S(1)} %copy-done.28), channel_id=1, source_target_pairs={{0,5},{1,4},{2,7},{3,6},{4,1},{5,0},{6,3},{7,2},{8,13},{9,12},{10,... | collective-permute-start | bytes 1572872 | tf_op jit(solution)/shard_map/ppermute | solution.py:122
  243.0 48.6 %collective-permute-start.18 = (f32[32,4096]{1,0:T(8,128)S(1)}, f32[32,4096]{1,0:T(8,128)S(1)}, u32[]{:S(2)}, u32[]{:S(2)}) collective-permute-start(f32[32,4096]{1,0:T(8,128)S(1)} %copy-done.24), channel_id=1, source_target_pairs={{0,6},{1,7},{2,4},{3,5},{4,2},{5,3},{6,0},{7,1},{8,14},{9,15},{10,... | collective-permute-start | bytes 1572872 | tf_op jit(solution)/shard_map/ppermute | solution.py:122
  243.1 49.7 %collective-permute-start.19 = (f32[32,4096]{1,0:T(8,128)S(1)}, f32[32,4096]{1,0:T(8,128)S(1)}, u32[]{:S(2)}, u32[]{:S(2)}) collective-permute-start(f32[32,4096]{1,0:T(8,128)S(1)} %copy-done.23), channel_id=1, source_target_pairs={{0,7},{1,6},{2,5},{3,4},{4,3},{5,2},{6,1},{7,0},{8,15},{9,14},{10,... | collective-permute-start | bytes 1572872 | tf_op jit(solution)/shard_map/ppermute | solution.py:122
  287.1 25.7 %collective-permute-start.21 = (f32[32,4096]{1,0:T(8,128)S(1)}, f32[32,4096]{1,0:T(8,128)S(1)}, u32[]{:S(2)}, u32[]{:S(2)}) collective-permute-start(f32[32,4096]{1,0:T(8,128)S(1)} %copy-done.21), channel_id=1, source_target_pairs={{0,3},{1,2},{2,1},{3,0},{4,7},{5,6},{6,5},{7,4},{8,11},{9,10},{10,... | collective-permute-start | bytes 1572872 | tf_op jit(solution)/shard_map/ppermute | solution.py:122
  291.7 52.9 %collective-permute-start.28 = (f32[32,4096]{1,0:T(8,128)}, f32[32,4096]{1,0:T(8,128)}, u32[]{:S(2)}, u32[]{:S(2)}) collective-permute-start(f32[32,4096]{1,0:T(8,128)} %get-tuple-element.82), channel_id=1, source_target_pairs={{0,4},{1,5},{2,6},{3,7},{4,0},{5,1},{6,2},{7,3},{8,12},{9,13},{10,... | collective-permute-start | bytes 1572872 | tf_op jit(solution)/shard_map/ppermute | solution.py:122
  292.8 52.5 %collective-permute-start.29 = (f32[32,4096]{1,0:T(8,128)}, f32[32,4096]{1,0:T(8,128)}, u32[]{:S(2)}, u32[]{:S(2)}) collective-permute-start(f32[32,4096]{1,0:T(8,128)} %get-tuple-element.83), channel_id=1, source_target_pairs={{0,5},{1,4},{2,7},{3,6},{4,1},{5,0},{6,3},{7,2},{8,13},{9,12},{10,... | collective-permute-start | bytes 1572872 | tf_op jit(solution)/shard_map/ppermute | solution.py:122
  327.2 26.5 %collective-permute-start.30 = (f32[32,4096]{1,0:T(8,128)}, f32[32,4096]{1,0:T(8,128)S(1)}, u32[]{:S(2)}, u32[]{:S(2)}) collective-permute-start(f32[32,4096]{1,0:T(8,128)} %get-tuple-element.84), channel_id=1, source_target_pairs={{0,2},{1,3},{2,0},{3,1},{4,6},{5,7},{6,4},{7,5},{8,10},{9,11},{10,... | collective-permute-start | bytes 1572872 | tf_op jit(solution)/shard_map/ppermute | solution.py:122
  344.6 37.1 %collective-permute-start.26 = (f32[32,4096]{1,0:T(8,128)}, f32[32,4096]{1,0:T(8,128)S(1)}, u32[]{:S(2)}, u32[]{:S(2)}) collective-permute-start(f32[32,4096]{1,0:T(8,128)} %get-tuple-element.80), channel_id=1, source_target_pairs={{0,6},{1,7},{2,4},{3,5},{4,2},{5,3},{6,0},{7,1},{8,14},{9,15},{10,... | collective-permute-start | bytes 1572872 | tf_op jit(solution)/shard_map/ppermute | solution.py:122
  345.2 42.6 %collective-permute-start.27 = (f32[32,4096]{1,0:T(8,128)}, f32[32,4096]{1,0:T(8,128)S(1)}, u32[]{:S(2)}, u32[]{:S(2)}) collective-permute-start(f32[32,4096]{1,0:T(8,128)} %get-tuple-element.81), channel_id=1, source_target_pairs={{0,7},{1,6},{2,5},{3,4},{4,3},{5,2},{6,1},{7,0},{8,15},{9,14},{10,... | collective-permute-start | bytes 1572872 | tf_op jit(solution)/shard_map/ppermute | solution.py:122
  (45 other events, 1184.7 us)

commit v3 on v2

--- a/solution.py
+++ b/solution.py
@@ -447,7 +447,7 @@
     inner, outer = (quarter, vel_count, 0), (0, vel_count // 2, half)
     far, near = partners(vel_count)
     steps = (*far, *near, 0)
-    urgent, ready = far[:2], (*far[:2], *near[:1], *far[2:3])
+    urgent, ready = far[:2], (*far, *near[:1])
 
     def send(arrays):
         return {step: swap(array, "vel", step) if step else array for step, array in arrays.items()}
@@ -459,7 +459,13 @@
     *late, first_rows, last_rows = move(
         me, particles, rest(urgent), cells, *inner, points, after=early[:1], edges=True
     )
-    inner_cubes = send(dict(zip((*urgent, *rest(urgent)), (*early, *late))))
+    inner_moved = dict(zip((*urgent, *rest(urgent)), (*early, *late)))
+    inner_cubes = send({step: inner_moved[step] for step in far})
+    behind, ahead = near, far[:1]
+    tied = lax.optimization_barrier(tuple(inner_moved[step] for step in behind) + tuple(inner_cubes[step] for step in ahead))
+    inner_moved.update(zip(behind, tied))
+    inner_cubes.update(zip(ahead, tied[len(behind) :]))
+    inner_cubes.update(send({step: inner_moved[step] for step in (*near, 0)}))
     space_pairs = [(i, i + 1) for i in range(space_count - 1)]
     low = lax.ppermute(last_rows, "space", space_pairs)
     high = lax.ppermute(first_rows, "space", [(target, source) for source, target in space_pairs])
@@ -519,10 +525,8 @@
         posts = [posts[step] for step in part]
         return settle(me, posts, part, membership(ids), emit, earlier, particles.shape, *plan)
 
-    last = far[-2:]
     out = wall(inner_back, steps, inner, None)
-    out = wall(outer_back, rest(last), outer, out)
-    return wall(outer_back, last, outer, out)
+    return wall(outer_back, (*far[:2], near[0], far[2], *near[1:], *far[3:], 0), outer, out)
 
 
 def solution(mesh):

time: 392 us -> 382 us (0.974)
  waiting for transfers between devices: 205 us -> 189 us
  starting transfers between devices: 51.2 us -> 59.9 us
    ppermute x31, waiting for transfers between devices: 205 us -> 189 us  [swap(): lax.ppermute(values, axis, [(i, i ^ step) for i in range(lax.axis_size(ax...]
    ppermute x31, starting transfers between devices: 45.7 us -> 54.4 us  [swap(): lax.ppermute(values, axis, [(i, i ^ step) for i in range(lax.axis_size(ax...]
    pallas_call x3 -> x2, Pallas kernels: 11.8 us -> 9.15 us  [settle(): pl.pallas_call(functools.partial(settle_kernel, steps, offset, low_groups...]
  transfers between devices with their start and end apart: 33 -> 33, of which waited for: 15 -> 16; matrix products, arithmetic and copies ran while one was open for 2% -> 2% of each run, Pallas kernels for 28% -> 28%
where the time goes in v3:
time: 382 us; the launch traced here: 380 us
  waiting for transfers between devices  189 us (49%)
  Pallas kernels  113 us (30%)
  starting transfers between devices  59.9 us (16%)
  local copies, waits for them, and re-layouts  8.08 us (2%)
  blocking collectives  6.21 us (2%)
    ppermute x31, waiting for transfers between devices, swap(): lax.ppermute(values, axis, [(i, i ^ step) for i in range(lax.axis_size(ax...  189 us
    pallas_call x2, Pallas kernels, collide(): pl.pallas_call(functools.partial(collide_kernel, steps), grid=(cells // s...  84.2 us
    ppermute x31, starting transfers between devices, swap(): lax.ppermute(values, axis, [(i, i ^ step) for i in range(lax.axis_size(ax...  54.4 us
    pallas_call x4, Pallas kernels, move(): pl.pallas_call(functools.partial(move_kernel, order, offset, low_groups,...  14 us
    pallas_call x2, Pallas kernels, settle(): pl.pallas_call(functools.partial(settle_kernel, steps, offset, low_groups...  9.15 us
  transfers between devices with their start and end apart: 33, of which 16 were waited for; matrix products, arithmetic and copies ran while one was open for 2% of the time, Pallas kernels for 28%

profile of v3, /device:TPU:18, one launch (start us, length us, event | category | flops | bytes accessed | tf_op | source)
XLA Modules:
  0.0 380.1 jit_solution(10679134747570229881)
XLA Ops:
  6.4 3.7 shard_map.137
  12.1 3.6 collective-permute-start.8
  19.5 29.7 %collective-permute-done.rest_0_ = f32[32,4096]{1,0:T(8,128)S(1)} collective-permute-done((f32[32,4096]{1,0:T(8,128)}, f32[32,4096]{1,0:T(8,128)S(1)}, u32[]{:S(2)}, u32[]{:S(2)}) %collective-permute-start) | collective-permute-done | bytes 524320 | tf_op jit(solution)/shard_map/ppermute | solution.py:122
  54.9 16.8 %collective-permute-done.1.rest_1_ = f32[32,4096]{1,0:T(8,128)S(1)} collective-permute-done((f32[32,4096]{1,0:T(8,128)}, f32[32,4096]{1,0:T(8,128)S(1)}, u32[]{:S(2)}, u32[]{:S(2)}) %collective-permute-start.1) | collective-permute-done | bytes 524320 | tf_op jit(solution)/shard_map/ppermute | solution.py:122
  73.3 4.5 %shard_map.138 = (f32[256,640]{1,0:T(8,128)}, f32[256,640]{1,0:T(8,128)}) custom-call(f32[32,1024]{1,0:T(8,128)} %reshape.106.gain, f32[32,1024]{1,0:T(8,128)} %reshape.107.freq, bf16[2,1024,640]{2,1,0:T(8,128)(2,1)} %constant.140.clone.pick), custom_call_target="tpu_custom_call" | custom-call | flops 1006632960 | bytes 2621440 | tf_op jit(solution)/shard_map/pallas_call | solution.py:106
  77.8 4.2 %shard_map.140 = (f32[32,4096]{1,0:T(8,128)}, f32[32,4096]{1,0:T(8,128)}, f32[32,4096]{1,0:T(8,128)}, f32[32,4096]{1,0:T(8,128)}, f32[32,4096]{1,0:T(8,128)}) custom-call(s32[1]{0:T(128)} %bitcast.me, f32[512,4096]{1,0:T(8,128)} %particles.7, f32[8,4096]{1,0:T(8,128)} %copy-done.6, f32[8,4096]{1,0:T(8,128)} %copy-done.7), custom_call_target="tpu_custom_call" | custom-call | flops 3276800 | bytes 6553600 | tf_op jit(solution)/shard_map/pallas_call | solution.py:204
  85.3 25.6 %collective-permute-done.3.rest_3_ = f32[32,4096]{1,0:T(8,128)S(1)} collective-permute-done((f32[32,4096]{1,0:T(8,128)}, f32[32,4096]{1,0:T(8,128)S(1)}, u32[]{:S(2)}, u32[]{:S(2)}) %collective-permute-start.3) | collective-permute-done | bytes 524320 | tf_op jit(solution)/shard_map/ppermute | solution.py:122
  117.1 41.9 %shard_map.139 = (f32[32,4096]{1,0:T(8,128)}, f32[32,4096]{1,0:T(8,128)}, f32[32,4096]{1,0:T(8,128)}, f32[32,4096]{1,0:T(8,128)}, f32[32,4096]{1,0:T(8,128)}, /*...) custom-call(s32[1]{0:T(128)} %bitcast.me, f32[32,4096]{1,0:T(8,128)} %copy-done.16, ...), custom_call_target="tpu_custom_call" | custom-call | flops 43486543872 | bytes 8388608 | tf_op jit(solution)/shard_map/pallas_call | solution.py:332
  159.1 3.7 shard_map.141
  164.9 12.4 %collective-permute-done.11.rest_2_ = f32[32,4096]{1,0:T(8,128)S(1)} collective-permute-done((f32[32,4096]{1,0:T(8,128)}, f32[32,4096]{1,0:T(8,128)S(1)}, u32[]{:S(2)}, u32[]{:S(2)}) %collective-permute-start.11) | collective-permute-done | bytes 524320 | tf_op jit(solution)/shard_map/ppermute | solution.py:122
  178.2 22.6 %collective-permute-done.12.rest_3_ = f32[32,4096]{1,0:T(8,128)S(1)} collective-permute-done((f32[32,4096]{1,0:T(8,128)}, f32[32,4096]{1,0:T(8,128)S(1)}, u32[]{:S(2)}, u32[]{:S(2)}) %collective-permute-start.12) | collective-permute-done | bytes 524320 | tf_op jit(solution)/shard_map/ppermute | solution.py:122
  203.6 42.3 %shard_map.142 = (f32[32,4096]{1,0:T(8,128)}, f32[32,4096]{1,0:T(8,128)}, f32[32,4096]{1,0:T(8,128)}, f32[32,4096]{1,0:T(8,128)}, f32[32,4096]{1,0:T(8,128)}, /*...) custom-call(s32[1]{0:T(128)} %bitcast.me, f32[32,4096]{1,0:T(8,128)} %copy-done.22, ...), custom_call_target="tpu_custom_call" | custom-call | flops 43486543872 | bytes 8388608 | tf_op jit(solution)/shard_map/pallas_call | solution.py:332
  246.0 5.8 %collective-permute-start.20 = (f32[32,4096]{1,0:T(8,128)S(1)}, f32[32,4096]{1,0:T(8,128)S(1)}, u32[]{:S(2)}, u32[]{:S(2)}) collective-permute-start(f32[32,4096]{1,0:T(8,128)S(1)} %copy-done.21), channel_id=1, source_target_pairs={{0,2},{1,3},{2,0},{3,1},{4,6},{5,7},{6,4},{7,5},{8,10},{9,11},{10,... | collective-permute-start | bytes 1572872 | tf_op jit(solution)/shard_map/ppermute | solution.py:122
  256.9 10.4 %collective-permute-done.18.refs_6_.rest_2_ = f32[32,4096]{1,0:T(8,128)S(1)} collective-permute-done((f32[32,4096]{1,0:T(8,128)}, f32[32,4096]{1,0:T(8,128)S(1)}, u32[]{:S(2)}, u32[]{:S(2)}) %collective-permute-start.18) | collective-permute-done | bytes 524320 | tf_op jit(solution)/shard_map/ppermute | solution.py:122
  267.3 27.0 %collective-permute-done.19.refs_7_.rest_3_ = f32[32,4096]{1,0:T(8,128)S(1)} collective-permute-done((f32[32,4096]{1,0:T(8,128)}, f32[32,4096]{1,0:T(8,128)S(1)}, u32[]{:S(2)}, u32[]{:S(2)}) %collective-permute-start.19) | collective-permute-done | bytes 524320 | tf_op jit(solution)/shard_map/ppermute | solution.py:122
  296.9 6.2 %psum.7 = f32[1,32]{1,0:T(1,128)S(1)} all-reduce(f32[1,32]{1,0:T(1,128)} %shard_map.143), channel_id=1, replica_groups=mesh['space'=4,'vel'=8] {'space'}, use_global_device_ids=true, to_apply=%region_3.4 | all-reduce | flops 32 | bytes 256 | tf_op jit(solution)/shard_map/psum | solution.py:502
  310.3 14.8 %collective-permute-start.25 = (f32[1,32]{1,0:T(1,128)S(1)}, f32[1,32]{1,0:T(1,128)S(1)}, u32[]{:S(2)}, u32[]{:S(2)}) collective-permute-start(f32[1,32]{1,0:T(1,128)S(1)} %add.354), channel_id=1, source_target_pairs={{0,4},{1,5},{2,6},{3,7},{4,0},{5,1},{6,2},{7,3},{8,12},{9,13},{10,... | collective-permute-start | bytes 392 | tf_op jit(solution)/shard_map/ppermute | solution.py:122
  325.1 9.7 %collective-permute-done.25 = f32[1,32]{1,0:T(1,128)S(1)} collective-permute-done((f32[1,32]{1,0:T(1,128)S(1)}, f32[1,32]{1,0:T(1,128)S(1)}, u32[]{:S(2)}, u32[]{:S(2)}) %collective-permute-start.25) | collective-permute-done | bytes 160 | tf_op jit(solution)/shard_map/ppermute | solution.py:122
  334.8 4.8 %collective-permute-start.30 = (f32[32,4096]{1,0:T(8,128)}, f32[32,4096]{1,0:T(8,128)S(1)}, u32[]{:S(2)}, u32[]{:S(2)}) collective-permute-start(f32[32,4096]{1,0:T(8,128)} %get-tuple-element.92), channel_id=1, source_target_pairs={{0,3},{1,2},{2,1},{3,0},{4,7},{5,6},{6,5},{7,4},{8,11},{9,10},{10,... | collective-permute-start | bytes 1572872 | tf_op jit(solution)/shard_map/ppermute | solution.py:122
  343.3 4.6 %shard_map.144.rest_8_ = f32[512,4096]{1,0:T(8,128)} custom-call(s32[1]{0:T(128)} %bitcast.me, f32[256,32]{1,0:T(8,128)} %copy.22.member, bf16[64,4096]{1,0:T(8,128)(2,1)} %pad_maximum_fusion.emit, f32[32,4096]{1,0:T(8,128)} %copy-done, f32[32,4096]{1,0:T(8,128)} %copy-done.1, f32[32,4096]{1,0:T(8,128)} %copy-done.2, f32[32,4096]{1,0:T(8,128)} %copy-done.3, ...), custom_call_target="tpu_custom_call" | custom-call | flops 134217728 | bytes 8388608 | tf_op jit(solution)/shard_map/pallas_call | solution.py:413
  347.9 13.0 %collective-permute-done.28.rest_2_ = f32[32,4096]{1,0:T(8,128)S(1)} collective-permute-done((f32[32,4096]{1,0:T(8,128)}, f32[32,4096]{1,0:T(8,128)S(1)}, u32[]{:S(2)}, u32[]{:S(2)}) %collective-permute-start.28) | collective-permute-done | bytes 524320 | tf_op jit(solution)/shard_map/ppermute | solution.py:122
  361.8 8.5 %collective-permute-done.30.rest_4_ = f32[32,4096]{1,0:T(8,128)S(1)} collective-permute-done((f32[32,4096]{1,0:T(8,128)}, f32[32,4096]{1,0:T(8,128)S(1)}, u32[]{:S(2)}, u32[]{:S(2)}) %collective-permute-start.30) | collective-permute-done | bytes 524320 | tf_op jit(solution)/shard_map/ppermute | solution.py:122
  370.3 4.0 %collective-permute-done.31.rest_5_ = f32[32,4096]{1,0:T(8,128)S(1)} collective-permute-done((f32[32,4096]{1,0:T(8,128)}, f32[32,4096]{1,0:T(8,128)S(1)}, u32[]{:S(2)}, u32[]{:S(2)}) %collective-permute-start.31) | collective-permute-done | bytes 524320 | tf_op jit(solution)/shard_map/ppermute | solution.py:122
  375.4 4.6 %shard_map.145 = f32[512,4096]{1,0:T(8,128)} custom-call(s32[1]{0:T(128)} %bitcast.me, f32[256,32]{1,0:T(8,128)} %copy.23.member, bf16[64,4096]{1,0:T(8,128)(2,1)} %pad_maximum_fusion.emit, f32[32,4096]{1,0:T(8,128)} %collective-permute-done.26.rest_0_, f32[32,4096]{1,0:T(8,128)} %collective-permute-done.27.rest_1_, ...), custom_call_target="tpu_custom_call", output_to_operand_aliasing={{}: (11, {})} | custom-call | flops 134217728 | bytes 8388608 | tf_op jit(solution)/shard_map/pallas_call | solution.py:413
  (140 shorter events, 55.2 us)
Async XLA Ops:
  2.4 46.7 %collective-permute-start = (f32[32,4096]{1,0:T(8,128)}, f32[32,4096]{1,0:T(8,128)S(1)}, u32[]{:S(2)}, u32[]{:S(2)}) collective-permute-start(f32[32,4096]{1,0:T(8,128)} %get-tuple-element.51.rest_0_), channel_id=1, source_target_pairs={{0,4},{1,5},{2,6},{3,7},{4,0},{5,1},{6,2},{7,3},{8,12},{9,13},{10,... | collective-permute-start | bytes 1572872 | tf_op jit(solution)/shard_map/ppermute | solution.py:122
  2.8 68.8 %collective-permute-start.1 = (f32[32,4096]{1,0:T(8,128)}, f32[32,4096]{1,0:T(8,128)S(1)}, u32[]{:S(2)}, u32[]{:S(2)}) collective-permute-start(f32[32,4096]{1,0:T(8,128)} %get-tuple-element.56), channel_id=1, source_target_pairs={{0,5},{1,4},{2,7},{3,6},{4,1},{5,0},{6,3},{7,2},{8,13},{9,12},{10,... | collective-permute-start | bytes 1572872 | tf_op jit(solution)/shard_map/ppermute | solution.py:122
  10.1 41.5 %collective-permute-start.7 = (f32[8,4096]{1,0:T(8,128)}, f32[8,4096]{1,0:T(8,128)S(1)}, u32[]{:S(2)}, u32[]{:S(2)}) collective-permute-start(f32[8,4096]{1,0:T(8,128)} %get-tuple-element.69), channel_id=1, source_target_pairs={{0,8},{8,16},{16,24},{1,9},{9,17},{17,25},{2,10},{10,18},{18,26},{... | collective-permute-start | bytes 393224 | tf_op jit(solution)/shard_map/ppermute | solution.py:470
  12.1 42.8 %collective-permute-start.8 = (f32[8,4096]{1,0:T(8,128)}, f32[8,4096]{1,0:T(8,128)S(1)}, u32[]{:S(2)}, u32[]{:S(2)}) collective-permute-start(f32[8,4096]{1,0:T(8,128)} %get-tuple-element.70), channel_id=1, source_target_pairs={{8,0},{16,8},{24,16},{9,1},{17,9},{25,17},{10,2},{18,10},{26,18},{... | collective-permute-start | bytes 393224 | tf_op jit(solution)/shard_map/ppermute | solution.py:471
  15.7 69.1 %collective-permute-start.2 = (f32[32,4096]{1,0:T(8,128)}, f32[32,4096]{1,0:T(8,128)S(1)}, u32[]{:S(2)}, u32[]{:S(2)}) collective-permute-start(f32[32,4096]{1,0:T(8,128)} %get-tuple-element.57), channel_id=1, source_target_pairs={{0,6},{1,7},{2,4},{3,5},{4,2},{5,3},{6,0},{7,1},{8,14},{9,15},{10,... | collective-permute-start | bytes 1572872 | tf_op jit(solution)/shard_map/ppermute | solution.py:122
  49.2 61.7 %collective-permute-start.3 = (f32[32,4096]{1,0:T(8,128)}, f32[32,4096]{1,0:T(8,128)S(1)}, u32[]{:S(2)}, u32[]{:S(2)}) collective-permute-start(f32[32,4096]{1,0:T(8,128)} %get-tuple-element.58), channel_id=1, source_target_pairs={{0,7},{1,6},{2,5},{3,4},{4,3},{5,2},{6,1},{7,0},{8,15},{9,14},{10,... | collective-permute-start | bytes 1572872 | tf_op jit(solution)/shard_map/ppermute | solution.py:122
  51.7 60.0 %collective-permute-start.4 = (f32[32,4096]{1,0:T(8,128)}, f32[32,4096]{1,0:T(8,128)}, u32[]{:S(2)}, u32[]{:S(2)}) collective-permute-start(f32[32,4096]{1,0:T(8,128)} %get-tuple-element.59), channel_id=1, source_target_pairs={{0,2},{1,3},{2,0},{3,1},{4,6},{5,7},{6,4},{7,5},{8,10},{9,11},{10,... | collective-permute-start | bytes 1572872 | tf_op jit(solution)/shard_map/ppermute | solution.py:122
  54.9 56.8 %collective-permute-start.5 = (f32[32,4096]{1,0:T(8,128)}, f32[32,4096]{1,0:T(8,128)}, u32[]{:S(2)}, u32[]{:S(2)}) collective-permute-start(f32[32,4096]{1,0:T(8,128)} %get-tuple-element.60), channel_id=1, source_target_pairs={{0,3},{1,2},{2,1},{3,0},{4,7},{5,6},{6,5},{7,4},{8,11},{9,10},{10,... | collective-permute-start | bytes 1572872 | tf_op jit(solution)/shard_map/ppermute | solution.py:122
  71.7 42.0 %collective-permute-start.6 = (f32[32,4096]{1,0:T(8,128)}, f32[32,4096]{1,0:T(8,128)}, u32[]{:S(2)}, u32[]{:S(2)}) collective-permute-start(f32[32,4096]{1,0:T(8,128)} %get-tuple-element.61), channel_id=1, source_target_pairs={{0,1},{1,0},{2,3},{3,2},{4,5},{5,4},{6,7},{7,6},{8,9},{9,8},{10,11... | collective-permute-start | bytes 1572872 | tf_op jit(solution)/shard_map/ppermute | solution.py:122
  84.8 78.0 %collective-permute-start.9 = (f32[32,4096]{1,0:T(8,128)}, f32[32,4096]{1,0:T(8,128)S(1)}, u32[]{:S(2)}, u32[]{:S(2)}) collective-permute-start(f32[32,4096]{1,0:T(8,128)} %get-tuple-element.71), channel_id=1, source_target_pairs={{0,4},{1,5},{2,6},{3,7},{4,0},{5,1},{6,2},{7,3},{8,12},{9,13},{10,... | collective-permute-start | bytes 1572872 | tf_op jit(solution)/shard_map/ppermute | solution.py:122
  111.7 51.6 %collective-permute-start.10 = (f32[32,4096]{1,0:T(8,128)}, f32[32,4096]{1,0:T(8,128)S(1)}, u32[]{:S(2)}, u32[]{:S(2)}) collective-permute-start(f32[32,4096]{1,0:T(8,128)} %get-tuple-element.72), channel_id=1, source_target_pairs={{0,5},{1,4},{2,7},{3,6},{4,1},{5,0},{6,3},{7,2},{8,13},{9,12},{10,... | collective-permute-start | bytes 1572872 | tf_op jit(solution)/shard_map/ppermute | solution.py:122
  111.7 65.7 %collective-permute-start.11 = (f32[32,4096]{1,0:T(8,128)}, f32[32,4096]{1,0:T(8,128)S(1)}, u32[]{:S(2)}, u32[]{:S(2)}) collective-permute-start(f32[32,4096]{1,0:T(8,128)} %get-tuple-element.73), channel_id=1, source_target_pairs={{0,6},{1,7},{2,4},{3,5},{4,2},{5,3},{6,0},{7,1},{8,14},{9,15},{10,... | collective-permute-start | bytes 1572872 | tf_op jit(solution)/shard_map/ppermute | solution.py:122
  111.7 89.1 %collective-permute-start.12 = (f32[32,4096]{1,0:T(8,128)}, f32[32,4096]{1,0:T(8,128)S(1)}, u32[]{:S(2)}, u32[]{:S(2)}) collective-permute-start(f32[32,4096]{1,0:T(8,128)} %get-tuple-element.74), channel_id=1, source_target_pairs={{0,7},{1,6},{2,5},{3,4},{4,3},{5,2},{6,1},{7,0},{8,15},{9,14},{10,... | collective-permute-start | bytes 1572872 | tf_op jit(solution)/shard_map/ppermute | solution.py:122
  113.7 88.0 %collective-permute-start.13 = (f32[32,4096]{1,0:T(8,128)}, f32[32,4096]{1,0:T(8,128)}, u32[]{:S(2)}, u32[]{:S(2)}) collective-permute-start(f32[32,4096]{1,0:T(8,128)} %get-tuple-element.75), channel_id=1, source_target_pairs={{0,2},{1,3},{2,0},{3,1},{4,6},{5,7},{6,4},{7,5},{8,10},{9,11},{10,... | collective-permute-start | bytes 1572872 | tf_op jit(solution)/shard_map/ppermute | solution.py:122
  162.8 40.3 %collective-permute-start.14 = (f32[32,4096]{1,0:T(8,128)}, f32[32,4096]{1,0:T(8,128)}, u32[]{:S(2)}, u32[]{:S(2)}) collective-permute-start(f32[32,4096]{1,0:T(8,128)} %get-tuple-element.76), channel_id=1, source_target_pairs={{0,3},{1,2},{2,1},{3,0},{4,7},{5,6},{6,5},{7,4},{8,11},{9,10},{10,... | collective-permute-start | bytes 1572872 | tf_op jit(solution)/shard_map/ppermute | solution.py:122
  178.2 73.5 %collective-permute-start.16 = (f32[32,4096]{1,0:T(8,128)}, f32[32,4096]{1,0:T(8,128)S(1)}, u32[]{:S(2)}, u32[]{:S(2)}) collective-permute-start(f32[32,4096]{1,0:T(8,128)} %get-tuple-element.81), channel_id=1, source_target_pairs={{0,4},{1,5},{2,6},{3,7},{4,0},{5,1},{6,2},{7,3},{8,12},{9,13},{10,... | collective-permute-start | bytes 1572872 | tf_op jit(solution)/shard_map/ppermute | solution.py:122
  201.6 53.6 %collective-permute-start.17 = (f32[32,4096]{1,0:T(8,128)}, f32[32,4096]{1,0:T(8,128)S(1)}, u32[]{:S(2)}, u32[]{:S(2)}) collective-permute-start(f32[32,4096]{1,0:T(8,128)} %get-tuple-element.82), channel_id=1, source_target_pairs={{0,5},{1,4},{2,7},{3,6},{4,1},{5,0},{6,3},{7,2},{8,13},{9,12},{10,... | collective-permute-start | bytes 1572872 | tf_op jit(solution)/shard_map/ppermute | solution.py:122
  201.6 65.7 %collective-permute-start.18 = (f32[32,4096]{1,0:T(8,128)}, f32[32,4096]{1,0:T(8,128)S(1)}, u32[]{:S(2)}, u32[]{:S(2)}) collective-permute-start(f32[32,4096]{1,0:T(8,128)} %get-tuple-element.83), channel_id=1, source_target_pairs={{0,6},{1,7},{2,4},{3,5},{4,2},{5,3},{6,0},{7,1},{8,14},{9,15},{10,... | collective-permute-start | bytes 1572872 | tf_op jit(solution)/shard_map/ppermute | solution.py:122
  203.1 91.2 %collective-permute-start.19 = (f32[32,4096]{1,0:T(8,128)}, f32[32,4096]{1,0:T(8,128)S(1)}, u32[]{:S(2)}, u32[]{:S(2)}) collective-permute-start(f32[32,4096]{1,0:T(8,128)} %get-tuple-element.84), channel_id=1, source_target_pairs={{0,7},{1,6},{2,5},{3,4},{4,3},{5,2},{6,1},{7,0},{8,15},{9,14},{10,... | collective-permute-start | bytes 1572872 | tf_op jit(solution)/shard_map/ppermute | solution.py:122
  246.0 48.4 %collective-permute-start.20 = (f32[32,4096]{1,0:T(8,128)S(1)}, f32[32,4096]{1,0:T(8,128)S(1)}, u32[]{:S(2)}, u32[]{:S(2)}) collective-permute-start(f32[32,4096]{1,0:T(8,128)S(1)} %copy-done.21), channel_id=1, source_target_pairs={{0,2},{1,3},{2,0},{3,1},{4,6},{5,7},{6,4},{7,5},{8,10},{9,11},{10,... | collective-permute-start | bytes 1572872 | tf_op jit(solution)/shard_map/ppermute | solution.py:122
  251.7 42.7 %collective-permute-start.21 = (f32[32,4096]{1,0:T(8,128)S(1)}, f32[32,4096]{1,0:T(8,128)S(1)}, u32[]{:S(2)}, u32[]{:S(2)}) collective-permute-start(f32[32,4096]{1,0:T(8,128)S(1)} %copy-done.20), channel_id=1, source_target_pairs={{0,3},{1,2},{2,1},{3,0},{4,7},{5,6},{6,5},{7,4},{8,11},{9,10},{10,... | collective-permute-start | bytes 1572872 | tf_op jit(solution)/shard_map/ppermute | solution.py:122
  267.3 72.3 %collective-permute-start.26 = (f32[32,4096]{1,0:T(8,128)}, f32[32,4096]{1,0:T(8,128)}, u32[]{:S(2)}, u32[]{:S(2)}) collective-permute-start(f32[32,4096]{1,0:T(8,128)} %get-tuple-element.88), channel_id=1, source_target_pairs={{0,4},{1,5},{2,6},{3,7},{4,0},{5,1},{6,2},{7,3},{8,12},{9,13},{10,... | collective-permute-start | bytes 1572872 | tf_op jit(solution)/shard_map/ppermute | solution.py:122
  294.3 47.9 %collective-permute-start.27 = (f32[32,4096]{1,0:T(8,128)}, f32[32,4096]{1,0:T(8,128)}, u32[]{:S(2)}, u32[]{:S(2)}) collective-permute-start(f32[32,4096]{1,0:T(8,128)} %get-tuple-element.89), channel_id=1, source_target_pairs={{0,5},{1,4},{2,7},{3,6},{4,1},{5,0},{6,3},{7,2},{8,13},{9,12},{10,... | collective-permute-start | bytes 1572872 | tf_op jit(solution)/shard_map/ppermute | solution.py:122
  307.6 53.3 %collective-permute-start.28 = (f32[32,4096]{1,0:T(8,128)}, f32[32,4096]{1,0:T(8,128)S(1)}, u32[]{:S(2)}, u32[]{:S(2)}) collective-permute-start(f32[32,4096]{1,0:T(8,128)} %get-tuple-element.90), channel_id=1, source_target_pairs={{0,2},{1,3},{2,0},{3,1},{4,6},{5,7},{6,4},{7,5},{8,10},{9,11},{10,... | collective-permute-start | bytes 1572872 | tf_op jit(solution)/shard_map/ppermute | solution.py:122
  (37 other events, 793.8 us)

commit v4 on v3

--- a/solution.py
+++ b/solution.py
@@ -370,18 +370,19 @@
     )(*flat, *after)
 
 
-def settle_kernel(steps, offset, low_groups, gap, me, member, emit, *rest):
-    count = len(steps)
+def settle_kernel(groups, me, member, emit, *rest):
+    count = len(groups)
     posts = rest[:count]
     out, held, emission, in_sems, out_sems = rest[-5:]
-    cells, width = held.shape[1:]
+    cells = held.shape[1]
     at = me[0]
 
     def fetch(k):
         return pltpu.make_async_copy(posts[k], held.at[k], in_sems.at[k])
 
     def store(k):
-        first = offset + start_of(at ^ steps[k], cells, low_groups, gap)
+        step, (offset, low_groups, gap) = groups[k]
+        first = offset + start_of(at ^ step, cells, low_groups, gap)
         return pltpu.make_async_copy(held.at[k], out.at[pl.ds(first, cells)], out_sems.at[k])
 
     for k in range(count):
@@ -391,15 +392,15 @@
     emission[...] = dot(jnp.concatenate([chosen, chosen], axis=1).astype(jnp.bfloat16), emit[...])
     for k in range(count):
         fetch(k).wait()
-        rows = pl.ds(pl.multiple_of(k * cells, sub), cells)
+        rows = slice(k * cells, (k + 1) * cells)
         post = held[k]
-        held[k] = post + (accommodation * emission[rows, :] - share[k * cells : (k + 1) * cells] * post)
+        held[k] = post + (accommodation * emission[rows, :] - share[rows] * post)
         store(k).start()
     for k in range(count):
         store(k).wait()
 
 
-def settle(me, posts, steps, member, emit, earlier, shape, offset, low_groups, gap):
+def settle(me, posts, groups, member, emit, earlier, shape):
     cells, width = posts[0].shape
     count = len(posts)
     size = count * cells * width
@@ -411,7 +412,7 @@
         operands.append(earlier)
         in_specs.append(local(pltpu.HBM))
     return pl.pallas_call(
-        functools.partial(settle_kernel, steps, offset, low_groups, gap),
+        functools.partial(settle_kernel, groups),
         in_specs=in_specs,
         out_specs=local(pltpu.HBM),
         out_shape=jax.ShapeDtypeStruct(shape, jnp.float32),
@@ -422,7 +423,7 @@
             pltpu.SemaphoreType.DMA((count,)),
         ],
         input_output_aliases=aliases,
-        compiler_params=pltpu.CompilerParams(vmem_limit_bytes=vmem_bytes),
+        compiler_params=pltpu.CompilerParams(vmem_limit_bytes=8 * size + 6 * 2**20),
         cost_estimate=pl.CostEstimate(
             flops=4 * member.shape[1] * size, bytes_accessed=8 * size, transcendentals=0
         ),
@@ -447,7 +448,7 @@
     inner, outer = (quarter, vel_count, 0), (0, vel_count // 2, half)
     far, near = partners(vel_count)
     steps = (*far, *near, 0)
-    urgent, ready = far[:2], (*far, *near[:1])
+    urgent, ready = far[:1], (*far, *near[:1])
 
     def send(arrays):
         return {step: swap(array, "vel", step) if step else array for step, array in arrays.items()}
@@ -520,13 +521,15 @@
     emit_high = lax.reduce_precision(emission, exponent_bits=8, mantissa_bits=7)
     emit = jnp.concatenate([emit_high, emission - emit_high], axis=0).astype(jnp.bfloat16)
 
-    def wall(posts, part, plan, earlier):
-        ids = jnp.concatenate([cells_of(plan, vel_at ^ step) for step in part])
-        posts = [posts[step] for step in part]
-        return settle(me, posts, part, membership(ids), emit, earlier, particles.shape, *plan)
-
-    out = wall(inner_back, steps, inner, None)
-    return wall(outer_back, (*far[:2], near[0], far[2], *near[1:], *far[3:], 0), outer, out)
+    def wall(arrived, earlier):
+        groups, posts = zip(*arrived)
+        ids = jnp.concatenate([cells_of(plan, vel_at ^ step) for step, plan in groups])
+        return settle(me, posts, groups, membership(ids), emit, earlier, particles.shape)
+
+    final = (near[0], far[2], *near[1:], *far[3:])
+    first = [((step, inner), inner_back[step]) for step in steps]
+    first += [((step, outer), outer_back[step]) for step in rest(final)]
+    return wall([((step, outer), outer_back[step]) for step in final], wall(first, None))
 
 
 def solution(mesh):

time: 382 us -> 378 us (0.990)
  waiting for transfers between devices: 189 us -> 180 us
  local copies, waits for them, and re-layouts: 8.08 us -> 14.1 us
    ppermute x31, waiting for transfers between devices: 189 us -> 180 us  [swap(): lax.ppermute(values, axis, [(i, i ^ step) for i in range(lax.axis_size(ax...]
    unnamed x57 -> x63, local copies, waits for them, and re-layouts: 4.66 us -> 11.9 us
  transfers between devices with their start and end apart: 33 -> 33, of which waited for: 16 -> 17; matrix products, arithmetic and copies ran while one was open for 2% -> 1% of each run, Pallas kernels for 28% -> 28%
where the time goes in v4:
time: 378 us; the launch traced here: 376 us
  waiting for transfers between devices  180 us (48%)
  Pallas kernels  111 us (29%)
  starting transfers between devices  61 us (16%)
  local copies, waits for them, and re-layouts  14.1 us (4%)
  blocking collectives  6.19 us (2%)
    ppermute x31, waiting for transfers between devices, swap(): lax.ppermute(values, axis, [(i, i ^ step) for i in range(lax.axis_size(ax...  180 us
    pallas_call x2, Pallas kernels, collide(): pl.pallas_call(functools.partial(collide_kernel, steps), grid=(cells // s...  84.2 us
    ppermute x31, starting transfers between devices, swap(): lax.ppermute(values, axis, [(i, i ^ step) for i in range(lax.axis_size(ax...  55.4 us
    pallas_call x4, Pallas kernels, move(): pl.pallas_call(functools.partial(move_kernel, order, offset, low_groups,...  14.6 us
    unnamed x63, local copies, waits for them, and re-layouts  11.9 us
  transfers between devices with their start and end apart: 33, of which 17 were waited for; matrix products, arithmetic and copies ran while one was open for 1% of the time, Pallas kernels for 28%

profile of v4, /device:TPU:18, one launch (start us, length us, event | category | flops | bytes accessed | tf_op | source)
XLA Modules:
  0.0 375.7 jit_solution(4470948895619230649)
XLA Ops:
  2.6 4.6 %shard_map.137 = (f32[32,4096]{1,0:T(8,128)}, f32[32,4096]{1,0:T(8,128)}, f32[32,4096]{1,0:T(8,128)}, f32[32,4096]{1,0:T(8,128)}, f32[32,4096]{1,0:T(8,128)}, /*...) custom-call(s32[1]{0:T(128)} %bitcast.me, f32[512,4096]{1,0:T(8,128)} %particles.7, ...), custom_call_target="tpu_custom_call" | custom-call | flops 4587520 | bytes 9175040 | tf_op jit(solution)/shard_map/pallas_call | solution.py:204
  18.5 30.5 %collective-permute-done.rest_0_ = f32[32,4096]{1,0:T(8,128)S(1)} collective-permute-done((f32[32,4096]{1,0:T(8,128)}, f32[32,4096]{1,0:T(8,128)S(1)}, u32[]{:S(2)}, u32[]{:S(2)}) %collective-permute-start) | collective-permute-done | bytes 524320 | tf_op jit(solution)/shard_map/ppermute | solution.py:122
  54.7 16.8 %collective-permute-done.1.rest_1_ = f32[32,4096]{1,0:T(8,128)S(1)} collective-permute-done((f32[32,4096]{1,0:T(8,128)}, f32[32,4096]{1,0:T(8,128)S(1)}, u32[]{:S(2)}, u32[]{:S(2)}) %collective-permute-start.1) | collective-permute-done | bytes 524320 | tf_op jit(solution)/shard_map/ppermute | solution.py:122
  75.0 4.5 %shard_map.138 = (f32[256,640]{1,0:T(8,128)}, f32[256,640]{1,0:T(8,128)}) custom-call(f32[32,1024]{1,0:T(8,128)} %reshape.106.gain, f32[32,1024]{1,0:T(8,128)} %reshape.107.freq, bf16[2,1024,640]{2,1,0:T(8,128)(2,1)} %constant.140.clone.pick), custom_call_target="tpu_custom_call" | custom-call | flops 1006632960 | bytes 2621440 | tf_op jit(solution)/shard_map/pallas_call | solution.py:106
  79.5 4.2 %shard_map.140 = (f32[32,4096]{1,0:T(8,128)}, f32[32,4096]{1,0:T(8,128)}, f32[32,4096]{1,0:T(8,128)}, f32[32,4096]{1,0:T(8,128)}, f32[32,4096]{1,0:T(8,128)}) custom-call(s32[1]{0:T(128)} %bitcast.me, f32[512,4096]{1,0:T(8,128)} %particles.7, f32[8,4096]{1,0:T(8,128)} %copy-done.14, f32[8,4096]{1,0:T(8,128)} %copy-done.15), custom_call_target="tpu_custom_call" | custom-call | flops 3276800 | bytes 6553600 | tf_op jit(solution)/shard_map/pallas_call | solution.py:204
  87.0 23.7 %collective-permute-done.3.rest_3_ = f32[32,4096]{1,0:T(8,128)S(1)} collective-permute-done((f32[32,4096]{1,0:T(8,128)}, f32[32,4096]{1,0:T(8,128)S(1)}, u32[]{:S(2)}, u32[]{:S(2)}) %collective-permute-start.3) | collective-permute-done | bytes 524320 | tf_op jit(solution)/shard_map/ppermute | solution.py:122
  113.5 4.1 %collective-permute-start.13 = (f32[32,4096]{1,0:T(8,128)}, f32[32,4096]{1,0:T(8,128)}, u32[]{:S(2)}, u32[]{:S(2)}) collective-permute-start(f32[32,4096]{1,0:T(8,128)} %get-tuple-element.73), channel_id=1, source_target_pairs={{0,2},{1,3},{2,0},{3,1},{4,6},{5,7},{6,4},{7,5},{8,10},{9,11},{10,... | collective-permute-start | bytes 1572872 | tf_op jit(solution)/shard_map/ppermute | solution.py:122
  117.5 42.0 %shard_map.139 = (f32[32,4096]{1,0:T(8,128)}, f32[32,4096]{1,0:T(8,128)}, f32[32,4096]{1,0:T(8,128)}, f32[32,4096]{1,0:T(8,128)}, f32[32,4096]{1,0:T(8,128)}, /*...) custom-call(s32[1]{0:T(128)} %bitcast.me, f32[32,4096]{1,0:T(8,128)} %copy-done.19, ...), custom_call_target="tpu_custom_call" | custom-call | flops 43486543872 | bytes 8388608 | tf_op jit(solution)/shard_map/pallas_call | solution.py:332
  159.5 3.7 shard_map.141
  165.3 11.9 %collective-permute-done.11.rest_2_ = f32[32,4096]{1,0:T(8,128)S(1)} collective-permute-done((f32[32,4096]{1,0:T(8,128)}, f32[32,4096]{1,0:T(8,128)S(1)}, u32[]{:S(2)}, u32[]{:S(2)}) %collective-permute-start.11) | collective-permute-done | bytes 524320 | tf_op jit(solution)/shard_map/ppermute | solution.py:122
  178.0 22.6 %collective-permute-done.12.rest_3_ = f32[32,4096]{1,0:T(8,128)S(1)} collective-permute-done((f32[32,4096]{1,0:T(8,128)}, f32[32,4096]{1,0:T(8,128)S(1)}, u32[]{:S(2)}, u32[]{:S(2)}) %collective-permute-start.12) | collective-permute-done | bytes 524320 | tf_op jit(solution)/shard_map/ppermute | solution.py:122
  203.4 42.3 %shard_map.142 = (f32[32,4096]{1,0:T(8,128)}, f32[32,4096]{1,0:T(8,128)}, f32[32,4096]{1,0:T(8,128)}, f32[32,4096]{1,0:T(8,128)}, f32[32,4096]{1,0:T(8,128)}, /*...) custom-call(s32[1]{0:T(128)} %bitcast.me, f32[32,4096]{1,0:T(8,128)} %copy-done.25, ...), custom_call_target="tpu_custom_call" | custom-call | flops 43486543872 | bytes 8388608 | tf_op jit(solution)/shard_map/pallas_call | solution.py:332
  245.7 5.3 %collective-permute-start.20 = (f32[32,4096]{1,0:T(8,128)S(1)}, f32[32,4096]{1,0:T(8,128)S(1)}, u32[]{:S(2)}, u32[]{:S(2)}) collective-permute-start(f32[32,4096]{1,0:T(8,128)S(1)} %copy-done.24), channel_id=1, source_target_pairs={{0,2},{1,3},{2,0},{3,1},{4,6},{5,7},{6,4},{7,5},{8,10},{9,11},{10,... | collective-permute-start | bytes 1572872 | tf_op jit(solution)/shard_map/ppermute | solution.py:122
  251.1 4.2 %collective-permute-done.17.refs_5_.rest_1_ = f32[32,4096]{1,0:T(8,128)S(1)} collective-permute-done((f32[32,4096]{1,0:T(8,128)}, f32[32,4096]{1,0:T(8,128)S(1)}, u32[]{:S(2)}, u32[]{:S(2)}) %collective-permute-start.17) | collective-permute-done | bytes 524320 | tf_op jit(solution)/shard_map/ppermute | solution.py:122
  257.0 10.1 %collective-permute-done.18.refs_6_.rest_2_ = f32[32,4096]{1,0:T(8,128)S(1)} collective-permute-done((f32[32,4096]{1,0:T(8,128)}, f32[32,4096]{1,0:T(8,128)S(1)}, u32[]{:S(2)}, u32[]{:S(2)}) %collective-permute-start.18) | collective-permute-done | bytes 524320 | tf_op jit(solution)/shard_map/ppermute | solution.py:122
  267.1 26.1 %collective-permute-done.19.refs_7_.rest_3_ = f32[32,4096]{1,0:T(8,128)S(1)} collective-permute-done((f32[32,4096]{1,0:T(8,128)}, f32[32,4096]{1,0:T(8,128)S(1)}, u32[]{:S(2)}, u32[]{:S(2)}) %collective-permute-start.19) | collective-permute-done | bytes 524320 | tf_op jit(solution)/shard_map/ppermute | solution.py:122
  295.7 6.2 %psum.7 = f32[1,32]{1,0:T(1,128)S(1)} all-reduce(f32[1,32]{1,0:T(1,128)} %shard_map.143), channel_id=1, replica_groups=mesh['space'=4,'vel'=8] {'space'}, use_global_device_ids=true, to_apply=%region_3.4 | all-reduce | flops 32 | bytes 256 | tf_op jit(solution)/shard_map/psum | solution.py:503
  309.1 15.1 %collective-permute-start.25 = (f32[1,32]{1,0:T(1,128)S(1)}, f32[1,32]{1,0:T(1,128)S(1)}, u32[]{:S(2)}, u32[]{:S(2)}) collective-permute-start(f32[1,32]{1,0:T(1,128)S(1)} %add.346), channel_id=1, source_target_pairs={{0,4},{1,5},{2,6},{3,7},{4,0},{5,1},{6,2},{7,3},{8,12},{9,13},{10,... | collective-permute-start | bytes 392 | tf_op jit(solution)/shard_map/ppermute | solution.py:122
  324.2 10.6 %collective-permute-done.25 = f32[1,32]{1,0:T(1,128)S(1)} collective-permute-done((f32[1,32]{1,0:T(1,128)S(1)}, f32[1,32]{1,0:T(1,128)S(1)}, u32[]{:S(2)}, u32[]{:S(2)}) %collective-permute-start.25) | collective-permute-done | bytes 160 | tf_op jit(solution)/shard_map/ppermute | solution.py:122
  334.8 3.7 collective-permute-start.28
  349.7 4.0 %shard_map.144.rest_5_ = f32[512,4096]{1,0:T(8,128)} custom-call(s32[1]{0:T(128)} %bitcast.me, f32[352,32]{1,0:T(8,128)S(1)} %copy.25.member, bf16[64,4096]{1,0:T(8,128)(2,1)S(1)} %pad_maximum_fusion.emit, f32[32,4096]{1,0:T(8,128)S(1)} %copy-done.1, f32[32,4096]{1,0:T(8,128)S(1)} %copy-done.3, f32[32,4096]{1,0:T(8,128)S(1)} %copy-done.5, ...), custom_call_target="tpu_custom_call" | custom-call | flops 184549376 | bytes 11534336 | tf_op jit(solution)/shard_map/pallas_call | solution.py:414
  353.7 6.0 %collective-permute-done.26.rest_0_ = f32[32,4096]{1,0:T(8,128)S(1)} collective-permute-done((f32[32,4096]{1,0:T(8,128)}, f32[32,4096]{1,0:T(8,128)S(1)}, u32[]{:S(2)}, u32[]{:S(2)}) %collective-permute-start.26) | collective-permute-done | bytes 524320 | tf_op jit(solution)/shard_map/ppermute | solution.py:122
  360.7 8.4 %collective-permute-done.28.rest_2_ = f32[32,4096]{1,0:T(8,128)S(1)} collective-permute-done((f32[32,4096]{1,0:T(8,128)}, f32[32,4096]{1,0:T(8,128)S(1)}, u32[]{:S(2)}, u32[]{:S(2)}) %collective-permute-start.28) | collective-permute-done | bytes 524320 | tf_op jit(solution)/shard_map/ppermute | solution.py:122
  369.1 4.0 %collective-permute-done.29.rest_3_ = f32[32,4096]{1,0:T(8,128)S(1)} collective-permute-done((f32[32,4096]{1,0:T(8,128)}, f32[32,4096]{1,0:T(8,128)S(1)}, u32[]{:S(2)}, u32[]{:S(2)}) %collective-permute-start.29) | collective-permute-done | bytes 524320 | tf_op jit(solution)/shard_map/ppermute | solution.py:122
  (148 shorter events, 60.5 us)
Async XLA Ops:
  2.2 46.7 %collective-permute-start = (f32[32,4096]{1,0:T(8,128)}, f32[32,4096]{1,0:T(8,128)S(1)}, u32[]{:S(2)}, u32[]{:S(2)}) collective-permute-start(f32[32,4096]{1,0:T(8,128)} %shard_map.136.rest_0_), channel_id=1, source_target_pairs={{0,4},{1,5},{2,6},{3,7},{4,0},{5,1},{6,2},{7,3},{8,12},{9,13},{10,... | collective-permute-start | bytes 1572872 | tf_op jit(solution)/shard_map/ppermute | solution.py:122
  7.2 44.2 %collective-permute-start.7 = (f32[8,4096]{1,0:T(8,128)}, f32[8,4096]{1,0:T(8,128)S(1)}, u32[]{:S(2)}, u32[]{:S(2)}) collective-permute-start(f32[8,4096]{1,0:T(8,128)} %get-tuple-element.67), channel_id=1, source_target_pairs={{0,8},{8,16},{16,24},{1,9},{9,17},{17,25},{2,10},{10,18},{18,26},{... | collective-permute-start | bytes 393224 | tf_op jit(solution)/shard_map/ppermute | solution.py:471
  9.1 45.5 %collective-permute-start.8 = (f32[8,4096]{1,0:T(8,128)}, f32[8,4096]{1,0:T(8,128)S(1)}, u32[]{:S(2)}, u32[]{:S(2)}) collective-permute-start(f32[8,4096]{1,0:T(8,128)} %get-tuple-element.68), channel_id=1, source_target_pairs={{8,0},{16,8},{24,16},{9,1},{17,9},{25,17},{10,2},{18,10},{26,18},{... | collective-permute-start | bytes 393224 | tf_op jit(solution)/shard_map/ppermute | solution.py:472
  12.8 58.7 %collective-permute-start.1 = (f32[32,4096]{1,0:T(8,128)}, f32[32,4096]{1,0:T(8,128)S(1)}, u32[]{:S(2)}, u32[]{:S(2)}) collective-permute-start(f32[32,4096]{1,0:T(8,128)} %get-tuple-element.54), channel_id=1, source_target_pairs={{0,5},{1,4},{2,7},{3,6},{4,1},{5,0},{6,3},{7,2},{8,13},{9,12},{10,... | collective-permute-start | bytes 1572872 | tf_op jit(solution)/shard_map/ppermute | solution.py:122
  16.4 68.2 %collective-permute-start.2 = (f32[32,4096]{1,0:T(8,128)}, f32[32,4096]{1,0:T(8,128)S(1)}, u32[]{:S(2)}, u32[]{:S(2)}) collective-permute-start(f32[32,4096]{1,0:T(8,128)} %get-tuple-element.55), channel_id=1, source_target_pairs={{0,6},{1,7},{2,4},{3,5},{4,2},{5,3},{6,0},{7,1},{8,14},{9,15},{10,... | collective-permute-start | bytes 1572872 | tf_op jit(solution)/shard_map/ppermute | solution.py:122
  48.9 61.7 %collective-permute-start.3 = (f32[32,4096]{1,0:T(8,128)}, f32[32,4096]{1,0:T(8,128)S(1)}, u32[]{:S(2)}, u32[]{:S(2)}) collective-permute-start(f32[32,4096]{1,0:T(8,128)} %get-tuple-element.56), channel_id=1, source_target_pairs={{0,7},{1,6},{2,5},{3,4},{4,3},{5,2},{6,1},{7,0},{8,15},{9,14},{10,... | collective-permute-start | bytes 1572872 | tf_op jit(solution)/shard_map/ppermute | solution.py:122
  51.5 60.0 %collective-permute-start.4 = (f32[32,4096]{1,0:T(8,128)}, f32[32,4096]{1,0:T(8,128)}, u32[]{:S(2)}, u32[]{:S(2)}) collective-permute-start(f32[32,4096]{1,0:T(8,128)} %get-tuple-element.57), channel_id=1, source_target_pairs={{0,2},{1,3},{2,0},{3,1},{4,6},{5,7},{6,4},{7,5},{8,10},{9,11},{10,... | collective-permute-start | bytes 1572872 | tf_op jit(solution)/shard_map/ppermute | solution.py:122
  54.6 56.8 %collective-permute-start.5 = (f32[32,4096]{1,0:T(8,128)}, f32[32,4096]{1,0:T(8,128)}, u32[]{:S(2)}, u32[]{:S(2)}) collective-permute-start(f32[32,4096]{1,0:T(8,128)} %get-tuple-element.58), channel_id=1, source_target_pairs={{0,3},{1,2},{2,1},{3,0},{4,7},{5,6},{6,5},{7,4},{8,11},{9,10},{10,... | collective-permute-start | bytes 1572872 | tf_op jit(solution)/shard_map/ppermute | solution.py:122
  71.4 42.0 %collective-permute-start.6 = (f32[32,4096]{1,0:T(8,128)}, f32[32,4096]{1,0:T(8,128)}, u32[]{:S(2)}, u32[]{:S(2)}) collective-permute-start(f32[32,4096]{1,0:T(8,128)} %get-tuple-element.59), channel_id=1, source_target_pairs={{0,1},{1,0},{2,3},{3,2},{4,5},{5,4},{6,7},{7,6},{8,9},{9,8},{10,11... | collective-permute-start | bytes 1572872 | tf_op jit(solution)/shard_map/ppermute | solution.py:122
  84.6 78.6 %collective-permute-start.9 = (f32[32,4096]{1,0:T(8,128)}, f32[32,4096]{1,0:T(8,128)S(1)}, u32[]{:S(2)}, u32[]{:S(2)}) collective-permute-start(f32[32,4096]{1,0:T(8,128)} %get-tuple-element.69), channel_id=1, source_target_pairs={{0,4},{1,5},{2,6},{3,7},{4,0},{5,1},{6,2},{7,3},{8,12},{9,13},{10,... | collective-permute-start | bytes 1572872 | tf_op jit(solution)/shard_map/ppermute | solution.py:122
  111.5 52.0 %collective-permute-start.10 = (f32[32,4096]{1,0:T(8,128)}, f32[32,4096]{1,0:T(8,128)S(1)}, u32[]{:S(2)}, u32[]{:S(2)}) collective-permute-start(f32[32,4096]{1,0:T(8,128)} %get-tuple-element.70), channel_id=1, source_target_pairs={{0,5},{1,4},{2,7},{3,6},{4,1},{5,0},{6,3},{7,2},{8,13},{9,12},{10,... | collective-permute-start | bytes 1572872 | tf_op jit(solution)/shard_map/ppermute | solution.py:122
  111.5 65.7 %collective-permute-start.11 = (f32[32,4096]{1,0:T(8,128)}, f32[32,4096]{1,0:T(8,128)S(1)}, u32[]{:S(2)}, u32[]{:S(2)}) collective-permute-start(f32[32,4096]{1,0:T(8,128)} %get-tuple-element.71), channel_id=1, source_target_pairs={{0,6},{1,7},{2,4},{3,5},{4,2},{5,3},{6,0},{7,1},{8,14},{9,15},{10,... | collective-permute-start | bytes 1572872 | tf_op jit(solution)/shard_map/ppermute | solution.py:122
  111.5 89.1 %collective-permute-start.12 = (f32[32,4096]{1,0:T(8,128)}, f32[32,4096]{1,0:T(8,128)S(1)}, u32[]{:S(2)}, u32[]{:S(2)}) collective-permute-start(f32[32,4096]{1,0:T(8,128)} %get-tuple-element.72), channel_id=1, source_target_pairs={{0,7},{1,6},{2,5},{3,4},{4,3},{5,2},{6,1},{7,0},{8,15},{9,14},{10,... | collective-permute-start | bytes 1572872 | tf_op jit(solution)/shard_map/ppermute | solution.py:122
  113.5 87.2 %collective-permute-start.13 = (f32[32,4096]{1,0:T(8,128)}, f32[32,4096]{1,0:T(8,128)}, u32[]{:S(2)}, u32[]{:S(2)}) collective-permute-start(f32[32,4096]{1,0:T(8,128)} %get-tuple-element.73), channel_id=1, source_target_pairs={{0,2},{1,3},{2,0},{3,1},{4,6},{5,7},{6,4},{7,5},{8,10},{9,11},{10,... | collective-permute-start | bytes 1572872 | tf_op jit(solution)/shard_map/ppermute | solution.py:122
  163.4 40.0 %collective-permute-start.15 = (f32[32,4096]{1,0:T(8,128)}, f32[32,4096]{1,0:T(8,128)}, u32[]{:S(2)}, u32[]{:S(2)}) collective-permute-start(f32[32,4096]{1,0:T(8,128)} %get-tuple-element.75), channel_id=1, source_target_pairs={{0,1},{1,0},{2,3},{3,2},{4,5},{5,4},{6,7},{7,6},{8,9},{9,8},{10,11... | collective-permute-start | bytes 1572872 | tf_op jit(solution)/shard_map/ppermute | solution.py:122
  178.0 73.0 %collective-permute-start.16 = (f32[32,4096]{1,0:T(8,128)}, f32[32,4096]{1,0:T(8,128)S(1)}, u32[]{:S(2)}, u32[]{:S(2)}) collective-permute-start(f32[32,4096]{1,0:T(8,128)} %get-tuple-element.79), channel_id=1, source_target_pairs={{0,4},{1,5},{2,6},{3,7},{4,0},{5,1},{6,2},{7,3},{8,12},{9,13},{10,... | collective-permute-start | bytes 1572872 | tf_op jit(solution)/shard_map/ppermute | solution.py:122
  200.6 54.7 %collective-permute-start.17 = (f32[32,4096]{1,0:T(8,128)}, f32[32,4096]{1,0:T(8,128)S(1)}, u32[]{:S(2)}, u32[]{:S(2)}) collective-permute-start(f32[32,4096]{1,0:T(8,128)} %get-tuple-element.80), channel_id=1, source_target_pairs={{0,5},{1,4},{2,7},{3,6},{4,1},{5,0},{6,3},{7,2},{8,13},{9,12},{10,... | collective-permute-start | bytes 1572872 | tf_op jit(solution)/shard_map/ppermute | solution.py:122
  201.4 65.7 %collective-permute-start.18 = (f32[32,4096]{1,0:T(8,128)}, f32[32,4096]{1,0:T(8,128)S(1)}, u32[]{:S(2)}, u32[]{:S(2)}) collective-permute-start(f32[32,4096]{1,0:T(8,128)} %get-tuple-element.81), channel_id=1, source_target_pairs={{0,6},{1,7},{2,4},{3,5},{4,2},{5,3},{6,0},{7,1},{8,14},{9,15},{10,... | collective-permute-start | bytes 1572872 | tf_op jit(solution)/shard_map/ppermute | solution.py:122
  203.2 90.0 %collective-permute-start.19 = (f32[32,4096]{1,0:T(8,128)}, f32[32,4096]{1,0:T(8,128)S(1)}, u32[]{:S(2)}, u32[]{:S(2)}) collective-permute-start(f32[32,4096]{1,0:T(8,128)} %get-tuple-element.82), channel_id=1, source_target_pairs={{0,7},{1,6},{2,5},{3,4},{4,3},{5,2},{6,1},{7,0},{8,15},{9,14},{10,... | collective-permute-start | bytes 1572872 | tf_op jit(solution)/shard_map/ppermute | solution.py:122
  245.7 47.5 %collective-permute-start.20 = (f32[32,4096]{1,0:T(8,128)S(1)}, f32[32,4096]{1,0:T(8,128)S(1)}, u32[]{:S(2)}, u32[]{:S(2)}) collective-permute-start(f32[32,4096]{1,0:T(8,128)S(1)} %copy-done.24), channel_id=1, source_target_pairs={{0,2},{1,3},{2,0},{3,1},{4,6},{5,7},{6,4},{7,5},{8,10},{9,11},{10,... | collective-permute-start | bytes 1572872 | tf_op jit(solution)/shard_map/ppermute | solution.py:122
  251.0 42.3 %collective-permute-start.21 = (f32[32,4096]{1,0:T(8,128)S(1)}, f32[32,4096]{1,0:T(8,128)S(1)}, u32[]{:S(2)}, u32[]{:S(2)}) collective-permute-start(f32[32,4096]{1,0:T(8,128)S(1)} %copy-done.23), channel_id=1, source_target_pairs={{0,3},{1,2},{2,1},{3,0},{4,7},{5,6},{6,5},{7,4},{8,11},{9,10},{10,... | collective-permute-start | bytes 1572872 | tf_op jit(solution)/shard_map/ppermute | solution.py:122
  267.1 71.4 %collective-permute-start.31 = (f32[32,4096]{1,0:T(8,128)}, f32[32,4096]{1,0:T(8,128)}, u32[]{:S(2)}, u32[]{:S(2)}) collective-permute-start(f32[32,4096]{1,0:T(8,128)} %get-tuple-element.92), channel_id=1, source_target_pairs={{0,4},{1,5},{2,6},{3,7},{4,0},{5,1},{6,2},{7,3},{8,12},{9,13},{10,... | collective-permute-start | bytes 1572872 | tf_op jit(solution)/shard_map/ppermute | solution.py:122
  293.2 47.9 %collective-permute-start.32 = (f32[32,4096]{1,0:T(8,128)}, f32[32,4096]{1,0:T(8,128)}, u32[]{:S(2)}, u32[]{:S(2)}) collective-permute-start(f32[32,4096]{1,0:T(8,128)} %get-tuple-element.93), channel_id=1, source_target_pairs={{0,5},{1,4},{2,7},{3,6},{4,1},{5,0},{6,3},{7,2},{8,13},{9,12},{10,... | collective-permute-start | bytes 1572872 | tf_op jit(solution)/shard_map/ppermute | solution.py:122
  306.7 53.0 %collective-permute-start.26 = (f32[32,4096]{1,0:T(8,128)}, f32[32,4096]{1,0:T(8,128)S(1)}, u32[]{:S(2)}, u32[]{:S(2)}) collective-permute-start(f32[32,4096]{1,0:T(8,128)} %get-tuple-element.86), channel_id=1, source_target_pairs={{0,2},{1,3},{2,0},{3,1},{4,6},{5,7},{6,4},{7,5},{8,10},{9,11},{10,... | collective-permute-start | bytes 1572872 | tf_op jit(solution)/shard_map/ppermute | solution.py:122
  (40 other events, 886.5 us)

commit v5 on v4

--- a/solution.py
+++ b/solution.py
@@ -526,7 +526,7 @@
         ids = jnp.concatenate([cells_of(plan, vel_at ^ step) for step, plan in groups])
         return settle(me, posts, groups, membership(ids), emit, earlier, particles.shape)
 
-    final = (near[0], far[2], *near[1:], *far[3:])
+    final = (*near[:2], far[2], *near[2:], *far[3:])
     first = [((step, inner), inner_back[step]) for step in steps]
     first += [((step, outer), outer_back[step]) for step in rest(final)]
     return wall([((step, outer), outer_back[step]) for step in final], wall(first, None))

time: 378 us -> 377 us (level)
  transfers between devices with their start and end apart: 33 -> 33, of which waited for: 17 -> 15; matrix products, arithmetic and copies ran while one was open for 1% -> 1% of each run, Pallas kernels for 28% -> 28%
where the time goes in v5:
time: 377 us; the launch traced here: 375 us
  waiting for transfers between devices  178 us (47%)
  Pallas kernels  111 us (29%)
  starting transfers between devices  62.6 us (17%)
  local copies, waits for them, and re-layouts  14.1 us (4%)
  blocking collectives  6.19 us (2%)
    ppermute x31, waiting for transfers between devices, swap(): lax.ppermute(values, axis, [(i, i ^ step) for i in range(lax.axis_size(ax...  178 us
    pallas_call x2, Pallas kernels, collide(): pl.pallas_call(functools.partial(collide_kernel, steps), grid=(cells // s...  84.2 us
    ppermute x31, starting transfers between devices, swap(): lax.ppermute(values, axis, [(i, i ^ step) for i in range(lax.axis_size(ax...  57 us
    pallas_call x4, Pallas kernels, move(): pl.pallas_call(functools.partial(move_kernel, order, offset, low_groups,...  14.6 us
    unnamed x63, local copies, waits for them, and re-layouts  11.9 us
  transfers between devices with their start and end apart: 33, of which 15 were waited for; matrix products, arithmetic and copies ran while one was open for 1% of the time, Pallas kernels for 28%

profile of v5, /device:TPU:18, one launch (start us, length us, event | category | flops | bytes accessed | tf_op | source)
XLA Modules:
  0.0 375.1 jit_solution(6235536680119210963)
XLA Ops:
  2.6 4.6 %shard_map.137 = (f32[32,4096]{1,0:T(8,128)}, f32[32,4096]{1,0:T(8,128)}, f32[32,4096]{1,0:T(8,128)}, f32[32,4096]{1,0:T(8,128)}, f32[32,4096]{1,0:T(8,128)}, /*...) custom-call(s32[1]{0:T(128)} %bitcast.me, f32[512,4096]{1,0:T(8,128)} %particles.7, ...), custom_call_target="tpu_custom_call" | custom-call | flops 4587520 | bytes 9175040 | tf_op jit(solution)/shard_map/pallas_call | solution.py:204
  9.1 3.6 collective-permute-start.8
  18.5 30.5 %collective-permute-done.rest_0_ = f32[32,4096]{1,0:T(8,128)S(1)} collective-permute-done((f32[32,4096]{1,0:T(8,128)}, f32[32,4096]{1,0:T(8,128)S(1)}, u32[]{:S(2)}, u32[]{:S(2)}) %collective-permute-start) | collective-permute-done | bytes 524320 | tf_op jit(solution)/shard_map/ppermute | solution.py:122
  54.7 16.8 %collective-permute-done.1.rest_1_ = f32[32,4096]{1,0:T(8,128)S(1)} collective-permute-done((f32[32,4096]{1,0:T(8,128)}, f32[32,4096]{1,0:T(8,128)S(1)}, u32[]{:S(2)}, u32[]{:S(2)}) %collective-permute-start.1) | collective-permute-done | bytes 524320 | tf_op jit(solution)/shard_map/ppermute | solution.py:122
  75.0 4.5 %shard_map.138 = (f32[256,640]{1,0:T(8,128)}, f32[256,640]{1,0:T(8,128)}) custom-call(f32[32,1024]{1,0:T(8,128)} %reshape.106.gain, f32[32,1024]{1,0:T(8,128)} %reshape.107.freq, bf16[2,1024,640]{2,1,0:T(8,128)(2,1)} %constant.140.clone.pick), custom_call_target="tpu_custom_call" | custom-call | flops 1006632960 | bytes 2621440 | tf_op jit(solution)/shard_map/pallas_call | solution.py:106
  79.5 4.2 %shard_map.140 = (f32[32,4096]{1,0:T(8,128)}, f32[32,4096]{1,0:T(8,128)}, f32[32,4096]{1,0:T(8,128)}, f32[32,4096]{1,0:T(8,128)}, f32[32,4096]{1,0:T(8,128)}) custom-call(s32[1]{0:T(128)} %bitcast.me, f32[512,4096]{1,0:T(8,128)} %particles.7, f32[8,4096]{1,0:T(8,128)} %copy-done.14, f32[8,4096]{1,0:T(8,128)} %copy-done.15), custom_call_target="tpu_custom_call" | custom-call | flops 3276800 | bytes 6553600 | tf_op jit(solution)/shard_map/pallas_call | solution.py:204
  87.0 23.7 %collective-permute-done.3.rest_3_ = f32[32,4096]{1,0:T(8,128)S(1)} collective-permute-done((f32[32,4096]{1,0:T(8,128)}, f32[32,4096]{1,0:T(8,128)S(1)}, u32[]{:S(2)}, u32[]{:S(2)}) %collective-permute-start.3) | collective-permute-done | bytes 524320 | tf_op jit(solution)/shard_map/ppermute | solution.py:122
  113.5 4.1 %collective-permute-start.13 = (f32[32,4096]{1,0:T(8,128)}, f32[32,4096]{1,0:T(8,128)}, u32[]{:S(2)}, u32[]{:S(2)}) collective-permute-start(f32[32,4096]{1,0:T(8,128)} %get-tuple-element.73), channel_id=1, source_target_pairs={{0,2},{1,3},{2,0},{3,1},{4,6},{5,7},{6,4},{7,5},{8,10},{9,11},{10,... | collective-permute-start | bytes 1572872 | tf_op jit(solution)/shard_map/ppermute | solution.py:122
  117.5 42.0 %shard_map.139 = (f32[32,4096]{1,0:T(8,128)}, f32[32,4096]{1,0:T(8,128)}, f32[32,4096]{1,0:T(8,128)}, f32[32,4096]{1,0:T(8,128)}, f32[32,4096]{1,0:T(8,128)}, /*...) custom-call(s32[1]{0:T(128)} %bitcast.me, f32[32,4096]{1,0:T(8,128)} %copy-done.19, ...), custom_call_target="tpu_custom_call" | custom-call | flops 43486543872 | bytes 8388608 | tf_op jit(solution)/shard_map/pallas_call | solution.py:332
  159.5 3.7 shard_map.141
  165.3 11.9 %collective-permute-done.11.rest_2_ = f32[32,4096]{1,0:T(8,128)S(1)} collective-permute-done((f32[32,4096]{1,0:T(8,128)}, f32[32,4096]{1,0:T(8,128)S(1)}, u32[]{:S(2)}, u32[]{:S(2)}) %collective-permute-start.11) | collective-permute-done | bytes 524320 | tf_op jit(solution)/shard_map/ppermute | solution.py:122
  178.0 22.6 %collective-permute-done.12.rest_3_ = f32[32,4096]{1,0:T(8,128)S(1)} collective-permute-done((f32[32,4096]{1,0:T(8,128)}, f32[32,4096]{1,0:T(8,128)S(1)}, u32[]{:S(2)}, u32[]{:S(2)}) %collective-permute-start.12) | collective-permute-done | bytes 524320 | tf_op jit(solution)/shard_map/ppermute | solution.py:122
  203.4 42.3 %shard_map.142 = (f32[32,4096]{1,0:T(8,128)}, f32[32,4096]{1,0:T(8,128)}, f32[32,4096]{1,0:T(8,128)}, f32[32,4096]{1,0:T(8,128)}, f32[32,4096]{1,0:T(8,128)}, /*...) custom-call(s32[1]{0:T(128)} %bitcast.me, f32[32,4096]{1,0:T(8,128)} %copy-done.25, ...), custom_call_target="tpu_custom_call" | custom-call | flops 43486543872 | bytes 8388608 | tf_op jit(solution)/shard_map/pallas_call | solution.py:332
  245.7 5.3 %collective-permute-start.20 = (f32[32,4096]{1,0:T(8,128)S(1)}, f32[32,4096]{1,0:T(8,128)S(1)}, u32[]{:S(2)}, u32[]{:S(2)}) collective-permute-start(f32[32,4096]{1,0:T(8,128)S(1)} %copy-done.24), channel_id=1, source_target_pairs={{0,2},{1,3},{2,0},{3,1},{4,6},{5,7},{6,4},{7,5},{8,10},{9,11},{10,... | collective-permute-start | bytes 1572872 | tf_op jit(solution)/shard_map/ppermute | solution.py:122
  251.1 4.2 %collective-permute-done.17.refs_5_.rest_1_ = f32[32,4096]{1,0:T(8,128)S(1)} collective-permute-done((f32[32,4096]{1,0:T(8,128)}, f32[32,4096]{1,0:T(8,128)S(1)}, u32[]{:S(2)}, u32[]{:S(2)}) %collective-permute-start.17) | collective-permute-done | bytes 524320 | tf_op jit(solution)/shard_map/ppermute | solution.py:122
  257.0 10.1 %collective-permute-done.18.refs_6_.rest_2_ = f32[32,4096]{1,0:T(8,128)S(1)} collective-permute-done((f32[32,4096]{1,0:T(8,128)}, f32[32,4096]{1,0:T(8,128)S(1)}, u32[]{:S(2)}, u32[]{:S(2)}) %collective-permute-start.18) | collective-permute-done | bytes 524320 | tf_op jit(solution)/shard_map/ppermute | solution.py:122
  267.1 26.1 %collective-permute-done.19.refs_7_.rest_3_ = f32[32,4096]{1,0:T(8,128)S(1)} collective-permute-done((f32[32,4096]{1,0:T(8,128)}, f32[32,4096]{1,0:T(8,128)S(1)}, u32[]{:S(2)}, u32[]{:S(2)}) %collective-permute-start.19) | collective-permute-done | bytes 524320 | tf_op jit(solution)/shard_map/ppermute | solution.py:122
  295.7 6.2 %psum.7 = f32[1,32]{1,0:T(1,128)S(1)} all-reduce(f32[1,32]{1,0:T(1,128)} %shard_map.143), channel_id=1, replica_groups=mesh['space'=4,'vel'=8] {'space'}, use_global_device_ids=true, to_apply=%region_3.4 | all-reduce | flops 32 | bytes 256 | tf_op jit(solution)/shard_map/psum | solution.py:503
  309.1 15.1 %collective-permute-start.25 = (f32[1,32]{1,0:T(1,128)S(1)}, f32[1,32]{1,0:T(1,128)S(1)}, u32[]{:S(2)}, u32[]{:S(2)}) collective-permute-start(f32[1,32]{1,0:T(1,128)S(1)} %add.346), channel_id=1, source_target_pairs={{0,4},{1,5},{2,6},{3,7},{4,0},{5,1},{6,2},{7,3},{8,12},{9,13},{10,... | collective-permute-start | bytes 392 | tf_op jit(solution)/shard_map/ppermute | solution.py:122
  324.2 4.2 %collective-permute-start.27 = (f32[32,4096]{1,0:T(8,128)}, f32[32,4096]{1,0:T(8,128)S(1)}, u32[]{:S(2)}, u32[]{:S(2)}) collective-permute-start(f32[32,4096]{1,0:T(8,128)} %get-tuple-element.87), channel_id=1, source_target_pairs={{0,3},{1,2},{2,1},{3,0},{4,7},{5,6},{6,5},{7,4},{8,11},{9,10},{10,... | collective-permute-start | bytes 1572872 | tf_op jit(solution)/shard_map/ppermute | solution.py:122
  328.5 3.6 collective-permute-start.29
  340.7 4.0 %shard_map.144.rest_5_ = f32[512,4096]{1,0:T(8,128)} custom-call(s32[1]{0:T(128)} %bitcast.me, f32[352,32]{1,0:T(8,128)S(1)} %copy.25.member, bf16[64,4096]{1,0:T(8,128)(2,1)S(1)} %pad_maximum_fusion.emit, f32[32,4096]{1,0:T(8,128)S(1)} %copy-done.1, f32[32,4096]{1,0:T(8,128)S(1)} %copy-done.3, f32[32,4096]{1,0:T(8,128)S(1)} %copy-done.5, ...), custom_call_target="tpu_custom_call" | custom-call | flops 184549376 | bytes 11534336 | tf_op jit(solution)/shard_map/pallas_call | solution.py:414
  344.7 15.1 %collective-permute-done.26.rest_0_ = f32[32,4096]{1,0:T(8,128)S(1)} collective-permute-done((f32[32,4096]{1,0:T(8,128)}, f32[32,4096]{1,0:T(8,128)S(1)}, u32[]{:S(2)}, u32[]{:S(2)}) %collective-permute-start.26) | collective-permute-done | bytes 524320 | tf_op jit(solution)/shard_map/ppermute | solution.py:122
  359.8 9.3 %collective-permute-done.27.rest_1_ = f32[32,4096]{1,0:T(8,128)S(1)} collective-permute-done((f32[32,4096]{1,0:T(8,128)}, f32[32,4096]{1,0:T(8,128)S(1)}, u32[]{:S(2)}, u32[]{:S(2)}) %collective-permute-start.27) | collective-permute-done | bytes 524320 | tf_op jit(solution)/shard_map/ppermute | solution.py:122
  (148 shorter events, 56.9 us)
Async XLA Ops:
  2.2 46.7 %collective-permute-start = (f32[32,4096]{1,0:T(8,128)}, f32[32,4096]{1,0:T(8,128)S(1)}, u32[]{:S(2)}, u32[]{:S(2)}) collective-permute-start(f32[32,4096]{1,0:T(8,128)} %shard_map.136.rest_0_), channel_id=1, source_target_pairs={{0,4},{1,5},{2,6},{3,7},{4,0},{5,1},{6,2},{7,3},{8,12},{9,13},{10,... | collective-permute-start | bytes 1572872 | tf_op jit(solution)/shard_map/ppermute | solution.py:122
  7.2 44.2 %collective-permute-start.7 = (f32[8,4096]{1,0:T(8,128)}, f32[8,4096]{1,0:T(8,128)S(1)}, u32[]{:S(2)}, u32[]{:S(2)}) collective-permute-start(f32[8,4096]{1,0:T(8,128)} %get-tuple-element.67), channel_id=1, source_target_pairs={{0,8},{8,16},{16,24},{1,9},{9,17},{17,25},{2,10},{10,18},{18,26},{... | collective-permute-start | bytes 393224 | tf_op jit(solution)/shard_map/ppermute | solution.py:471
  9.1 45.5 %collective-permute-start.8 = (f32[8,4096]{1,0:T(8,128)}, f32[8,4096]{1,0:T(8,128)S(1)}, u32[]{:S(2)}, u32[]{:S(2)}) collective-permute-start(f32[8,4096]{1,0:T(8,128)} %get-tuple-element.68), channel_id=1, source_target_pairs={{8,0},{16,8},{24,16},{9,1},{17,9},{25,17},{10,2},{18,10},{26,18},{... | collective-permute-start | bytes 393224 | tf_op jit(solution)/shard_map/ppermute | solution.py:472
  12.8 58.7 %collective-permute-start.1 = (f32[32,4096]{1,0:T(8,128)}, f32[32,4096]{1,0:T(8,128)S(1)}, u32[]{:S(2)}, u32[]{:S(2)}) collective-permute-start(f32[32,4096]{1,0:T(8,128)} %get-tuple-element.54), channel_id=1, source_target_pairs={{0,5},{1,4},{2,7},{3,6},{4,1},{5,0},{6,3},{7,2},{8,13},{9,12},{10,... | collective-permute-start | bytes 1572872 | tf_op jit(solution)/shard_map/ppermute | solution.py:122
  16.4 68.2 %collective-permute-start.2 = (f32[32,4096]{1,0:T(8,128)}, f32[32,4096]{1,0:T(8,128)S(1)}, u32[]{:S(2)}, u32[]{:S(2)}) collective-permute-start(f32[32,4096]{1,0:T(8,128)} %get-tuple-element.55), channel_id=1, source_target_pairs={{0,6},{1,7},{2,4},{3,5},{4,2},{5,3},{6,0},{7,1},{8,14},{9,15},{10,... | collective-permute-start | bytes 1572872 | tf_op jit(solution)/shard_map/ppermute | solution.py:122
  48.9 61.7 %collective-permute-start.3 = (f32[32,4096]{1,0:T(8,128)}, f32[32,4096]{1,0:T(8,128)S(1)}, u32[]{:S(2)}, u32[]{:S(2)}) collective-permute-start(f32[32,4096]{1,0:T(8,128)} %get-tuple-element.56), channel_id=1, source_target_pairs={{0,7},{1,6},{2,5},{3,4},{4,3},{5,2},{6,1},{7,0},{8,15},{9,14},{10,... | collective-permute-start | bytes 1572872 | tf_op jit(solution)/shard_map/ppermute | solution.py:122
  51.5 60.0 %collective-permute-start.4 = (f32[32,4096]{1,0:T(8,128)}, f32[32,4096]{1,0:T(8,128)}, u32[]{:S(2)}, u32[]{:S(2)}) collective-permute-start(f32[32,4096]{1,0:T(8,128)} %get-tuple-element.57), channel_id=1, source_target_pairs={{0,2},{1,3},{2,0},{3,1},{4,6},{5,7},{6,4},{7,5},{8,10},{9,11},{10,... | collective-permute-start | bytes 1572872 | tf_op jit(solution)/shard_map/ppermute | solution.py:122
  54.6 56.8 %collective-permute-start.5 = (f32[32,4096]{1,0:T(8,128)}, f32[32,4096]{1,0:T(8,128)}, u32[]{:S(2)}, u32[]{:S(2)}) collective-permute-start(f32[32,4096]{1,0:T(8,128)} %get-tuple-element.58), channel_id=1, source_target_pairs={{0,3},{1,2},{2,1},{3,0},{4,7},{5,6},{6,5},{7,4},{8,11},{9,10},{10,... | collective-permute-start | bytes 1572872 | tf_op jit(solution)/shard_map/ppermute | solution.py:122
  71.4 42.0 %collective-permute-start.6 = (f32[32,4096]{1,0:T(8,128)}, f32[32,4096]{1,0:T(8,128)}, u32[]{:S(2)}, u32[]{:S(2)}) collective-permute-start(f32[32,4096]{1,0:T(8,128)} %get-tuple-element.59), channel_id=1, source_target_pairs={{0,1},{1,0},{2,3},{3,2},{4,5},{5,4},{6,7},{7,6},{8,9},{9,8},{10,11... | collective-permute-start | bytes 1572872 | tf_op jit(solution)/shard_map/ppermute | solution.py:122
  84.6 78.6 %collective-permute-start.9 = (f32[32,4096]{1,0:T(8,128)}, f32[32,4096]{1,0:T(8,128)S(1)}, u32[]{:S(2)}, u32[]{:S(2)}) collective-permute-start(f32[32,4096]{1,0:T(8,128)} %get-tuple-element.69), channel_id=1, source_target_pairs={{0,4},{1,5},{2,6},{3,7},{4,0},{5,1},{6,2},{7,3},{8,12},{9,13},{10,... | collective-permute-start | bytes 1572872 | tf_op jit(solution)/shard_map/ppermute | solution.py:122
  111.5 52.0 %collective-permute-start.10 = (f32[32,4096]{1,0:T(8,128)}, f32[32,4096]{1,0:T(8,128)S(1)}, u32[]{:S(2)}, u32[]{:S(2)}) collective-permute-start(f32[32,4096]{1,0:T(8,128)} %get-tuple-element.70), channel_id=1, source_target_pairs={{0,5},{1,4},{2,7},{3,6},{4,1},{5,0},{6,3},{7,2},{8,13},{9,12},{10,... | collective-permute-start | bytes 1572872 | tf_op jit(solution)/shard_map/ppermute | solution.py:122
  111.5 65.7 %collective-permute-start.11 = (f32[32,4096]{1,0:T(8,128)}, f32[32,4096]{1,0:T(8,128)S(1)}, u32[]{:S(2)}, u32[]{:S(2)}) collective-permute-start(f32[32,4096]{1,0:T(8,128)} %get-tuple-element.71), channel_id=1, source_target_pairs={{0,6},{1,7},{2,4},{3,5},{4,2},{5,3},{6,0},{7,1},{8,14},{9,15},{10,... | collective-permute-start | bytes 1572872 | tf_op jit(solution)/shard_map/ppermute | solution.py:122
  111.5 89.1 %collective-permute-start.12 = (f32[32,4096]{1,0:T(8,128)}, f32[32,4096]{1,0:T(8,128)S(1)}, u32[]{:S(2)}, u32[]{:S(2)}) collective-permute-start(f32[32,4096]{1,0:T(8,128)} %get-tuple-element.72), channel_id=1, source_target_pairs={{0,7},{1,6},{2,5},{3,4},{4,3},{5,2},{6,1},{7,0},{8,15},{9,14},{10,... | collective-permute-start | bytes 1572872 | tf_op jit(solution)/shard_map/ppermute | solution.py:122
  113.5 87.2 %collective-permute-start.13 = (f32[32,4096]{1,0:T(8,128)}, f32[32,4096]{1,0:T(8,128)}, u32[]{:S(2)}, u32[]{:S(2)}) collective-permute-start(f32[32,4096]{1,0:T(8,128)} %get-tuple-element.73), channel_id=1, source_target_pairs={{0,2},{1,3},{2,0},{3,1},{4,6},{5,7},{6,4},{7,5},{8,10},{9,11},{10,... | collective-permute-start | bytes 1572872 | tf_op jit(solution)/shard_map/ppermute | solution.py:122
  178.0 73.0 %collective-permute-start.16 = (f32[32,4096]{1,0:T(8,128)}, f32[32,4096]{1,0:T(8,128)S(1)}, u32[]{:S(2)}, u32[]{:S(2)}) collective-permute-start(f32[32,4096]{1,0:T(8,128)} %get-tuple-element.79), channel_id=1, source_target_pairs={{0,4},{1,5},{2,6},{3,7},{4,0},{5,1},{6,2},{7,3},{8,12},{9,13},{10,... | collective-permute-start | bytes 1572872 | tf_op jit(solution)/shard_map/ppermute | solution.py:122
  200.6 54.7 %collective-permute-start.17 = (f32[32,4096]{1,0:T(8,128)}, f32[32,4096]{1,0:T(8,128)S(1)}, u32[]{:S(2)}, u32[]{:S(2)}) collective-permute-start(f32[32,4096]{1,0:T(8,128)} %get-tuple-element.80), channel_id=1, source_target_pairs={{0,5},{1,4},{2,7},{3,6},{4,1},{5,0},{6,3},{7,2},{8,13},{9,12},{10,... | collective-permute-start | bytes 1572872 | tf_op jit(solution)/shard_map/ppermute | solution.py:122
  201.4 65.7 %collective-permute-start.18 = (f32[32,4096]{1,0:T(8,128)}, f32[32,4096]{1,0:T(8,128)S(1)}, u32[]{:S(2)}, u32[]{:S(2)}) collective-permute-start(f32[32,4096]{1,0:T(8,128)} %get-tuple-element.81), channel_id=1, source_target_pairs={{0,6},{1,7},{2,4},{3,5},{4,2},{5,3},{6,0},{7,1},{8,14},{9,15},{10,... | collective-permute-start | bytes 1572872 | tf_op jit(solution)/shard_map/ppermute | solution.py:122
  203.2 90.0 %collective-permute-start.19 = (f32[32,4096]{1,0:T(8,128)}, f32[32,4096]{1,0:T(8,128)S(1)}, u32[]{:S(2)}, u32[]{:S(2)}) collective-permute-start(f32[32,4096]{1,0:T(8,128)} %get-tuple-element.82), channel_id=1, source_target_pairs={{0,7},{1,6},{2,5},{3,4},{4,3},{5,2},{6,1},{7,0},{8,15},{9,14},{10,... | collective-permute-start | bytes 1572872 | tf_op jit(solution)/shard_map/ppermute | solution.py:122
  245.7 47.5 %collective-permute-start.20 = (f32[32,4096]{1,0:T(8,128)S(1)}, f32[32,4096]{1,0:T(8,128)S(1)}, u32[]{:S(2)}, u32[]{:S(2)}) collective-permute-start(f32[32,4096]{1,0:T(8,128)S(1)} %copy-done.24), channel_id=1, source_target_pairs={{0,2},{1,3},{2,0},{3,1},{4,6},{5,7},{6,4},{7,5},{8,10},{9,11},{10,... | collective-permute-start | bytes 1572872 | tf_op jit(solution)/shard_map/ppermute | solution.py:122
  251.0 42.3 %collective-permute-start.21 = (f32[32,4096]{1,0:T(8,128)S(1)}, f32[32,4096]{1,0:T(8,128)S(1)}, u32[]{:S(2)}, u32[]{:S(2)}) collective-permute-start(f32[32,4096]{1,0:T(8,128)S(1)} %copy-done.23), channel_id=1, source_target_pairs={{0,3},{1,2},{2,1},{3,0},{4,7},{5,6},{6,5},{7,4},{8,11},{9,10},{10,... | collective-permute-start | bytes 1572872 | tf_op jit(solution)/shard_map/ppermute | solution.py:122
  267.1 61.3 %collective-permute-start.31 = (f32[32,4096]{1,0:T(8,128)}, f32[32,4096]{1,0:T(8,128)}, u32[]{:S(2)}, u32[]{:S(2)}) collective-permute-start(f32[32,4096]{1,0:T(8,128)} %get-tuple-element.92), channel_id=1, source_target_pairs={{0,4},{1,5},{2,6},{3,7},{4,0},{5,1},{6,2},{7,3},{8,12},{9,13},{10,... | collective-permute-start | bytes 1572872 | tf_op jit(solution)/shard_map/ppermute | solution.py:122
  306.7 53.0 %collective-permute-start.26 = (f32[32,4096]{1,0:T(8,128)}, f32[32,4096]{1,0:T(8,128)S(1)}, u32[]{:S(2)}, u32[]{:S(2)}) collective-permute-start(f32[32,4096]{1,0:T(8,128)} %get-tuple-element.86), channel_id=1, source_target_pairs={{0,2},{1,3},{2,0},{3,1},{4,6},{5,7},{6,4},{7,5},{8,10},{9,11},{10,... | collective-permute-start | bytes 1572872 | tf_op jit(solution)/shard_map/ppermute | solution.py:122
  324.2 44.9 %collective-permute-start.27 = (f32[32,4096]{1,0:T(8,128)}, f32[32,4096]{1,0:T(8,128)S(1)}, u32[]{:S(2)}, u32[]{:S(2)}) collective-permute-start(f32[32,4096]{1,0:T(8,128)} %get-tuple-element.87), channel_id=1, source_target_pairs={{0,3},{1,2},{2,1},{3,0},{4,7},{5,6},{6,5},{7,4},{8,11},{9,10},{10,... | collective-permute-start | bytes 1572872 | tf_op jit(solution)/shard_map/ppermute | solution.py:122
  328.4 40.7 %collective-permute-start.28 = (f32[32,4096]{1,0:T(8,128)}, f32[32,4096]{1,0:T(8,128)S(1)}, u32[]{:S(2)}, u32[]{:S(2)}) collective-permute-start(f32[32,4096]{1,0:T(8,128)} %get-tuple-element.88), channel_id=1, source_target_pairs={{0,6},{1,7},{2,4},{3,5},{4,2},{5,3},{6,0},{7,1},{8,14},{9,15},{10,... | collective-permute-start | bytes 1572872 | tf_op jit(solution)/shard_map/ppermute | solution.py:122
  (40 other events, 902.6 us)

commit v6 on v5

--- a/solution.py
+++ b/solution.py
@@ -206,7 +206,7 @@
         in_specs=[local(pltpu.SMEM), local(pltpu.HBM)]
         + [local(pltpu.VMEM)] * len(halo)
         + [local(pltpu.HBM)] * len(after),
-        out_specs=[local(pltpu.HBM)] * (count + 2 * edges),
+        out_specs=[local(pl.ANY)] * (count + 2 * edges),
         out_shape=[shape] * count + [rim] * (2 * edges),
         scratch_shapes=[
             pltpu.VMEM((count, span, width), jnp.float32),
@@ -215,7 +215,7 @@
             pltpu.SemaphoreType.DMA((count + 2,)),
             pltpu.SemaphoreType.DMA((count + 2,)),
         ],
-        compiler_params=pltpu.CompilerParams(vmem_limit_bytes=vmem_bytes),
+        compiler_params=pltpu.CompilerParams(vmem_limit_bytes=4 * count * (span + cells) * width + 6 * 2**20),
         cost_estimate=pl.CostEstimate(flops=5 * size, bytes_accessed=10 * size, transcendentals=0),
     )(me, particles, *halo, *after)
 
@@ -448,7 +448,7 @@
     inner, outer = (quarter, vel_count, 0), (0, vel_count // 2, half)
     far, near = partners(vel_count)
     steps = (*far, *near, 0)
-    urgent, ready = far[:1], (*far, *near[:1])
+    urgent, ready = far[:1], (*far, *near[:2])
 
     def send(arrays):
         return {step: swap(array, "vel", step) if step else array for step, array in arrays.items()}

time: 377 us -> 379 us (level)
  waiting for transfers between devices: 178 us -> 160 us
  local copies, waits for them, and re-layouts: 14.1 us -> 30.8 us
  Pallas kernels: 111 us -> 103 us
  starting transfers between devices: 62.6 us -> 67.8 us
  other arithmetic: 2.37 us -> 6.69 us
    ppermute x31, waiting for transfers between devices: 178 us -> 160 us  [swap(): lax.ppermute(values, axis, [(i, i ^ step) for i in range(lax.axis_size(ax...]
    unnamed x63 -> x65, local copies, waits for them, and re-layouts: 11.9 us -> 25.3 us
    pallas_call x4, Pallas kernels: 14.6 us -> 6.97 us  [move(): pl.pallas_call(functools.partial(move_kernel, order, offset, low_groups,...]
    ppermute x31, starting transfers between devices: 57 us -> 62.1 us  [swap(): lax.ppermute(values, axis, [(i, i ^ step) for i in range(lax.axis_size(ax...]
  transfers between devices with their start and end apart: 33 -> 33, of which waited for: 15 -> 13; matrix products, arithmetic and copies ran while one was open for 1% -> 3% of each run, Pallas kernels for 28% -> 27%
where the time goes in v6:
time: 379 us; the launch traced here: 376 us
  waiting for transfers between devices  160 us (42%)
  Pallas kernels  103 us (27%)
  starting transfers between devices  67.8 us (18%)
  local copies, waits for them, and re-layouts  30.8 us (8%)
  other arithmetic  6.69 us (2%)
  blocking collectives  6.67 us (2%)
    ppermute x31, waiting for transfers between devices, swap(): lax.ppermute(values, axis, [(i, i ^ step) for i in range(lax.axis_size(ax...  160 us
    pallas_call x2, Pallas kernels, collide(): pl.pallas_call(functools.partial(collide_kernel, steps), grid=(cells // s...  84.3 us
    ppermute x31, starting transfers between devices, swap(): lax.ppermute(values, axis, [(i, i ^ step) for i in range(lax.axis_size(ax...  62.1 us
    unnamed x65, local copies, waits for them, and re-layouts  25.3 us
  transfers between devices with their start and end apart: 33, of which 13 were waited for; matrix products, arithmetic and copies ran while one was open for 3% of the time, Pallas kernels for 27%

profile of v6, /device:TPU:18, one launch (start us, length us, event | category | flops | bytes accessed | tf_op | source)
XLA Modules:
  0.0 376.3 jit_solution(8531597877324306476)
XLA Ops:
  0.0 3.4 copy-done
  12.8 3.8 %collective-permute-start.8 = (f32[8,4096]{1,0:T(8,128)S(1)}, f32[8,4096]{1,0:T(8,128)S(1)}, u32[]{:S(2)}, u32[]{:S(2)}) collective-permute-start(f32[8,4096]{1,0:T(8,128)S(1)} %get-tuple-element.68), channel_id=1, source_target_pairs={{8,0},{16,8},{24,16},{9,1},{17,9},{25,17},{10,2},{18,10},{26,18},{... | collective-permute-start | bytes 393224 | tf_op jit(solution)/shard_map/ppermute | solution.py:472
  27.9 22.3 %collective-permute-done.rest_0_ = f32[32,4096]{1,0:T(8,128)} collective-permute-done((f32[32,4096]{1,0:T(8,128)S(1)}, f32[32,4096]{1,0:T(8,128)}, u32[]{:S(2)}, u32[]{:S(2)}) %collective-permute-start) | collective-permute-done | bytes 524320 | tf_op jit(solution)/shard_map/ppermute | solution.py:122
  52.7 3.4 collective-permute-start.4
  56.1 16.7 %collective-permute-done.1.rest_1_ = f32[32,4096]{1,0:T(8,128)} collective-permute-done((f32[32,4096]{1,0:T(8,128)}, f32[32,4096]{1,0:T(8,128)}, u32[]{:S(2)}, u32[]{:S(2)}) %collective-permute-start.1) | collective-permute-done | bytes 524320 | tf_op jit(solution)/shard_map/ppermute | solution.py:122
  79.0 4.5 %shard_map.138 = (f32[256,640]{1,0:T(8,128)}, f32[256,640]{1,0:T(8,128)}) custom-call(f32[32,1024]{1,0:T(8,128)} %reshape.106.gain, f32[32,1024]{1,0:T(8,128)} %reshape.107.freq, bf16[2,1024,640]{2,1,0:T(8,128)(2,1)} %constant.140.clone.pick), custom_call_target="tpu_custom_call" | custom-call | flops 1006632960 | bytes 2621440 | tf_op jit(solution)/shard_map/pallas_call | solution.py:106
  83.5 3.4 copy-done.2
  89.6 3.4 collective-permute-start.9
  93.0 19.0 %collective-permute-done.3.rest_3_ = f32[32,4096]{1,0:T(8,128)} collective-permute-done((f32[32,4096]{1,0:T(8,128)S(1)}, f32[32,4096]{1,0:T(8,128)}, u32[]{:S(2)}, u32[]{:S(2)}) %collective-permute-start.3) | collective-permute-done | bytes 524320 | tf_op jit(solution)/shard_map/ppermute | solution.py:122
  114.1 6.2 %collective-permute-start.13 = (f32[32,4096]{1,0:T(8,128)}, f32[32,4096]{1,0:T(8,128)}, u32[]{:S(2)}, u32[]{:S(2)}) collective-permute-start(f32[32,4096]{1,0:T(8,128)} %get-tuple-element.73), channel_id=1, source_target_pairs={{0,2},{1,3},{2,0},{3,1},{4,6},{5,7},{6,4},{7,5},{8,10},{9,11},{10,... | collective-permute-start | bytes 1572872 | tf_op jit(solution)/shard_map/ppermute | solution.py:122
  120.2 41.9 %shard_map.139 = (f32[32,4096]{1,0:T(8,128)}, f32[32,4096]{1,0:T(8,128)}, f32[32,4096]{1,0:T(8,128)}, f32[32,4096]{1,0:T(8,128)}, f32[32,4096]{1,0:T(8,128)}, /*...) custom-call(s32[1]{0:T(128)} %bitcast.me, ...), custom_call_target="tpu_custom_call" | custom-call | flops 43486543872 | bytes 8388608 | tf_op jit(solution)/shard_map/pallas_call | solution.py:332
  162.2 3.4 copy-done.3
  169.6 8.8 %collective-permute-done.11.rest_2_ = f32[32,4096]{1,0:T(8,128)} collective-permute-done((f32[32,4096]{1,0:T(8,128)S(1)}, f32[32,4096]{1,0:T(8,128)}, u32[]{:S(2)}, u32[]{:S(2)}) %collective-permute-start.11) | collective-permute-done | bytes 524320 | tf_op jit(solution)/shard_map/ppermute | solution.py:122
  178.5 23.7 %collective-permute-done.12.rest_3_ = f32[32,4096]{1,0:T(8,128)} collective-permute-done((f32[32,4096]{1,0:T(8,128)}, f32[32,4096]{1,0:T(8,128)}, u32[]{:S(2)}, u32[]{:S(2)}) %collective-permute-start.12) | collective-permute-done | bytes 524320 | tf_op jit(solution)/shard_map/ppermute | solution.py:122
  204.9 42.4 %shard_map.142 = (f32[32,4096]{1,0:T(8,128)}, f32[32,4096]{1,0:T(8,128)}, f32[32,4096]{1,0:T(8,128)}, f32[32,4096]{1,0:T(8,128)}, f32[32,4096]{1,0:T(8,128)}, /*...) custom-call(s32[1]{0:T(128)} %bitcast.me, f32[32,4096]{1,0:T(8,128)} %copy-done.29, ...), custom_call_target="tpu_custom_call" | custom-call | flops 43486543872 | bytes 8388608 | tf_op jit(solution)/shard_map/pallas_call | solution.py:332
  247.2 6.1 %collective-permute-start.20 = (f32[32,4096]{1,0:T(8,128)S(1)}, f32[32,4096]{1,0:T(8,128)S(1)}, u32[]{:S(2)}, u32[]{:S(2)}) collective-permute-start(f32[32,4096]{1,0:T(8,128)S(1)} %copy-done.28), channel_id=1, source_target_pairs={{0,2},{1,3},{2,0},{3,1},{4,6},{5,7},{6,4},{7,5},{8,10},{9,11},{10,... | collective-permute-start | bytes 1572872 | tf_op jit(solution)/shard_map/ppermute | solution.py:122
  253.4 4.1 %collective-permute-done.17.refs_5_.rest_1_ = f32[32,4096]{1,0:T(8,128)S(1)} collective-permute-done((f32[32,4096]{1,0:T(8,128)}, f32[32,4096]{1,0:T(8,128)S(1)}, u32[]{:S(2)}, u32[]{:S(2)}) %collective-permute-start.17) | collective-permute-done | bytes 524320 | tf_op jit(solution)/shard_map/ppermute | solution.py:122
  259.2 9.6 %collective-permute-done.18.refs_6_.rest_2_ = f32[32,4096]{1,0:T(8,128)S(1)} collective-permute-done((f32[32,4096]{1,0:T(8,128)}, f32[32,4096]{1,0:T(8,128)S(1)}, u32[]{:S(2)}, u32[]{:S(2)}) %collective-permute-start.18) | collective-permute-done | bytes 524320 | tf_op jit(solution)/shard_map/ppermute | solution.py:122
  268.7 25.6 %collective-permute-done.19.refs_7_.rest_3_ = f32[32,4096]{1,0:T(8,128)S(1)} collective-permute-done((f32[32,4096]{1,0:T(8,128)}, f32[32,4096]{1,0:T(8,128)S(1)}, u32[]{:S(2)}, u32[]{:S(2)}) %collective-permute-start.19) | collective-permute-done | bytes 524320 | tf_op jit(solution)/shard_map/ppermute | solution.py:122
  296.9 6.7 %psum.7 = f32[1,32]{1,0:T(1,128)S(1)} all-reduce(f32[1,32]{1,0:T(1,128)} %shard_map.143), channel_id=1, replica_groups=mesh['space'=4,'vel'=8] {'space'}, use_global_device_ids=true, to_apply=%region_3.4 | all-reduce | flops 32 | bytes 256 | tf_op jit(solution)/shard_map/psum | solution.py:503
  310.7 17.2 %collective-permute-start.25 = (f32[1,32]{1,0:T(1,128)S(1)}, f32[1,32]{1,0:T(1,128)S(1)}, u32[]{:S(2)}, u32[]{:S(2)}) collective-permute-start(f32[1,32]{1,0:T(1,128)S(1)} %add.346), channel_id=1, source_target_pairs={{0,4},{1,5},{2,6},{3,7},{4,0},{5,1},{6,2},{7,3},{8,12},{9,13},{10,... | collective-permute-start | bytes 392 | tf_op jit(solution)/shard_map/ppermute | solution.py:122
  342.9 4.0 %shard_map.144.rest_5_ = f32[512,4096]{1,0:T(8,128)} custom-call(s32[1]{0:T(128)} %bitcast.me, f32[352,32]{1,0:T(8,128)S(1)} %copy.25.member, bf16[64,4096]{1,0:T(8,128)(2,1)S(1)} %pad_maximum_fusion.emit, f32[32,4096]{1,0:T(8,128)S(1)} %copy-done.5, f32[32,4096]{1,0:T(8,128)S(1)} %copy-done.7, f32[32,4096]{1,0:T(8,128)S(1)} %copy-done.9, ...), custom_call_target="tpu_custom_call" | custom-call | flops 184549376 | bytes 11534336 | tf_op jit(solution)/shard_map/pallas_call | solution.py:414
  346.9 14.1 %collective-permute-done.26.rest_0_ = f32[32,4096]{1,0:T(8,128)S(1)} collective-permute-done((f32[32,4096]{1,0:T(8,128)}, f32[32,4096]{1,0:T(8,128)S(1)}, u32[]{:S(2)}, u32[]{:S(2)}) %collective-permute-start.26) | collective-permute-done | bytes 524320 | tf_op jit(solution)/shard_map/ppermute | solution.py:122
  361.0 9.7 %collective-permute-done.27.rest_1_ = f32[32,4096]{1,0:T(8,128)S(1)} collective-permute-done((f32[32,4096]{1,0:T(8,128)}, f32[32,4096]{1,0:T(8,128)S(1)}, u32[]{:S(2)}, u32[]{:S(2)}) %collective-permute-start.27) | collective-permute-done | bytes 524320 | tf_op jit(solution)/shard_map/ppermute | solution.py:122
  (150 shorter events, 72.5 us)
Async XLA Ops:
  3.7 46.4 %collective-permute-start = (f32[32,4096]{1,0:T(8,128)S(1)}, f32[32,4096]{1,0:T(8,128)}, u32[]{:S(2)}, u32[]{:S(2)}) collective-permute-start(f32[32,4096]{1,0:T(8,128)S(1)} %shard_map.136.rest_0_), channel_id=1, source_target_pairs={{0,4},{1,5},{2,6},{3,7},{4,0},{5,1},{6,2},{7,3},{8,12},{9,13},{10,... | collective-permute-start | bytes 1572872 | tf_op jit(solution)/shard_map/ppermute | solution.py:122
  10.9 41.8 %collective-permute-start.7 = (f32[8,4096]{1,0:T(8,128)}, f32[8,4096]{1,0:T(8,128)S(1)}, u32[]{:S(2)}, u32[]{:S(2)}) collective-permute-start(f32[8,4096]{1,0:T(8,128)} %get-tuple-element.67), channel_id=1, source_target_pairs={{0,8},{8,16},{16,24},{1,9},{9,17},{17,25},{2,10},{10,18},{18,26},{... | collective-permute-start | bytes 393224 | tf_op jit(solution)/shard_map/ppermute | solution.py:471
  12.8 43.3 %collective-permute-start.8 = (f32[8,4096]{1,0:T(8,128)S(1)}, f32[8,4096]{1,0:T(8,128)S(1)}, u32[]{:S(2)}, u32[]{:S(2)}) collective-permute-start(f32[8,4096]{1,0:T(8,128)S(1)} %get-tuple-element.68), channel_id=1, source_target_pairs={{8,0},{16,8},{24,16},{9,1},{17,9},{25,17},{10,2},{18,10},{26,18},{... | collective-permute-start | bytes 393224 | tf_op jit(solution)/shard_map/ppermute | solution.py:472
  16.6 56.2 %collective-permute-start.1 = (f32[32,4096]{1,0:T(8,128)}, f32[32,4096]{1,0:T(8,128)}, u32[]{:S(2)}, u32[]{:S(2)}) collective-permute-start(f32[32,4096]{1,0:T(8,128)} %get-tuple-element.54), channel_id=1, source_target_pairs={{0,5},{1,4},{2,7},{3,6},{4,1},{5,0},{6,3},{7,2},{8,13},{9,12},{10,... | collective-permute-start | bytes 1572872 | tf_op jit(solution)/shard_map/ppermute | solution.py:122
  18.0 71.6 %collective-permute-start.2 = (f32[32,4096]{1,0:T(8,128)S(1)}, f32[32,4096]{1,0:T(8,128)}, u32[]{:S(2)}, u32[]{:S(2)}) collective-permute-start(f32[32,4096]{1,0:T(8,128)S(1)} %get-tuple-element.55), channel_id=1, source_target_pairs={{0,6},{1,7},{2,4},{3,5},{4,2},{5,3},{6,0},{7,1},{8,14},{9,15},{10,... | collective-permute-start | bytes 1572872 | tf_op jit(solution)/shard_map/ppermute | solution.py:122
  50.1 61.8 %collective-permute-start.3 = (f32[32,4096]{1,0:T(8,128)S(1)}, f32[32,4096]{1,0:T(8,128)}, u32[]{:S(2)}, u32[]{:S(2)}) collective-permute-start(f32[32,4096]{1,0:T(8,128)S(1)} %get-tuple-element.56), channel_id=1, source_target_pairs={{0,7},{1,6},{2,5},{3,4},{4,3},{5,2},{6,1},{7,0},{8,15},{9,14},{10,... | collective-permute-start | bytes 1572872 | tf_op jit(solution)/shard_map/ppermute | solution.py:122
  52.7 59.3 %collective-permute-start.4 = (f32[32,4096]{1,0:T(8,128)S(1)}, f32[32,4096]{1,0:T(8,128)}, u32[]{:S(2)}, u32[]{:S(2)}) collective-permute-start(f32[32,4096]{1,0:T(8,128)S(1)} %get-tuple-element.57), channel_id=1, source_target_pairs={{0,2},{1,3},{2,0},{3,1},{4,6},{5,7},{6,4},{7,5},{8,10},{9,11},{10,... | collective-permute-start | bytes 1572872 | tf_op jit(solution)/shard_map/ppermute | solution.py:122
  56.1 58.0 %collective-permute-start.5 = (f32[32,4096]{1,0:T(8,128)S(1)}, f32[32,4096]{1,0:T(8,128)}, u32[]{:S(2)}, u32[]{:S(2)}) collective-permute-start(f32[32,4096]{1,0:T(8,128)S(1)} %get-tuple-element.58), channel_id=1, source_target_pairs={{0,3},{1,2},{2,1},{3,0},{4,7},{5,6},{6,5},{7,4},{8,11},{9,10},{10,... | collective-permute-start | bytes 1572872 | tf_op jit(solution)/shard_map/ppermute | solution.py:122
  72.8 41.3 %collective-permute-start.6 = (f32[32,4096]{1,0:T(8,128)S(1)}, f32[32,4096]{1,0:T(8,128)}, u32[]{:S(2)}, u32[]{:S(2)}) collective-permute-start(f32[32,4096]{1,0:T(8,128)S(1)} %get-tuple-element.59), channel_id=1, source_target_pairs={{0,1},{1,0},{2,3},{3,2},{4,5},{5,4},{6,7},{7,6},{8,9},{9,8},{10,11... | collective-permute-start | bytes 1572872 | tf_op jit(solution)/shard_map/ppermute | solution.py:122
  89.6 78.2 %collective-permute-start.9 = (f32[32,4096]{1,0:T(8,128)S(1)}, f32[32,4096]{1,0:T(8,128)S(1)}, u32[]{:S(2)}, u32[]{:S(2)}) collective-permute-start(f32[32,4096]{1,0:T(8,128)S(1)} %get-tuple-element.69), channel_id=1, source_target_pairs={{0,4},{1,5},{2,6},{3,7},{4,0},{5,1},{6,2},{7,3},{8,12},{9,13},{10,... | collective-permute-start | bytes 1572872 | tf_op jit(solution)/shard_map/ppermute | solution.py:122
  112.0 55.8 %collective-permute-start.10 = (f32[32,4096]{1,0:T(8,128)S(1)}, f32[32,4096]{1,0:T(8,128)S(1)}, u32[]{:S(2)}, u32[]{:S(2)}) collective-permute-start(f32[32,4096]{1,0:T(8,128)S(1)} %get-tuple-element.70), channel_id=1, source_target_pairs={{0,5},{1,4},{2,7},{3,6},{4,1},{5,0},{6,3},{7,2},{8,13},{9,12},{10,... | collective-permute-start | bytes 1572872 | tf_op jit(solution)/shard_map/ppermute | solution.py:122
  112.0 66.5 %collective-permute-start.11 = (f32[32,4096]{1,0:T(8,128)S(1)}, f32[32,4096]{1,0:T(8,128)}, u32[]{:S(2)}, u32[]{:S(2)}) collective-permute-start(f32[32,4096]{1,0:T(8,128)S(1)} %get-tuple-element.71), channel_id=1, source_target_pairs={{0,6},{1,7},{2,4},{3,5},{4,2},{5,3},{6,0},{7,1},{8,14},{9,15},{10,... | collective-permute-start | bytes 1572872 | tf_op jit(solution)/shard_map/ppermute | solution.py:122
  114.1 88.1 %collective-permute-start.12 = (f32[32,4096]{1,0:T(8,128)}, f32[32,4096]{1,0:T(8,128)}, u32[]{:S(2)}, u32[]{:S(2)}) collective-permute-start(f32[32,4096]{1,0:T(8,128)} %get-tuple-element.72), channel_id=1, source_target_pairs={{0,7},{1,6},{2,5},{3,4},{4,3},{5,2},{6,1},{7,0},{8,15},{9,14},{10,... | collective-permute-start | bytes 1572872 | tf_op jit(solution)/shard_map/ppermute | solution.py:122
  114.1 88.1 %collective-permute-start.13 = (f32[32,4096]{1,0:T(8,128)}, f32[32,4096]{1,0:T(8,128)}, u32[]{:S(2)}, u32[]{:S(2)}) collective-permute-start(f32[32,4096]{1,0:T(8,128)} %get-tuple-element.73), channel_id=1, source_target_pairs={{0,2},{1,3},{2,0},{3,1},{4,6},{5,7},{6,4},{7,5},{8,10},{9,11},{10,... | collective-permute-start | bytes 1572872 | tf_op jit(solution)/shard_map/ppermute | solution.py:122
  178.5 74.9 %collective-permute-start.16 = (f32[32,4096]{1,0:T(8,128)}, f32[32,4096]{1,0:T(8,128)S(1)}, u32[]{:S(2)}, u32[]{:S(2)}) collective-permute-start(f32[32,4096]{1,0:T(8,128)} %get-tuple-element.79), channel_id=1, source_target_pairs={{0,4},{1,5},{2,6},{3,7},{4,0},{5,1},{6,2},{7,3},{8,12},{9,13},{10,... | collective-permute-start | bytes 1572872 | tf_op jit(solution)/shard_map/ppermute | solution.py:122
  202.2 55.3 %collective-permute-start.17 = (f32[32,4096]{1,0:T(8,128)}, f32[32,4096]{1,0:T(8,128)S(1)}, u32[]{:S(2)}, u32[]{:S(2)}) collective-permute-start(f32[32,4096]{1,0:T(8,128)} %get-tuple-element.80), channel_id=1, source_target_pairs={{0,5},{1,4},{2,7},{3,6},{4,1},{5,0},{6,3},{7,2},{8,13},{9,12},{10,... | collective-permute-start | bytes 1572872 | tf_op jit(solution)/shard_map/ppermute | solution.py:122
  202.2 66.6 %collective-permute-start.18 = (f32[32,4096]{1,0:T(8,128)}, f32[32,4096]{1,0:T(8,128)S(1)}, u32[]{:S(2)}, u32[]{:S(2)}) collective-permute-start(f32[32,4096]{1,0:T(8,128)} %get-tuple-element.81), channel_id=1, source_target_pairs={{0,6},{1,7},{2,4},{3,5},{4,2},{5,3},{6,0},{7,1},{8,14},{9,15},{10,... | collective-permute-start | bytes 1572872 | tf_op jit(solution)/shard_map/ppermute | solution.py:122
  204.8 89.6 %collective-permute-start.19 = (f32[32,4096]{1,0:T(8,128)}, f32[32,4096]{1,0:T(8,128)S(1)}, u32[]{:S(2)}, u32[]{:S(2)}) collective-permute-start(f32[32,4096]{1,0:T(8,128)} %get-tuple-element.82), channel_id=1, source_target_pairs={{0,7},{1,6},{2,5},{3,4},{4,3},{5,2},{6,1},{7,0},{8,15},{9,14},{10,... | collective-permute-start | bytes 1572872 | tf_op jit(solution)/shard_map/ppermute | solution.py:122
  247.2 47.2 %collective-permute-start.20 = (f32[32,4096]{1,0:T(8,128)S(1)}, f32[32,4096]{1,0:T(8,128)S(1)}, u32[]{:S(2)}, u32[]{:S(2)}) collective-permute-start(f32[32,4096]{1,0:T(8,128)S(1)} %copy-done.28), channel_id=1, source_target_pairs={{0,2},{1,3},{2,0},{3,1},{4,6},{5,7},{6,4},{7,5},{8,10},{9,11},{10,... | collective-permute-start | bytes 1572872 | tf_op jit(solution)/shard_map/ppermute | solution.py:122
  253.3 41.1 %collective-permute-start.21 = (f32[32,4096]{1,0:T(8,128)S(1)}, f32[32,4096]{1,0:T(8,128)S(1)}, u32[]{:S(2)}, u32[]{:S(2)}) collective-permute-start(f32[32,4096]{1,0:T(8,128)S(1)} %copy-done.27), channel_id=1, source_target_pairs={{0,3},{1,2},{2,1},{3,0},{4,7},{5,6},{6,5},{7,4},{8,11},{9,10},{10,... | collective-permute-start | bytes 1572872 | tf_op jit(solution)/shard_map/ppermute | solution.py:122
  268.7 64.0 %collective-permute-start.31 = (f32[32,4096]{1,0:T(8,128)}, f32[32,4096]{1,0:T(8,128)}, u32[]{:S(2)}, u32[]{:S(2)}) collective-permute-start(f32[32,4096]{1,0:T(8,128)} %get-tuple-element.92), channel_id=1, source_target_pairs={{0,4},{1,5},{2,6},{3,7},{4,0},{5,1},{6,2},{7,3},{8,12},{9,13},{10,... | collective-permute-start | bytes 1572872 | tf_op jit(solution)/shard_map/ppermute | solution.py:122
  308.9 52.1 %collective-permute-start.26 = (f32[32,4096]{1,0:T(8,128)}, f32[32,4096]{1,0:T(8,128)S(1)}, u32[]{:S(2)}, u32[]{:S(2)}) collective-permute-start(f32[32,4096]{1,0:T(8,128)} %get-tuple-element.86), channel_id=1, source_target_pairs={{0,2},{1,3},{2,0},{3,1},{4,6},{5,7},{6,4},{7,5},{8,10},{9,11},{10,... | collective-permute-start | bytes 1572872 | tf_op jit(solution)/shard_map/ppermute | solution.py:122
  327.9 42.8 %collective-permute-start.27 = (f32[32,4096]{1,0:T(8,128)}, f32[32,4096]{1,0:T(8,128)S(1)}, u32[]{:S(2)}, u32[]{:S(2)}) collective-permute-start(f32[32,4096]{1,0:T(8,128)} %get-tuple-element.87), channel_id=1, source_target_pairs={{0,3},{1,2},{2,1},{3,0},{4,7},{5,6},{6,5},{7,4},{8,11},{9,10},{10,... | collective-permute-start | bytes 1572872 | tf_op jit(solution)/shard_map/ppermute | solution.py:122
  329.6 41.2 %collective-permute-start.28 = (f32[32,4096]{1,0:T(8,128)}, f32[32,4096]{1,0:T(8,128)S(1)}, u32[]{:S(2)}, u32[]{:S(2)}) collective-permute-start(f32[32,4096]{1,0:T(8,128)} %get-tuple-element.88), channel_id=1, source_target_pairs={{0,6},{1,7},{2,4},{3,5},{4,2},{5,3},{6,0},{7,1},{8,14},{9,15},{10,... | collective-permute-start | bytes 1572872 | tf_op jit(solution)/shard_map/ppermute | solution.py:122
  (41 other events, 628.6 us)
